TPU v7x, 256 devices: a whole 4x4x8 slice. The times are simulated.
256 devices in a mesh: chain: 8 (over z), bond: 32 (over y, x, core).
Axes of the slice: x: 4, y: 4, z: 8, core: 2. Of those that a mesh axis runs over, the one named last changes fastest.
Arguments:
- site_tensors: bfloat16 [8, 1024, 4, 1024], P('chain', 'bond')
- start_env: bfloat16 [4, 1024, 1024], P(None, 'bond'), may hold values from -6 to 6
- operators: float32 [6, 4, 4], replicated, may hold values from -4 to 4
- op_site: int32 [4], replicated, may hold values from 0 to 7
- op_kind: int32 [4], replicated, may hold values from 0 to 5
- probe: float32 [4, 4], replicated
Outputs:
- block_env: bfloat16 [8, 4, 1024, 1024], P('chain', None, 'bond')
- correlation: float32 [4, 8], P(None, 'chain')
All inputs are finite; a program needn't handle non-finite values.
Results may differ from a plain program's by a relative error of at most 0.03.
Values may be sent and summed in bfloat16 or wider, within the bound.
No kernel may reach another device: no remote copies, remote signals or barrier semaphores. Data moves between devices by JAX's collectives and lax.ppermute only.
A program may use at most 128 MiB of HBM per device.

v0:
```python
import math

import jax
import jax.numpy as jnp
from jax import lax
from jax.sharding import PartitionSpec as P


def from_behind(array, axis, by):
    peers = lax.axis_size(axis)
    pairs = [(i, i + by) for i in range(peers) if 0 <= i + by < peers]
    return lax.ppermute(array, axis, pairs)


def on_device(site_tensors, start_env, operators, op_site, op_kind, probe):
    fronts = start_env.shape[0]
    panel = start_env.shape[1]
    width = start_env.shape[2]
    phys = site_tensors.shape[2]
    kinds = operators.shape[0]
    links = lax.axis_size("chain")
    link = lax.axis_index("chain")
    local_tensor = site_tensors[0]
    local_f32 = local_tensor.astype(jnp.float32)
    full_tensor = lax.all_gather(local_tensor, "bond", axis=0, tiled=True)
    flat_right = full_tensor.reshape(width, phys * width)
    flat_left = full_tensor.reshape(width * phys, width)
    is_odd = link % 2 == 1
    eye = jnp.eye(phys, dtype=jnp.float32)
    onehot = (op_kind[:, None] == jnp.arange(kinds, dtype=jnp.int32)[None, :]).astype(jnp.float32)
    chosen = jnp.einsum("fn,nst->fst", onehot, operators)
    mixes = jnp.where((op_site == link)[:, None, None], chosen, eye[None])
    mixes = jnp.where(is_odd, jnp.swapaxes(mixes, 1, 2), mixes)
    looking = jnp.where(is_odd, probe.T, probe)
    group = 2
    groups = fronts // group
    turns = links + groups - 1

    def advance(turn, carry):
        incoming, env_out, corr_acc = carry
        slot = turn - link
        valid = jnp.logical_and(slot >= 0, slot < groups)
        start = jnp.clip(slot, 0, groups - 1) * group
        first = lax.dynamic_slice_in_dim(start_env, start, group, 0)
        current = jnp.where(link == 0, first, incoming)
        prod32 = jnp.dot(
            current.reshape(group * panel, width), flat_right, preferred_element_type=jnp.float32
        ).reshape(group, panel, phys, width)
        intersection = jnp.einsum("rsb,krtb->kst", local_f32, prod32)
        partial_value = jnp.sum(intersection * looking[None], axis=(1, 2)) / math.sqrt(width)
        moved = lax.all_to_all(
            prod32.astype(jnp.bfloat16), "bond", split_axis=3, concat_axis=1, tiled=True
        )
        mix_here = lax.dynamic_slice_in_dim(mixes, start, group, 0)
        mixed = jnp.einsum("kst,krtb->krsb", mix_here, moved.astype(jnp.float32)).astype(
            jnp.bfloat16
        )
        fresh = lax.dot_general(
            mixed.reshape(group, width * phys, panel),
            flat_left,
            (((1,), (0,)), ((), ())),
            preferred_element_type=jnp.float32,
        )
        fresh = fresh.astype(jnp.bfloat16)
        written = lax.dynamic_update_slice_in_dim(env_out, fresh, start, 0)
        env_out = jnp.where(valid, written, env_out)
        summed = lax.psum(partial_value, "bond")
        placed = lax.dynamic_update_slice_in_dim(corr_acc, summed, start, 0)
        corr_acc = jnp.where(valid, placed, corr_acc)
        incoming = from_behind(fresh, "chain", 1)
        return (incoming, env_out, corr_acc)

    initial = (
        jnp.zeros((group, panel, width), jnp.bfloat16),
        jnp.zeros((fronts, panel, width), jnp.bfloat16),
        jnp.zeros((fronts,), jnp.float32),
    )
    final_in, env_out, corr_acc = lax.fori_loop(0, turns, advance, initial)
    return (env_out[None], corr_acc[:, None])


def solution(mesh):
    placed = (P("chain", "bond", None, None), P(None, "bond", None), P(), P(), P(), P())
    return jax.shard_map(
        on_device,
        mesh=mesh,
        in_specs=placed,
        out_specs=(P("chain", None, "bond", None), P(None, "chain")),
        check_vma=False,
    )
```

profile of v0, /device:TPU:192, one launch (start us, length us, event | category | flops | bytes accessed | tf_op | source)
XLA Modules:
  0.0 1067.8 jit_solution(2040461570417333173)
XLA Ops:
  11.7 57.6 %all-gather.3.cloned.1.call-done = bf16[1,1024,4,1024]{3,2,0,1:T(4,128)(2,1)} async-done(((bf16[1,32,4,1024]{3,2,0,1:T(4,128)(2,1)}), bf16[1,1024,4,1024]{3,2,0,1:T(4,128)(2,1)}) %all-gather.3.cloned.1.call-update) | async-done | bytes 8388624 | tf_op jit(solution)/shard_map/all_gather | solution.py:25
  69.3 13.8 %copy.36 = bf16[1,1024,4,1024]{1,3,2,0:T(8,128)(2,1)} copy(bf16[1,1024,4,1024]{3,2,0,1:T(4,128)(2,1)} %all-gather.3.cloned.1.call-done) | data formatting | bytes 16777216 | tf_op jit(solution)/shard_map/while | solution.py:78
  83.1 12.5 %reshape.42 = bf16[4096,1024]{1,0:T(8,128)(2,1)} reshape(bf16[1,1024,4,1024]{3,2,0,1:T(4,128)(2,1)} %all-gather.3.cloned.1.call-done) | data formatting | bytes 16777216 | tf_op jit(solution)/shard_map/reshape | solution.py:27
  95.6 964.6 %while.18 = (s32[]{:T(128)}, bf16[2,32,1024]{2,1,0:T(8,128)(2,1)S(1)}, bf16[4,32,1024]{2,1,0:T(8,128)(2,1)S(1)}, f32[4]{0:T(128)S(1)}, pred[]{:T(512)}, /*index=...) while((s32[]{:T(128)}, ...), condition=%wide.region_3.4_spmd, body=%wide.region_0.3_spmd.sunk | while | flops 1078132736 | bytes 30278820 | solution.py:78
  95.7 6.1 fusion.44
  105.9 5.5 all-to-all-start
  113.6 67.6 %psum.13 = f32[2]{0:T(128)S(1)} all-reduce(f32[2]{0:T(128)S(1)} %broadcast_multiply_fusion.2), channel_id=1, replica_groups=mesh['chain'=8,'bond'=32] {'bond'}, use_global_device_ids=true, to_apply=%region_2.2 | all-reduce | flops 2 | bytes 16 | tf_op jit(solution)/shard_map/while/body/eval_jaxpr/psum | solution.py:67
  182.2 3.8 copy.52
  186.0 3.5 all_to_all.36
  191.5 5.1 select_dynamic-update-slice_fusion.2
  199.3 4.1 collective-permute-done
  203.4 6.1 fusion.44
  213.7 3.9 all-to-all-start
  219.8 67.6 %psum.13 = f32[2]{0:T(128)S(1)} all-reduce(f32[2]{0:T(128)S(1)} %broadcast_multiply_fusion.2), channel_id=1, replica_groups=mesh['chain'=8,'bond'=32] {'bond'}, use_global_device_ids=true, to_apply=%region_2.2 | all-reduce | flops 2 | bytes 16 | tf_op jit(solution)/shard_map/while/body/eval_jaxpr/psum | solution.py:67
  288.4 3.8 copy.52
  292.2 3.5 all_to_all.36
  297.7 5.1 select_dynamic-update-slice_fusion.2
  305.5 4.1 collective-permute-done
  309.7 6.1 fusion.44
  319.9 3.9 all-to-all-start
  326.0 67.6 %psum.13 = f32[2]{0:T(128)S(1)} all-reduce(f32[2]{0:T(128)S(1)} %broadcast_multiply_fusion.2), channel_id=1, replica_groups=mesh['chain'=8,'bond'=32] {'bond'}, use_global_device_ids=true, to_apply=%region_2.2 | all-reduce | flops 2 | bytes 16 | tf_op jit(solution)/shard_map/while/body/eval_jaxpr/psum | solution.py:67
  394.7 3.8 copy.52
  398.4 3.5 all_to_all.36
  403.9 5.1 select_dynamic-update-slice_fusion.2
  411.7 4.1 collective-permute-done
  415.9 6.1 fusion.44
  426.1 3.9 all-to-all-start
  432.2 67.6 %psum.13 = f32[2]{0:T(128)S(1)} all-reduce(f32[2]{0:T(128)S(1)} %broadcast_multiply_fusion.2), channel_id=1, replica_groups=mesh['chain'=8,'bond'=32] {'bond'}, use_global_device_ids=true, to_apply=%region_2.2 | all-reduce | flops 2 | bytes 16 | tf_op jit(solution)/shard_map/while/body/eval_jaxpr/psum | solution.py:67
  500.9 3.8 copy.52
  504.6 3.5 all_to_all.36
  510.1 5.1 select_dynamic-update-slice_fusion.2
  517.9 5.2 collective-permute-done
  523.2 6.1 fusion.44
  533.5 3.9 all-to-all-start
  539.5 67.6 %psum.13 = f32[2]{0:T(128)S(1)} all-reduce(f32[2]{0:T(128)S(1)} %broadcast_multiply_fusion.2), channel_id=1, replica_groups=mesh['chain'=8,'bond'=32] {'bond'}, use_global_device_ids=true, to_apply=%region_2.2 | all-reduce | flops 2 | bytes 16 | tf_op jit(solution)/shard_map/while/body/eval_jaxpr/psum | solution.py:67
  608.2 3.8 copy.52
  617.5 5.1 select_dynamic-update-slice_fusion.2
  624.6 6.0 collective-permute-done
  630.6 6.1 fusion.44
  640.9 3.9 all-to-all-start
  646.9 67.6 %psum.13 = f32[2]{0:T(128)S(1)} all-reduce(f32[2]{0:T(128)S(1)} %broadcast_multiply_fusion.2), channel_id=1, replica_groups=mesh['chain'=8,'bond'=32] {'bond'}, use_global_device_ids=true, to_apply=%region_2.2 | all-reduce | flops 2 | bytes 16 | tf_op jit(solution)/shard_map/while/body/eval_jaxpr/psum | solution.py:67
  715.6 3.8 copy.52
  719.4 3.5 all_to_all.36
  724.9 5.1 select_dynamic-update-slice_fusion.2
  732.0 6.0 collective-permute-done
  738.0 6.1 fusion.44
  748.3 3.9 all-to-all-start
  754.3 67.6 %psum.13 = f32[2]{0:T(128)S(1)} all-reduce(f32[2]{0:T(128)S(1)} %broadcast_multiply_fusion.2), channel_id=1, replica_groups=mesh['chain'=8,'bond'=32] {'bond'}, use_global_device_ids=true, to_apply=%region_2.2 | all-reduce | flops 2 | bytes 16 | tf_op jit(solution)/shard_map/while/body/eval_jaxpr/psum | solution.py:67
  823.0 3.8 copy.52
  832.3 5.1 select_dynamic-update-slice_fusion.2
  839.5 6.0 collective-permute-done
  845.4 6.1 fusion.44
  855.7 3.9 all-to-all-start
  861.8 67.6 %psum.13 = f32[2]{0:T(128)S(1)} all-reduce(f32[2]{0:T(128)S(1)} %broadcast_multiply_fusion.2), channel_id=1, replica_groups=mesh['chain'=8,'bond'=32] {'bond'}, use_global_device_ids=true, to_apply=%region_2.2 | all-reduce | flops 2 | bytes 16 | tf_op jit(solution)/shard_map/while/body/eval_jaxpr/psum | solution.py:67
  930.4 3.8 copy.52
  939.7 5.1 select_dynamic-update-slice_fusion.2
  946.9 6.0 collective-permute-done
  952.8 6.1 fusion.44
  963.1 3.9 all-to-all-start
  969.2 67.6 %psum.13 = f32[2]{0:T(128)S(1)} all-reduce(f32[2]{0:T(128)S(1)} %broadcast_multiply_fusion.2), channel_id=1, replica_groups=mesh['chain'=8,'bond'=32] {'bond'}, use_global_device_ids=true, to_apply=%region_2.2 | all-reduce | flops 2 | bytes 16 | tf_op jit(solution)/shard_map/while/body/eval_jaxpr/psum | solution.py:67
  1037.8 3.8 copy.52
  1041.6 3.5 all_to_all.36
  1047.1 5.1 select_dynamic-update-slice_fusion.2
  1054.3 6.0 collective-permute-done
  (120 shorter events, 120.7 us)
Async XLA Ops:
  7.2 0.8 copy-start
  7.2 62.1 %all-gather.3.cloned.1.call-start = ((), (), s32[]{:S(2)}) async-start(), calls=%async_computation.1 | async-start | bytes 8650752 | tf_op jit(solution)/shard_map/all_gather | solution.py:25
  105.9 75.3 %all-to-all-start = ((bf16[32,2,4096]{2,1,0:T(2,128)(2,1)}), bf16[32,2,4096]{2,1,0:T(2,128)(2,1)S(1)}, u32[]{:S(2)}, u32[]{:S(2)}) async-start(bf16[32,2,4096]{2,1,0:T(2,128)(2,1)} %reshape.58), calls=%async_computation | async-start | bytes 1048576 | tf_op jit(solution)/shard_map/while/body/eval_jaxpr/all_to_all | solution.py:51
  196.6 6.9 collective-permute-start
  213.7 73.7 %all-to-all-start = ((bf16[32,2,4096]{2,1,0:T(2,128)(2,1)}), bf16[32,2,4096]{2,1,0:T(2,128)(2,1)S(1)}, u32[]{:S(2)}, u32[]{:S(2)}) async-start(bf16[32,2,4096]{2,1,0:T(2,128)(2,1)} %reshape.58), calls=%async_computation | async-start | bytes 1048576 | tf_op jit(solution)/shard_map/while/body/eval_jaxpr/all_to_all | solution.py:51
  302.8 6.9 collective-permute-start
  319.9 73.7 %all-to-all-start = ((bf16[32,2,4096]{2,1,0:T(2,128)(2,1)}), bf16[32,2,4096]{2,1,0:T(2,128)(2,1)S(1)}, u32[]{:S(2)}, u32[]{:S(2)}) async-start(bf16[32,2,4096]{2,1,0:T(2,128)(2,1)} %reshape.58), calls=%async_computation | async-start | bytes 1048576 | tf_op jit(solution)/shard_map/while/body/eval_jaxpr/all_to_all | solution.py:51
  409.0 6.9 collective-permute-start
  426.1 73.7 %all-to-all-start = ((bf16[32,2,4096]{2,1,0:T(2,128)(2,1)}), bf16[32,2,4096]{2,1,0:T(2,128)(2,1)S(1)}, u32[]{:S(2)}, u32[]{:S(2)}) async-start(bf16[32,2,4096]{2,1,0:T(2,128)(2,1)} %reshape.58), calls=%async_computation | async-start | bytes 1048576 | tf_op jit(solution)/shard_map/while/body/eval_jaxpr/all_to_all | solution.py:51
  515.2 8.0 collective-permute-start
  533.5 73.7 %all-to-all-start = ((bf16[32,2,4096]{2,1,0:T(2,128)(2,1)}), bf16[32,2,4096]{2,1,0:T(2,128)(2,1)S(1)}, u32[]{:S(2)}, u32[]{:S(2)}) async-start(bf16[32,2,4096]{2,1,0:T(2,128)(2,1)} %reshape.58), calls=%async_computation | async-start | bytes 1048576 | tf_op jit(solution)/shard_map/while/body/eval_jaxpr/all_to_all | solution.py:51
  622.5 8.1 collective-permute-start
  640.9 73.7 %all-to-all-start = ((bf16[32,2,4096]{2,1,0:T(2,128)(2,1)}), bf16[32,2,4096]{2,1,0:T(2,128)(2,1)S(1)}, u32[]{:S(2)}, u32[]{:S(2)}) async-start(bf16[32,2,4096]{2,1,0:T(2,128)(2,1)} %reshape.58), calls=%async_computation | async-start | bytes 1048576 | tf_op jit(solution)/shard_map/while/body/eval_jaxpr/all_to_all | solution.py:51
  729.9 8.1 collective-permute-start
  748.3 73.7 %all-to-all-start = ((bf16[32,2,4096]{2,1,0:T(2,128)(2,1)}), bf16[32,2,4096]{2,1,0:T(2,128)(2,1)S(1)}, u32[]{:S(2)}, u32[]{:S(2)}) async-start(bf16[32,2,4096]{2,1,0:T(2,128)(2,1)} %reshape.58), calls=%async_computation | async-start | bytes 1048576 | tf_op jit(solution)/shard_map/while/body/eval_jaxpr/all_to_all | solution.py:51
  837.4 8.1 collective-permute-start
  855.7 73.7 %all-to-all-start = ((bf16[32,2,4096]{2,1,0:T(2,128)(2,1)}), bf16[32,2,4096]{2,1,0:T(2,128)(2,1)S(1)}, u32[]{:S(2)}, u32[]{:S(2)}) async-start(bf16[32,2,4096]{2,1,0:T(2,128)(2,1)} %reshape.58), calls=%async_computation | async-start | bytes 1048576 | tf_op jit(solution)/shard_map/while/body/eval_jaxpr/all_to_all | solution.py:51
  944.8 8.1 collective-permute-start
  963.1 73.7 %all-to-all-start = ((bf16[32,2,4096]{2,1,0:T(2,128)(2,1)}), bf16[32,2,4096]{2,1,0:T(2,128)(2,1)S(1)}, u32[]{:S(2)}, u32[]{:S(2)}) async-start(bf16[32,2,4096]{2,1,0:T(2,128)(2,1)} %reshape.58), calls=%async_computation | async-start | bytes 1048576 | tf_op jit(solution)/shard_map/while/body/eval_jaxpr/all_to_all | solution.py:51
  1052.2 8.1 collective-permute-start
  1060.2 0.7 copy-start.1
  1060.2 0.7 copy-start.2
Sparse Core Ops, SparseCore 0:
  10.6 58.6 all-gather.2
where the time goes:
time: 1080 us; the launch traced here: 1070 us
  blocking collectives  608 us (56%)
  local copies, waits for them, and re-layouts  154 us (14%)
  matrix products  125 us (12%)
  waiting for transfers between devices  106 us (10%)
  starting transfers between devices  56.4 us (5%)
  between operations  14.1 us (1%)
    psum x9, blocking collectives, advance(): summed = lax.psum(partial_value, 'bond')  608 us
    all_to_all x18, local copies, waits for them, and re-layouts, advance(): lax.all_to_all(prod32.astype(jnp.bfloat16), 'bond', split_axis=3, concat_...  65.8 us
    all_gather x1, waiting for transfers between devices, on_device(): full_tensor = lax.all_gather(local_tensor, 'bond', axis=0, tiled=True)  57.6 us
    dot_general x9, matrix products, advance(): jnp.dot(current.reshape(group * panel, width), flat_right, preferred_elem...  55.1 us
    ppermute x9, waiting for transfers between devices, from_behind(): return lax.ppermute(array, axis, pairs)  47.5 us
    dot_general x9, matrix products, advance(): lax.dot_general(mixed.reshape(group, width * phys, panel), flat_left, (((...  45.7 us
    all_to_all x9, starting transfers between devices, advance(): lax.all_to_all(prod32.astype(jnp.bfloat16), 'bond', split_axis=3, concat_...  36.6 us
    while x18, local copies, waits for them, and re-layouts  34 us
  transfers between devices with their start and end apart: 19, of which 10 were waited for; matrix products, arithmetic and copies ran while one was open for 2% of the time, Pallas kernels for 0%

commit v1 on v0

v1 whole, which is shorter than its diff:
```python
import functools
import math

import jax
import jax.numpy as jnp
from jax import lax
from jax.experimental import pallas as pl
from jax.experimental.pallas import tpu as pltpu
from jax.sharding import PartitionSpec as P

EXTRA = 16
MIB = 1 << 20


def split3(value):
    high = value.astype(jnp.bfloat16)
    rest = value - high.astype(jnp.float32)
    mid = rest.astype(jnp.bfloat16)
    low = (rest - mid.astype(jnp.float32)).astype(jnp.bfloat16)
    return high, mid, low


def first_kernel(turn, group, mix_ref, env_ref, tensor_ref, look_ref, out_ref, total):
    step = pl.program_id(0)
    panel = tensor_ref.shape[2]
    phys = tensor_ref.shape[1]
    width = tensor_ref.shape[0] * panel
    cols = tensor_ref.shape[3]

    @pl.when(step == 0)
    def _():
        total[...] = jnp.zeros_like(total)

    prods = [
        jnp.dot(env_ref[...], tensor_ref[:, t].reshape(width, cols), preferred_element_type=jnp.float32)
        for t in range(phys)
    ]
    for f in range(group):
        rows = slice(f * panel, (f + 1) * panel)
        mine = [prods[t][rows] for t in range(phys)]
        seen = sum(look_ref[t] * mine[t] for t in range(phys))
        line = jnp.sum(seen, axis=0, keepdims=True)
        total[f : f + 1] += sum(line[:, c : c + 128] for c in range(0, cols, 128))
        mixed = [
            sum(mix_ref[turn, f, s, t] * mine[t] for t in range(phys)) for s in range(phys)
        ]
        turned = jnp.concatenate(mixed, axis=0).T.astype(jnp.bfloat16)
        out_ref[pl.ds(step * (cols // panel), cols // panel), rows, :] = turned.reshape(
            cols // panel, panel, phys * panel
        )

    @pl.when(step == pl.num_programs(0) - 1)
    def _():
        value = jnp.broadcast_to(jnp.sum(total[...], axis=1, keepdims=True), total.shape)
        parts = jnp.concatenate([p.astype(jnp.float32) for p in split3(value)], axis=0)
        block = jnp.concatenate([parts, jnp.zeros((EXTRA - parts.shape[0], 128), jnp.float32)], axis=0)
        block = block.astype(jnp.bfloat16)
        out_ref[:, group * panel :, :] = jnp.broadcast_to(block[None], (out_ref.shape[0], EXTRA, 128))


def first(turn, group, mixes, env, tensor, look):
    peers, phys, panel, width = tensor.shape
    cols = 256
    tall = group * panel + EXTRA
    return pl.pallas_call(
        functools.partial(first_kernel, turn, group),
        grid=(width // cols,),
        in_specs=[
            pl.BlockSpec(memory_space=pltpu.SMEM),
            pl.BlockSpec((group * panel, width), lambda i: (0, 0)),
            pl.BlockSpec((peers, phys, panel, cols), lambda i: (0, 0, 0, i)),
            pl.BlockSpec((phys, panel, cols), lambda i: (0, 0, i)),
        ],
        out_specs=pl.BlockSpec((peers, tall, phys * panel), lambda i: (0, 0, 0)),
        out_shape=jax.ShapeDtypeStruct((peers, tall, phys * panel), jnp.bfloat16),
        scratch_shapes=[pltpu.VMEM((group, 128), jnp.float32)],
        compiler_params=pltpu.CompilerParams(vmem_limit_bytes=24 * MIB),
    )(mixes, env, tensor, look)


def second_kernel(rows, moved_ref, tensor_ref, env_ref, sums_ref, acc):
    step = pl.program_id(0)
    chunk = moved_ref.shape[0]
    depth = tensor_ref.shape[1] * tensor_ref.shape[2]

    @pl.when(step == 0)
    def _():
        acc[...] = jnp.zeros_like(acc)
        sums_ref[...] = jnp.zeros_like(sums_ref)

    left = jnp.concatenate([moved_ref[d, :rows] for d in range(chunk)], axis=1)
    right = tensor_ref[...].reshape(chunk * depth, tensor_ref.shape[3])
    acc[...] += jnp.dot(left, right, preferred_element_type=jnp.float32)
    sums_ref[...] += jnp.sum(moved_ref[:, rows:].astype(jnp.float32), axis=0)

    @pl.when(step == pl.num_programs(0) - 1)
    def _():
        env_ref[...] = acc[...].astype(jnp.bfloat16)


def second(group, moved, tensor):
    peers, phys, panel, width = tensor.shape
    chunk = 8
    rows = group * panel
    return pl.pallas_call(
        functools.partial(second_kernel, rows),
        grid=(peers // chunk,),
        in_specs=[
            pl.BlockSpec((chunk,) + moved.shape[1:], lambda i: (i, 0, 0)),
            pl.BlockSpec((chunk, phys, panel, width), lambda i: (i, 0, 0, 0)),
        ],
        out_specs=[
            pl.BlockSpec((rows, width), lambda i: (0, 0)),
            pl.BlockSpec((EXTRA, 128), lambda i: (0, 0)),
        ],
        out_shape=[
            jax.ShapeDtypeStruct((rows, width), jnp.bfloat16),
            jax.ShapeDtypeStruct((EXTRA, 128), jnp.float32),
        ],
        scratch_shapes=[pltpu.VMEM((rows, width), jnp.float32)],
        compiler_params=pltpu.CompilerParams(vmem_limit_bytes=24 * MIB),
    )(moved, tensor)


def on_device(site_tensors, start_env, operators, op_site, op_kind, probe):
    fronts, panel, width = start_env.shape
    phys = site_tensors.shape[2]
    kinds = operators.shape[0]
    links = lax.axis_size("chain")
    link = lax.axis_index("chain")
    group = 2
    groups = fronts // group
    turns = links + groups - 1
    mine = jnp.swapaxes(site_tensors[0], 0, 1)
    tensor = lax.all_gather(mine, "bond", axis=0)
    is_odd = link % 2 == 1
    eye = jnp.eye(phys, dtype=jnp.float32)
    onehot = (op_kind[:, None] == jnp.arange(kinds, dtype=jnp.int32)[None, :]).astype(jnp.float32)
    chosen = jnp.sum(onehot[:, :, None, None] * operators[None], axis=1)
    mixes = jnp.where((op_site == link)[:, None, None], chosen, eye[None])
    mixes = jnp.where(is_odd, jnp.swapaxes(mixes, 1, 2), mixes)
    slots = jnp.clip(jnp.arange(turns) - link, 0, groups - 1)
    mixes = mixes.reshape(groups, group, phys, phys)
    per_turn = jnp.where((slots == 0)[:, None, None, None], mixes[0][None], mixes[1][None])
    looking = jnp.where(is_odd, probe.T, probe) / math.sqrt(width)
    mine32 = mine.astype(jnp.float32)
    look = jnp.stack([sum(looking[s, t] * mine32[s] for s in range(phys)) for t in range(phys)])
    starts = start_env.reshape(groups, group * panel, width)
    env = starts[0]
    envs, sums = [], []
    for turn in range(turns):
        if 0 < turn < groups:
            env = jnp.where(link == 0, starts[turn], env)
        sent = first(turn, group, per_turn, env, tensor, look)
        moved = lax.all_to_all(sent, "bond", 0, 0, tiled=True)
        fresh, total = second(group, moved, tensor)
        envs.append(fresh)
        sums.append(total)
        if turn + 1 < turns:
            env = lax.ppermute(fresh, "chain", [(i, i + 1) for i in range(links - 1)])
    picked = lax.dynamic_slice_in_dim(jnp.stack(envs), link, groups, 0)
    values = lax.dynamic_slice_in_dim(jnp.stack(sums), link, groups, 0)[:, :, 0]
    values = values[:, : 3 * group].reshape(groups, 3, group).sum(axis=1)
    return picked.reshape(1, fronts, panel, width), values.reshape(fronts, 1)


def solution(mesh):
    placed = (P("chain", "bond", None, None), P(None, "bond", None), P(), P(), P(), P())
    return jax.shard_map(
        on_device,
        mesh=mesh,
        in_specs=placed,
        out_specs=(P("chain", None, "bond", None), P(None, "chain")),
        check_vma=False,
    )
```

time: 1080 us -> 390 us (0.36)
  blocking collectives: 608 us -> 69.2 us
  local copies, waits for them, and re-layouts: 154 us -> 27.8 us
  matrix products: 125 us -> 0 us
  Pallas kernels: 0 us -> 61.8 us
  waiting for transfers between devices: 106 us -> 162 us
  starting transfers between devices: 56.4 us -> 37.7 us
    psum x9 -> x0, blocking collectives: 608 us -> none  [advance(): summed = lax.psum(partial_value, 'bond')]
    dot_general x37 -> x0, matrix products: 125 us -> none  [the longest x9 55.1 us: advance(): jnp.dot(current.reshape(group * panel, width), flat_right, preferred_elem...]
    all_to_all x0 -> x4, blocking collectives: none -> 69.2 us  [on_device(): moved = lax.all_to_all(sent, 'bond', 0, 0, tiled=True)]
    all_to_all x18 -> x0, local copies, waits for them, and re-layouts: 65.8 us -> none  [advance(): lax.all_to_all(prod32.astype(jnp.bfloat16), 'bond', split_axis=3, concat_...]
    all_to_all x9 -> x5, waiting for transfers between devices: 0.02 us -> 65.7 us  [on_device(): moved = lax.all_to_all(sent, 'bond', 0, 0, tiled=True)]
    pallas_call x0 -> x17, Pallas kernels: none -> 61.8 us  [the longest x9 45.8 us: first(): pl.pallas_call(functools.partial(first_kernel, turn, group), grid=(width...]
    while x19 -> x0, local copies, waits for them, and re-layouts: 47.8 us -> none
    convert_element_type x18 -> x0, local copies, waits for them, and re-layouts: 26.2 us -> none  [the longest x9 13.6 us: advance(): jnp.einsum('kst,krtb->krsb', mix_here, moved.astype(jnp.float32))]
  transfers between devices with their start and end apart: 19 -> 14, of which waited for: 10 -> 14; matrix products, arithmetic and copies ran while one was open for 2% -> 3% of each run, Pallas kernels for 0% -> 0%
where the time goes in v1:
time: 390 us; the launch traced here: 385 us
  waiting for transfers between devices  162 us (42%)
  blocking collectives  69.2 us (18%)
  Pallas kernels  61.8 us (16%)
  starting transfers between devices  37.7 us (10%)
  local copies, waits for them, and re-layouts  27.8 us (7%)
  between operations  14.5 us (4%)
  other arithmetic  12.2 us (3%)
    all_to_all x4, blocking collectives, on_device(): moved = lax.all_to_all(sent, 'bond', 0, 0, tiled=True)  69.2 us
    all_to_all x5, waiting for transfers between devices, on_device(): moved = lax.all_to_all(sent, 'bond', 0, 0, tiled=True)  65.7 us
    all_gather x1, waiting for transfers between devices, on_device(): tensor = lax.all_gather(mine, 'bond', axis=0)  49.4 us
    ppermute x8, waiting for transfers between devices, on_device(): env = lax.ppermute(fresh, 'chain', [(i, i + 1) for i in range(links - 1)])  46.6 us
    pallas_call x9, Pallas kernels, first(): pl.pallas_call(functools.partial(first_kernel, turn, group), grid=(width...  45.8 us
    unnamed x39, local copies, waits for them, and re-layouts  20.5 us
    all_to_all x5, starting transfers between devices, on_device(): moved = lax.all_to_all(sent, 'bond', 0, 0, tiled=True)  19.7 us
    ppermute x8, starting transfers between devices, on_device(): env = lax.ppermute(fresh, 'chain', [(i, i + 1) for i in range(links - 1)])  17.9 us
  transfers between devices with their start and end apart: 14, of which 14 were waited for; matrix products, arithmetic and copies ran while one was open for 3% of the time, Pallas kernels for 0%

profile of v1, /device:TPU:192, one launch (start us, length us, event | category | flops | bytes accessed | tf_op | source)
XLA Modules:
  0.0 384.9 jit_solution(17786562580511617644)
XLA Ops:
  7.2 1.8 fusion.5
  9.1 0.1 multiply_reduce_fusion
  9.2 0.1 copy.23
  9.3 0.1 copy.25
  9.5 0.7 fusion.11
  10.2 4.9 %multiply_add_fusion.1 = (f32[1,32,1024]{2,1,0:T(8,128)S(1)}, f32[1,32,1024]{2,1,0:T(8,128)S(1)}) fusion(f32[4,32,1024]{2,1,0:T(8,128)S(1)} %get-tuple-element.48, f32[]{:T(128)} %bitcast.18, f32[]{:T(128)} %bitcast.17, f32[]{:T(128)} %bitcast.16, f32[]{:T(128)} %bitcast.15, f32[]{:T(128)} %bitcast.22, f32[]{:T(128)} %bitcast.21, f32[]{:T(128)} %bitcast.20, ...), kind=kLoop, calls=%fused_computation.13 | loop fusion | flops 458752 | bytes 786464 | tf_op jit(solution)/shard_map/add | solution.py:147
  15.1 5.1 %multiply_add_fusion.3 = (f32[1,32,1024]{2,1,0:T(8,128)S(1)}, f32[1,32,1024]{2,1,0:T(8,128)S(1)}) fusion(f32[4,32,1024]{2,1,0:T(8,128)S(1)} %get-tuple-element.48, f32[]{:T(128)} %bitcast.10, f32[]{:T(128)} %bitcast.9, f32[]{:T(128)} %bitcast.8, f32[]{:T(128)} %bitcast.6, f32[]{:T(128)} %bitcast.14, f32[]{:T(128)} %bitcast.13, f32[]{:T(128)} %bitcast.12, ...), kind=kLoop, calls=%fused_computation.15 | loop fusion | flops 458752 | bytes 786464 | tf_op jit(solution)/shard_map/add | solution.py:147
  20.5 49.4 %all-gather.3.cloned.1.call-done = bf16[128,32,1024]{2,1,0:T(8,128)(2,1)} async-done(((bf16[4,32,1024]{2,1,0:T(8,128)(2,1)}), bf16[128,32,1024]{2,1,0:T(8,128)(2,1)}) %all-gather.3.cloned.1.call-update) | async-done | bytes 8388624 | tf_op jit(solution)/shard_map/all_gather | solution.py:135
  69.9 3.4 copy-done
  73.3 4.6 %shard_map.77 = bf16[32,80,128]{2,1,0:T(8,128)(2,1)S(1)} custom-call(f32[9,2,4,4]{3,2,1,0:T(4,128)S(1)} %broadcast_select_fusion.mix_ref, bf16[64,1024]{1,0:T(8,128)(2,1)S(1)} %bitcast.90, bf16[32,4,32,1024]{3,2,1,0:T(8,128)(2,1)S(1)} %bitcast.73, f32[4,32,1024]{2,1,0:T(8,128)S(1)} %pad_maximum_fusion.look_ref), custom_call_target="tpu_custom_call" | custom-call | tf_op jit(solution)/shard_map/pallas_call | solution.py:65
  77.9 18.5 %all_to_all.45.moved_ref = bf16[32,80,128]{2,1,0:T(8,128)(2,1)S(1)} all-to-all(bf16[32,80,128]{2,1,0:T(8,128)(2,1)S(1)} %shard_map.77), channel_id=1, replica_groups=mesh['chain'=8,'bond'=32] {'bond'}, dimensions={0} | all-to-all | bytes 1310720 | tf_op jit(solution)/shard_map/all_to_all | solution.py:155
  96.4 2.0 shard_map.78
  98.4 2.6 collective-permute-start
  100.9 4.7 %collective-permute-done = bf16[64,1024]{1,0:T(8,128)(2,1)S(1)} collective-permute-done((bf16[64,1024]{1,0:T(8,128)(2,1)S(1)}, bf16[64,1024]{1,0:T(8,128)(2,1)S(1)}, u32[]{:S(2)}, u32[]{:S(2)}) %collective-permute-start) | collective-permute-done | bytes 131104 | tf_op jit(solution)/shard_map/ppermute | solution.py:160
  105.7 3.4 copy-done.1
  109.0 4.6 %shard_map.79 = bf16[32,80,128]{2,1,0:T(8,128)(2,1)S(1)} custom-call(f32[9,2,4,4]{3,2,1,0:T(4,128)S(1)} %broadcast_select_fusion.mix_ref, bf16[64,1024]{1,0:T(8,128)(2,1)S(1)} %bitcast_select_fusion.env_ref, bf16[32,4,32,1024]{3,2,1,0:T(8,128)(2,1)S(1)} %bitcast.75, f32[4,32,1024]{2,1,0:T(8,128)S(1)} %pad_maximum_fusion.look_ref), custom_call_target="tpu_custom_call" | custom-call | tf_op jit(solution)/shard_map/pallas_call | solution.py:65
  113.6 16.9 %all_to_all.46.moved_ref = bf16[32,80,128]{2,1,0:T(8,128)(2,1)S(1)} all-to-all(bf16[32,80,128]{2,1,0:T(8,128)(2,1)S(1)} %shard_map.79), channel_id=1, replica_groups=mesh['chain'=8,'bond'=32] {'bond'}, dimensions={0} | all-to-all | bytes 1310720 | tf_op jit(solution)/shard_map/all_to_all | solution.py:155
  130.5 2.0 shard_map.80
  132.5 2.6 collective-permute-start.1
  135.1 4.7 %collective-permute-done.1.env_ref = bf16[64,1024]{1,0:T(8,128)(2,1)S(1)} collective-permute-done((bf16[64,1024]{1,0:T(8,128)(2,1)S(1)}, bf16[64,1024]{1,0:T(8,128)(2,1)S(1)}, u32[]{:S(2)}, u32[]{:S(2)}) %collective-permute-start.1) | collective-permute-done | bytes 131104 | tf_op jit(solution)/shard_map/ppermute | solution.py:160
  139.8 4.6 %shard_map.81 = bf16[32,80,128]{2,1,0:T(8,128)(2,1)S(1)} custom-call(f32[9,2,4,4]{3,2,1,0:T(4,128)S(1)} %broadcast_select_fusion.mix_ref, bf16[64,1024]{1,0:T(8,128)(2,1)S(1)} %collective-permute-done.1.env_ref, bf16[32,4,32,1024]{3,2,1,0:T(8,128)(2,1)S(1)} %bitcast.77, f32[4,32,1024]{2,1,0:T(8,128)S(1)} %pad_maximum_fusion.look_ref), custom_call_target="tpu_custom_call" | custom-call | tf_op jit(solution)/shard_map/pallas_call | solution.py:65
  144.4 16.9 %all_to_all.47.moved_ref = bf16[32,80,128]{2,1,0:T(8,128)(2,1)S(1)} all-to-all(bf16[32,80,128]{2,1,0:T(8,128)(2,1)S(1)} %shard_map.81), channel_id=1, replica_groups=mesh['chain'=8,'bond'=32] {'bond'}, dimensions={0} | all-to-all | bytes 1310720 | tf_op jit(solution)/shard_map/all_to_all | solution.py:155
  161.3 2.0 shard_map.82
  163.3 2.6 collective-permute-start.2
  165.9 4.7 %collective-permute-done.2.env_ref = bf16[64,1024]{1,0:T(8,128)(2,1)S(1)} collective-permute-done((bf16[64,1024]{1,0:T(8,128)(2,1)S(1)}, bf16[64,1024]{1,0:T(8,128)(2,1)S(1)}, u32[]{:S(2)}, u32[]{:S(2)}) %collective-permute-start.2) | collective-permute-done | bytes 131104 | tf_op jit(solution)/shard_map/ppermute | solution.py:160
  170.6 4.6 %shard_map.83 = bf16[32,80,128]{2,1,0:T(8,128)(2,1)S(1)} custom-call(f32[9,2,4,4]{3,2,1,0:T(4,128)S(1)} %broadcast_select_fusion.mix_ref, bf16[64,1024]{1,0:T(8,128)(2,1)S(1)} %collective-permute-done.2.env_ref, bf16[32,4,32,1024]{3,2,1,0:T(8,128)(2,1)S(1)} %bitcast.79, f32[4,32,1024]{2,1,0:T(8,128)S(1)} %pad_maximum_fusion.look_ref), custom_call_target="tpu_custom_call" | custom-call | tf_op jit(solution)/shard_map/pallas_call | solution.py:65
  175.2 16.9 %all_to_all.48.moved_ref = bf16[32,80,128]{2,1,0:T(8,128)(2,1)S(1)} all-to-all(bf16[32,80,128]{2,1,0:T(8,128)(2,1)S(1)} %shard_map.83), channel_id=1, replica_groups=mesh['chain'=8,'bond'=32] {'bond'}, dimensions={0} | all-to-all | bytes 1310720 | tf_op jit(solution)/shard_map/all_to_all | solution.py:155
  192.1 2.0 shard_map.84
  194.1 2.6 collective-permute-start.3
  196.7 5.9 %collective-permute-done.3.env_ref = bf16[64,1024]{1,0:T(8,128)(2,1)S(1)} collective-permute-done((bf16[64,1024]{1,0:T(8,128)(2,1)S(1)}, bf16[64,1024]{1,0:T(8,128)(2,1)S(1)}, u32[]{:S(2)}, u32[]{:S(2)}) %collective-permute-start.3) | collective-permute-done | bytes 131104 | tf_op jit(solution)/shard_map/ppermute | solution.py:160
  202.6 5.5 %shard_map.85 = bf16[32,80,128]{2,1,0:T(8,128)(2,1)} custom-call(f32[9,2,4,4]{3,2,1,0:T(4,128)S(1)} %broadcast_select_fusion.mix_ref, bf16[64,1024]{1,0:T(8,128)(2,1)S(1)} %collective-permute-done.3.env_ref, bf16[32,4,32,1024]{3,2,1,0:T(8,128)(2,1)S(1)} %bitcast.81, f32[4,32,1024]{2,1,0:T(8,128)S(1)} %pad_maximum_fusion.look_ref), custom_call_target="tpu_custom_call" | custom-call | tf_op jit(solution)/shard_map/pallas_call | solution.py:65
  208.0 3.9 %all-to-all-start.4 = ((bf16[32,80,128]{2,1,0:T(8,128)(2,1)}), bf16[32,80,128]{2,1,0:T(8,128)(2,1)S(1)}, u32[]{:S(2)}, u32[]{:S(2)}) async-start(bf16[32,80,128]{2,1,0:T(8,128)(2,1)} %shard_map.85), calls=%async_computation.4 | async-start | bytes 1310720 | tf_op jit(solution)/shard_map/all_to_all | solution.py:155
  211.9 13.2 %all-to-all-done.4.moved_ref = bf16[32,80,128]{2,1,0:T(8,128)(2,1)S(1)} async-done(((bf16[32,80,128]{2,1,0:T(8,128)(2,1)}), bf16[32,80,128]{2,1,0:T(8,128)(2,1)S(1)}, u32[]{:S(2)}, u32[]{:S(2)}) %all-to-all-start.4) | async-done | bytes 655392 | tf_op jit(solution)/shard_map/all_to_all | solution.py:155
  225.2 3.4 copy-done.2
  228.5 2.0 shard_map.86
  230.6 1.9 collective-permute-start.4
  232.5 7.0 %collective-permute-done.4.env_ref = bf16[64,1024]{1,0:T(8,128)(2,1)S(1)} collective-permute-done((bf16[64,1024]{1,0:T(8,128)(2,1)S(1)}, bf16[64,1024]{1,0:T(8,128)(2,1)S(1)}, u32[]{:S(2)}, u32[]{:S(2)}) %collective-permute-start.4) | collective-permute-done | bytes 131104 | tf_op jit(solution)/shard_map/ppermute | solution.py:160
  239.5 5.5 %shard_map.87 = bf16[32,80,128]{2,1,0:T(8,128)(2,1)} custom-call(f32[9,2,4,4]{3,2,1,0:T(4,128)S(1)} %broadcast_select_fusion.mix_ref, bf16[64,1024]{1,0:T(8,128)(2,1)S(1)} %collective-permute-done.4.env_ref, bf16[32,4,32,1024]{3,2,1,0:T(8,128)(2,1)S(1)} %bitcast.83, f32[4,32,1024]{2,1,0:T(8,128)S(1)} %pad_maximum_fusion.look_ref), custom_call_target="tpu_custom_call" | custom-call | tf_op jit(solution)/shard_map/pallas_call | solution.py:65
  245.0 3.9 %all-to-all-start.5 = ((bf16[32,80,128]{2,1,0:T(8,128)(2,1)}), bf16[32,80,128]{2,1,0:T(8,128)(2,1)S(1)}, u32[]{:S(2)}, u32[]{:S(2)}) async-start(bf16[32,80,128]{2,1,0:T(8,128)(2,1)} %shard_map.87), calls=%async_computation.5 | async-start | bytes 1310720 | tf_op jit(solution)/shard_map/all_to_all | solution.py:155
  249.0 13.2 %all-to-all-done.5.moved_ref = bf16[32,80,128]{2,1,0:T(8,128)(2,1)S(1)} async-done(((bf16[32,80,128]{2,1,0:T(8,128)(2,1)}), bf16[32,80,128]{2,1,0:T(8,128)(2,1)S(1)}, u32[]{:S(2)}, u32[]{:S(2)}) %all-to-all-start.5) | async-done | bytes 655392 | tf_op jit(solution)/shard_map/all_to_all | solution.py:155
  262.1 3.4 copy-done.3
  265.5 2.0 shard_map.88
  267.5 1.9 collective-permute-start.5
  269.5 6.5 %collective-permute-done.5.env_ref = bf16[64,1024]{1,0:T(8,128)(2,1)S(1)} collective-permute-done((bf16[64,1024]{1,0:T(8,128)(2,1)S(1)}, bf16[64,1024]{1,0:T(8,128)(2,1)S(1)}, u32[]{:S(2)}, u32[]{:S(2)}) %collective-permute-start.5) | collective-permute-done | bytes 131104 | tf_op jit(solution)/shard_map/ppermute | solution.py:160
  276.0 5.5 %shard_map.89 = bf16[32,80,128]{2,1,0:T(8,128)(2,1)} custom-call(f32[9,2,4,4]{3,2,1,0:T(4,128)S(1)} %broadcast_select_fusion.mix_ref, bf16[64,1024]{1,0:T(8,128)(2,1)S(1)} %collective-permute-done.5.env_ref, bf16[32,4,32,1024]{3,2,1,0:T(8,128)(2,1)S(1)} %bitcast.85, f32[4,32,1024]{2,1,0:T(8,128)S(1)} %pad_maximum_fusion.look_ref), custom_call_target="tpu_custom_call" | custom-call | tf_op jit(solution)/shard_map/pallas_call | solution.py:65
  281.5 4.1 %all-to-all-start.6 = ((bf16[32,80,128]{2,1,0:T(8,128)(2,1)}), bf16[32,80,128]{2,1,0:T(8,128)(2,1)S(1)}, u32[]{:S(2)}, u32[]{:S(2)}) async-start(bf16[32,80,128]{2,1,0:T(8,128)(2,1)} %shard_map.89), calls=%async_computation.6 | async-start | bytes 1310720 | tf_op jit(solution)/shard_map/all_to_all | solution.py:155
  285.6 13.0 %all-to-all-done.6.moved_ref = bf16[32,80,128]{2,1,0:T(8,128)(2,1)S(1)} async-done(((bf16[32,80,128]{2,1,0:T(8,128)(2,1)}), bf16[32,80,128]{2,1,0:T(8,128)(2,1)S(1)}, u32[]{:S(2)}, u32[]{:S(2)}) %all-to-all-start.6) | async-done | bytes 655392 | tf_op jit(solution)/shard_map/all_to_all | solution.py:155
  298.6 3.4 copy-done.4
  302.0 2.0 shard_map.90
  304.0 1.9 collective-permute-start.6
  305.9 6.5 %collective-permute-done.6.env_ref = bf16[64,1024]{1,0:T(8,128)(2,1)S(1)} collective-permute-done((bf16[64,1024]{1,0:T(8,128)(2,1)S(1)}, bf16[64,1024]{1,0:T(8,128)(2,1)S(1)}, u32[]{:S(2)}, u32[]{:S(2)}) %collective-permute-start.6) | collective-permute-done | bytes 131104 | tf_op jit(solution)/shard_map/ppermute | solution.py:160
  312.5 5.5 %shard_map.91 = bf16[32,80,128]{2,1,0:T(8,128)(2,1)} custom-call(f32[9,2,4,4]{3,2,1,0:T(4,128)S(1)} %broadcast_select_fusion.mix_ref, bf16[64,1024]{1,0:T(8,128)(2,1)S(1)} %collective-permute-done.6.env_ref, bf16[32,4,32,1024]{3,2,1,0:T(8,128)(2,1)S(1)} %bitcast.87, f32[4,32,1024]{2,1,0:T(8,128)S(1)} %pad_maximum_fusion.look_ref), custom_call_target="tpu_custom_call" | custom-call | tf_op jit(solution)/shard_map/pallas_call | solution.py:65
  318.0 3.9 %all-to-all-start.7 = ((bf16[32,80,128]{2,1,0:T(8,128)(2,1)}), bf16[32,80,128]{2,1,0:T(8,128)(2,1)S(1)}, u32[]{:S(2)}, u32[]{:S(2)}) async-start(bf16[32,80,128]{2,1,0:T(8,128)(2,1)} %shard_map.91), calls=%async_computation.7 | async-start | bytes 1310720 | tf_op jit(solution)/shard_map/all_to_all | solution.py:155
  321.9 13.2 %all-to-all-done.7.moved_ref = bf16[32,80,128]{2,1,0:T(8,128)(2,1)S(1)} async-done(((bf16[32,80,128]{2,1,0:T(8,128)(2,1)}), bf16[32,80,128]{2,1,0:T(8,128)(2,1)S(1)}, u32[]{:S(2)}, u32[]{:S(2)}) %all-to-all-start.7) | async-done | bytes 655392 | tf_op jit(solution)/shard_map/all_to_all | solution.py:155
  335.1 3.4 copy-done.5
  338.5 2.0 shard_map.92
  340.5 1.9 collective-permute-start.7
  342.4 6.5 %collective-permute-done.7.env_ref = bf16[64,1024]{1,0:T(8,128)(2,1)S(1)} collective-permute-done((bf16[64,1024]{1,0:T(8,128)(2,1)S(1)}, bf16[64,1024]{1,0:T(8,128)(2,1)S(1)}, u32[]{:S(2)}, u32[]{:S(2)}) %collective-permute-start.7) | collective-permute-done | bytes 131104 | tf_op jit(solution)/shard_map/ppermute | solution.py:160
  349.0 5.5 %shard_map.93 = bf16[32,80,128]{2,1,0:T(8,128)(2,1)} custom-call(f32[9,2,4,4]{3,2,1,0:T(4,128)S(1)} %broadcast_select_fusion.mix_ref, bf16[64,1024]{1,0:T(8,128)(2,1)S(1)} %collective-permute-done.7.env_ref, bf16[32,4,32,1024]{3,2,1,0:T(8,128)(2,1)S(1)} %bitcast.89, f32[4,32,1024]{2,1,0:T(8,128)S(1)} %pad_maximum_fusion.look_ref), custom_call_target="tpu_custom_call" | custom-call | tf_op jit(solution)/shard_map/pallas_call | solution.py:65
  354.4 3.9 %all-to-all-start.8 = ((bf16[32,80,128]{2,1,0:T(8,128)(2,1)}), bf16[32,80,128]{2,1,0:T(8,128)(2,1)S(1)}, u32[]{:S(2)}, u32[]{:S(2)}) async-start(bf16[32,80,128]{2,1,0:T(8,128)(2,1)} %shard_map.93), calls=%async_computation.8 | async-start | bytes 1310720 | tf_op jit(solution)/shard_map/all_to_all | solution.py:155
  358.4 13.2 %all-to-all-done.8 = bf16[32,80,128]{2,1,0:T(8,128)(2,1)S(1)} async-done(((bf16[32,80,128]{2,1,0:T(8,128)(2,1)}), bf16[32,80,128]{2,1,0:T(8,128)(2,1)S(1)}, u32[]{:S(2)}, u32[]{:S(2)}) %all-to-all-start.8) | async-done | bytes 655392 | tf_op jit(solution)/shard_map/all_to_all | solution.py:155
  371.6 5.0 %shard_map.94 = (bf16[9,64,1024]{2,1,0:T(8,128)(2,1)S(1)}, f32[16,128]{1,0:T(8,128)S(1)}) fusion(bf16[9,64,1024]{2,1,0:T(8,128)(2,1)S(1)} %bitcast_dynamic-update-slice_fusion.1, bf16[32,80,128]{2,1,0:T(8,128)(2,1)S(1)} %all-to-all-done.8, bf16[32,4,32,1024]{3,2,1,0:T(8,128)(2,1)} %bitcast.72), kind=kCustom, calls=%fused_computation.2 | custom fusion | bytes 9183232 | tf_op jit(solution)/shard_map/pallas_call | solution.py:105
  376.5 0.7 constant_dynamic-slice_fusion
  377.5 0.6 reshape.63
  (49 shorter events, 0.7 us)
Async XLA Ops:
  7.2 1.9 copy-start.9
  7.2 1.9 copy-start.7
  7.2 2.1 copy-start.8
  7.2 62.7 %all-gather.3.cloned.1.call-start = ((), (), s32[]{:S(2)}) async-start(), calls=%async_computation.9 | async-start | bytes 8650752 | tf_op jit(solution)/shard_map/all_gather | solution.py:135
  10.2 10.1 %copy-start.10 = (s32[4]{0:T(128)S(1)}, s32[4]{0:T(128)}, u32[]{:S(2)}) copy-start(s32[4]{0:T(128)} %param.9) | copy-start | bytes 52
  15.1 5.3 %copy-start.6 = (bf16[4,32,1024]{2,1,0:T(8,128)(2,1)S(1)}, bf16[4,32,1024]{2,1,0:T(8,128)(2,1)}, u32[]{:S(2)}) copy-start(bf16[4,32,1024]{2,1,0:T(8,128)(2,1)} %param.7) | copy-start | bytes 786436
  69.9 3.4 copy-start
  98.4 7.3 %collective-permute-start = (bf16[64,1024]{1,0:T(8,128)(2,1)S(1)}, bf16[64,1024]{1,0:T(8,128)(2,1)S(1)}, u32[]{:S(2)}, u32[]{:S(2)}) collective-permute-start(bf16[64,1024]{1,0:T(8,128)(2,1)S(1)} %get-tuple-element.20), channel_id=1, source_target_pairs={{0,32},{32,64},{64,96},{96,128},{128,160},{160,192},{192,224},{1,3... | collective-permute-start | bytes 393224 | tf_op jit(solution)/shard_map/ppermute | solution.py:160
  105.6 3.4 copy-start.1
  132.5 7.3 %collective-permute-start.1 = (bf16[64,1024]{1,0:T(8,128)(2,1)S(1)}, bf16[64,1024]{1,0:T(8,128)(2,1)S(1)}, u32[]{:S(2)}, u32[]{:S(2)}) collective-permute-start(bf16[64,1024]{1,0:T(8,128)(2,1)S(1)} %get-tuple-element.21), channel_id=1, source_target_pairs={{0,32},{32,64},{64,96},{96,128},{128,160},{160,192},{192,224},{1,3... | collective-permute-start | bytes 393224 | tf_op jit(solution)/shard_map/ppermute | solution.py:160
  163.3 7.3 %collective-permute-start.2 = (bf16[64,1024]{1,0:T(8,128)(2,1)S(1)}, bf16[64,1024]{1,0:T(8,128)(2,1)S(1)}, u32[]{:S(2)}, u32[]{:S(2)}) collective-permute-start(bf16[64,1024]{1,0:T(8,128)(2,1)S(1)} %get-tuple-element.22), channel_id=1, source_target_pairs={{0,32},{32,64},{64,96},{96,128},{128,160},{160,192},{192,224},{1,3... | collective-permute-start | bytes 393224 | tf_op jit(solution)/shard_map/ppermute | solution.py:160
  194.1 8.5 %collective-permute-start.3 = (bf16[64,1024]{1,0:T(8,128)(2,1)S(1)}, bf16[64,1024]{1,0:T(8,128)(2,1)S(1)}, u32[]{:S(2)}, u32[]{:S(2)}) collective-permute-start(bf16[64,1024]{1,0:T(8,128)(2,1)S(1)} %get-tuple-element.23), channel_id=1, source_target_pairs={{0,32},{32,64},{64,96},{96,128},{128,160},{160,192},{192,224},{1,3... | collective-permute-start | bytes 393224 | tf_op jit(solution)/shard_map/ppermute | solution.py:160
  208.0 17.1 %all-to-all-start.4 = ((bf16[32,80,128]{2,1,0:T(8,128)(2,1)}), bf16[32,80,128]{2,1,0:T(8,128)(2,1)S(1)}, u32[]{:S(2)}, u32[]{:S(2)}) async-start(bf16[32,80,128]{2,1,0:T(8,128)(2,1)} %shard_map.85), calls=%async_computation.4 | async-start | bytes 1310720 | tf_op jit(solution)/shard_map/all_to_all | solution.py:155
  225.2 3.4 copy-start.2
  230.6 9.0 %collective-permute-start.4 = (bf16[64,1024]{1,0:T(8,128)(2,1)S(1)}, bf16[64,1024]{1,0:T(8,128)(2,1)S(1)}, u32[]{:S(2)}, u32[]{:S(2)}) collective-permute-start(bf16[64,1024]{1,0:T(8,128)(2,1)S(1)} %get-tuple-element.24), channel_id=1, source_target_pairs={{0,32},{32,64},{64,96},{96,128},{128,160},{160,192},{192,224},{1,3... | collective-permute-start | bytes 393224 | tf_op jit(solution)/shard_map/ppermute | solution.py:160
  245.0 17.1 %all-to-all-start.5 = ((bf16[32,80,128]{2,1,0:T(8,128)(2,1)}), bf16[32,80,128]{2,1,0:T(8,128)(2,1)S(1)}, u32[]{:S(2)}, u32[]{:S(2)}) async-start(bf16[32,80,128]{2,1,0:T(8,128)(2,1)} %shard_map.87), calls=%async_computation.5 | async-start | bytes 1310720 | tf_op jit(solution)/shard_map/all_to_all | solution.py:155
  262.1 3.4 copy-start.3
  267.5 8.5 %collective-permute-start.5 = (bf16[64,1024]{1,0:T(8,128)(2,1)S(1)}, bf16[64,1024]{1,0:T(8,128)(2,1)S(1)}, u32[]{:S(2)}, u32[]{:S(2)}) collective-permute-start(bf16[64,1024]{1,0:T(8,128)(2,1)S(1)} %get-tuple-element.25), channel_id=1, source_target_pairs={{0,32},{32,64},{64,96},{96,128},{128,160},{160,192},{192,224},{1,3... | collective-permute-start | bytes 393224 | tf_op jit(solution)/shard_map/ppermute | solution.py:160
  281.5 17.1 %all-to-all-start.6 = ((bf16[32,80,128]{2,1,0:T(8,128)(2,1)}), bf16[32,80,128]{2,1,0:T(8,128)(2,1)S(1)}, u32[]{:S(2)}, u32[]{:S(2)}) async-start(bf16[32,80,128]{2,1,0:T(8,128)(2,1)} %shard_map.89), calls=%async_computation.6 | async-start | bytes 1310720 | tf_op jit(solution)/shard_map/all_to_all | solution.py:155
  298.6 3.4 copy-start.4
  304.0 8.5 %collective-permute-start.6 = (bf16[64,1024]{1,0:T(8,128)(2,1)S(1)}, bf16[64,1024]{1,0:T(8,128)(2,1)S(1)}, u32[]{:S(2)}, u32[]{:S(2)}) collective-permute-start(bf16[64,1024]{1,0:T(8,128)(2,1)S(1)} %get-tuple-element.26), channel_id=1, source_target_pairs={{0,32},{32,64},{64,96},{96,128},{128,160},{160,192},{192,224},{1,3... | collective-permute-start | bytes 393224 | tf_op jit(solution)/shard_map/ppermute | solution.py:160
  318.0 17.1 %all-to-all-start.7 = ((bf16[32,80,128]{2,1,0:T(8,128)(2,1)}), bf16[32,80,128]{2,1,0:T(8,128)(2,1)S(1)}, u32[]{:S(2)}, u32[]{:S(2)}) async-start(bf16[32,80,128]{2,1,0:T(8,128)(2,1)} %shard_map.91), calls=%async_computation.7 | async-start | bytes 1310720 | tf_op jit(solution)/shard_map/all_to_all | solution.py:155
  335.1 3.4 copy-start.5
  340.5 8.5 %collective-permute-start.7 = (bf16[64,1024]{1,0:T(8,128)(2,1)S(1)}, bf16[64,1024]{1,0:T(8,128)(2,1)S(1)}, u32[]{:S(2)}, u32[]{:S(2)}) collective-permute-start(bf16[64,1024]{1,0:T(8,128)(2,1)S(1)} %get-tuple-element.27), channel_id=1, source_target_pairs={{0,32},{32,64},{64,96},{96,128},{128,160},{160,192},{192,224},{1,3... | collective-permute-start | bytes 393224 | tf_op jit(solution)/shard_map/ppermute | solution.py:160
  354.4 17.1 %all-to-all-start.8 = ((bf16[32,80,128]{2,1,0:T(8,128)(2,1)}), bf16[32,80,128]{2,1,0:T(8,128)(2,1)S(1)}, u32[]{:S(2)}, u32[]{:S(2)}) async-start(bf16[32,80,128]{2,1,0:T(8,128)(2,1)} %shard_map.93), calls=%async_computation.8 | async-start | bytes 1310720 | tf_op jit(solution)/shard_map/all_to_all | solution.py:155
Sparse Core Ops, SparseCore 0:
  11.2 58.6 all-gather.2

commit v2 on v0

v2 whole, which is shorter than its diff:
```python
import functools
import math

import jax
import jax.numpy as jnp
from jax import lax
from jax.experimental import pallas as pl
from jax.experimental.pallas import tpu as pltpu
from jax.sharding import Mesh
from jax.sharding import PartitionSpec as P

EXTRA = 16
MIB = 1 << 20
COLS = 256


def split3(value):
    high = value.astype(jnp.bfloat16).astype(jnp.float32)
    rest = value - high
    mid = rest.astype(jnp.bfloat16).astype(jnp.float32)
    return high, mid, rest - mid


def parts_of(value, lanes):
    rows = [jnp.broadcast_to(p, (1, lanes)) for p in split3(value)]
    rows.append(jnp.zeros((EXTRA - 3, lanes), jnp.float32))
    return jnp.concatenate(rows, axis=0).astype(jnp.bfloat16)


def columns(tensor_ref, t, c):
    if len(tensor_ref.shape) == 4:
        return tensor_ref[:, t, :, c * COLS : (c + 1) * COLS].reshape(-1, COLS)
    per = tensor_ref.shape[5] // COLS
    at = c % per * COLS
    return tensor_ref[:, c // per, :, t, :, at : at + COLS].reshape(-1, COLS)


def block(tensor_ref, d, s, c):
    if len(tensor_ref.shape) == 4:
        return tensor_ref[d, s, :, c * COLS : (c + 1) * COLS].reshape(-1, COLS)
    per = tensor_ref.shape[5] // COLS
    at = c % per * COLS
    return tensor_ref[d // 2, c // per, d % 2, s, :, at : at + COLS].reshape(-1, COLS)


def spread(slot, where_ref, mix_ref, look_ref, env, tensor_ref, out_ref, arrived=None):
    width = env.shape[1]
    phys = mix_ref.shape[1]
    panel = env.shape[0] // 2
    half = width // panel // 2
    mem = where_ref[0]
    total = jnp.zeros((1, 128), jnp.float32)
    for c in range(width // COLS):
        if arrived is not None:
            arrived[c]()
        prods = [
            jnp.dot(env, columns(tensor_ref, t, c), preferred_element_type=jnp.float32)
            for t in range(phys)
        ]
        for s in range(phys):
            own = jnp.concatenate(
                [block(tensor_ref, h * half + mem, s, c) for h in range(2)], axis=0
            ).astype(jnp.float32)
            seen = own * sum(look_ref[slot, s, t] * prods[t] for t in range(phys))
            line = jnp.sum(seen, axis=0, keepdims=True)
            total += sum(line[:, b : b + 128] for b in range(0, COLS, 128))
        mixed = [sum(mix_ref[slot, s, t] * prods[t] for t in range(phys)) for s in range(phys)]
        tall = jnp.concatenate(
            [mixed[s][h * panel : (h + 1) * panel] for h in range(2) for s in range(phys)], axis=0
        )
        turned = tall.astype(jnp.bfloat16).T.reshape(COLS // panel, panel, 2 * phys * panel)
        first = c * (COLS // panel)
        h, first = first // half, first % half
        out_ref[first : first + COLS // panel, h * panel : (h + 1) * panel, :] = turned
    return jnp.sum(total, axis=1, keepdims=True)


def gather(moved_ref, tensor_ref, env_ref):
    rows, width = env_ref.shape
    half = moved_ref.shape[0]
    if moved_ref.shape[1] < rows:
        left = [
            jnp.concatenate([moved_ref[g], moved_ref[g + 1]], axis=0) for g in range(0, half, 2)
        ]
    else:
        left = [moved_ref[g, :rows] for g in range(half)]
    left = jnp.concatenate(left, axis=1)
    for c in range(width // COLS):
        right = jnp.concatenate(
            [
                block(tensor_ref, h * half + g, slice(None), c)
                for g in range(half)
                for h in range(2)
            ],
            axis=0,
        )
        env_ref[:, c * COLS : (c + 1) * COLS] = jnp.dot(
            left, right, preferred_element_type=jnp.float32
        ).astype(jnp.bfloat16)


def chip_of(side, where_ref, at, m, k):
    y, x = where_ref[2], where_ref[3]
    along = lax.rem(y + side - jnp.where(at == 0, m, k), side)
    across = lax.rem(x + side - jnp.where(at == 0, k, m), side)
    return along * side + across


def lay(side, where_ref, pieces, tensor_ref, sems):
    copies = []
    for i, ref in enumerate(pieces):
        at = where_ref[4] if i < side else 1 - where_ref[4]
        for k in range(side):
            place = tensor_ref.at[chip_of(side, where_ref, at, i % side, k), at]
            copies.append(pltpu.make_async_copy(ref.at[k], place, sems.at[i, k]))
    for copy in copies:
        copy.start()
    for copy in copies:
        copy.wait()


def lay_kernel(side, where_ref, *refs):
    lay(side, where_ref, refs[:-2], refs[-2], refs[-1])


def pieces_kernel(side, where_ref, moved_ref, *refs):
    pieces, (env_ref, tensor, sems) = refs[:-3], refs[-3:]
    lay(side, where_ref, pieces, tensor, sems)
    gather(moved_ref, tensor, env_ref)


def stream_kernel(
    now, where_ref, mix_ref, look_ref, env_ref, tensor_ref, seen_ref, out_ref, new_ref, held, sems
):
    copies = []
    for c in range(held.shape[3] // COLS):
        cols = pl.ds(c * COLS, COLS)
        copies.append(
            pltpu.make_async_copy(
                tensor_ref.at[:, :, :, cols], held.at[:, :, :, cols], sems.at[c]
            )
        )
        copies[-1].start()
    arrived = [copy.wait for copy in copies]
    value = spread(1, where_ref, mix_ref, look_ref, env_ref[...], held, out_ref, arrived)
    new_ref[0] = seen_ref[0]
    new_ref[1] = jnp.broadcast_to(value, new_ref.shape[1:])


def start_kernel(side, where_ref, mix_ref, look_ref, env_ref, twin_ref, *refs):
    pieces, (out_ref, new_ref, tensor, sems) = refs[:-4], refs[-4:]
    core = where_ref[4]
    copies = []
    for m, ref in enumerate(pieces):
        for k in range(side):
            place = tensor.at[chip_of(side, where_ref, core, m, k)]
            copies.append(pltpu.make_async_copy(ref.at[k], place, sems.at[m, k]))
    for copy in copies:
        copy.start()
    own, twin = env_ref[...], twin_ref[...]
    env = jnp.concatenate(
        [jnp.where(core == 0, own, twin), jnp.where(core == 0, twin, own)], axis=0
    )
    for copy in copies:
        copy.wait()
    chips, _, phys, panel, wide = tensor.shape
    mem = where_ref[0] // 2
    total = jnp.zeros((1, 128), jnp.float32)
    for c in range(wide // COLS):
        cols = slice(c * COLS, (c + 1) * COLS)
        prods = [
            jnp.dot(
                env, tensor[:, :, t, :, cols].reshape(-1, COLS), preferred_element_type=jnp.float32
            )
            for t in range(phys)
        ]
        for s in range(phys):
            rows = [tensor[h * (chips // 2) + mem, o, s, :, cols] for o in range(2) for h in range(2)]
            seen = jnp.concatenate(rows, axis=0).astype(jnp.float32)
            seen = seen * sum(look_ref[0, s, t] * prods[t] for t in range(phys))
            line = jnp.sum(seen, axis=0, keepdims=True)
            total += sum(line[:, b : b + 128] for b in range(0, COLS, 128))
        mixed = [sum(mix_ref[0, s, t] * prods[t] for t in range(phys)) for s in range(phys)]
        tall = [mixed[s][q * panel : (q + 1) * panel] for q in range(4) for s in range(phys)]
        turned = jnp.concatenate(tall, axis=0).astype(jnp.bfloat16).T
        per = COLS // panel
        out_ref[c * per : (c + 1) * per] = turned.reshape(per, panel, 4 * phys * panel)
    value = jnp.sum(total, axis=1, keepdims=True)
    new_ref[...] = jnp.broadcast_to(value, new_ref.shape)


def first_kernel(now, where_ref, mix_ref, look_ref, env_ref, tensor_ref, seen_ref, out_ref, new_ref):
    value = spread(0, where_ref, mix_ref, look_ref, env_ref[...], tensor_ref, out_ref)
    new_ref[0] = jnp.where(where_ref[1] == now, value, seen_ref[0])
    new_ref[1] = seen_ref[1]


def middle_kernel(
    now, where_ref, mix_ref, look_ref, moved_ref, old_ref, tensor_ref, seen_ref, out_ref, new_ref, env_ref
):
    gather(moved_ref, old_ref, env_ref)
    value = spread(1, where_ref, mix_ref, look_ref, env_ref[...], tensor_ref, out_ref)
    new_ref[0] = seen_ref[0]
    new_ref[1] = jnp.where(where_ref[1] == now, value, seen_ref[1])


def end_kernel(
    now, where_ref, mix_ref, look_ref, moved_ref, old_ref, tensor_ref, seen_ref, out_ref, env_ref
):
    gather(moved_ref, old_ref, env_ref)
    value = spread(1, where_ref, mix_ref, look_ref, env_ref[...], tensor_ref, out_ref)
    rows, lanes = env_ref.shape[0], out_ref.shape[2]
    odd = jnp.where(where_ref[1] == now, value, seen_ref[1][:1, :1])
    extra = jnp.concatenate([parts_of(v, lanes // 2) for v in (seen_ref[0][:1, :1], odd)], axis=1)
    out_ref[:, rows:, :] = jnp.broadcast_to(extra[None], (out_ref.shape[0], EXTRA, lanes))


def second_kernel(moved_ref, tensor_ref, env_ref):
    gather(moved_ref, tensor_ref, env_ref)


def home_kernel(where_ref, moved_ref, tensor_ref, *refs):
    kept, (out_ref, env, picked, sems) = refs[:-4], refs[-4:]
    count = (len(kept) + 1) // 2
    rows = env.shape[0]
    panel = rows // 2

    def each(act):
        for i, ref in enumerate(kept):
            q, p = i // count, i % count
            copy = pltpu.make_async_copy(ref, picked.at[q], sems.at[q])
            pl.when(where_ref[1] == p)(getattr(copy, act))

    each("start")
    gather(moved_ref, tensor_ref, env)
    each("wait")
    now = where_ref[1] == count - 1
    values = jnp.sum(moved_ref[:, rows:].astype(jnp.float32), axis=0)
    for q in range(2):
        result = picked[0] if q == 0 else jnp.where(now, env[...], picked[1])
        value = jnp.sum(values[:, q * 128 : q * 128 + 1], axis=0, keepdims=True)
        extra = parts_of(value, out_ref.shape[2])
        for h in range(2):
            out_ref[2 * q + h, :panel] = result[h * panel : (h + 1) * panel]
            out_ref[2 * q + h, panel:] = extra


def mix_kernel(width, where_ref, site_ref, kind_ref, operators_ref, probe_ref, mix_ref, look_ref):
    pair, front = where_ref[1], where_ref[6]
    kind, site = kind_ref[front], site_ref[front]
    phys = probe_ref.shape[0]
    scale = 1.0 / math.sqrt(width)
    for slot in range(2):
        for s in range(phys):
            for t in range(phys):
                row, col = (s, t) if slot == 0 else (t, s)
                own = 1.0 if s == t else 0.0
                mix_ref[slot, s, t] = jnp.where(
                    site == 2 * pair + slot, operators_ref[kind, row, col], own
                )
                look_ref[slot, s, t] = probe_ref[row, col] * scale


def cut_kernel(
    where_ref, mine_ref, near_ref, start_ref, other_ref, later_ref, keep_ref, give_ref, env_ref, sem
):
    core, half, front, parity = where_ref[4], where_ref[5], where_ref[6], where_ref[7]
    panel = other_ref.shape[0]
    copy = pltpu.make_async_copy(
        start_ref.at[front], env_ref.at[pl.ds(pl.multiple_of(half * panel, panel), panel)], sem.at[0]
    )
    copy.start()
    env_ref[pl.ds(pl.multiple_of((1 - half) * panel, panel), panel)] = other_ref[...]
    wide = keep_ref.shape[2]
    mine, near = mine_ref[...], near_ref[...]
    later_ref[...] = jnp.where(parity == 0, near, mine)
    begun = jnp.where(parity == 0, mine, near)
    low, high = begun[..., :wide], begun[..., wide:]
    keep_ref[...] = jnp.where(core == 0, low, high)
    give_ref[...] = jnp.where(core == 0, high, low)
    copy.wait()


SMEM = pl.BlockSpec(memory_space=pltpu.SMEM)
VMEM = pl.BlockSpec(memory_space=pltpu.VMEM)
ANY = pl.BlockSpec(memory_space=pl.ANY)
HBM = pl.BlockSpec(memory_space=pltpu.HBM)


def params():
    return pltpu.CompilerParams(vmem_limit_bytes=16 * MIB)


def shifts(side, by, first):
    pairs = []
    for y in range(side):
        for x in range(side):
            for core in range(2):
                across = (core == 0) == first
                to = y * side + (x + by) % side if across else (y + by) % side * side + x
                pairs.append(((y * side + x) * 2 + core, to * 2 + core))
    return pairs


def in_hbm(arrays):
    return [pltpu.with_memory_space_constraint(a, pltpu.HBM) for a in arrays]


def first_ring(keep, give, core, side):
    bond = ("half", "member")
    other = lax.ppermute(give, bond, twins(side))
    chip = jnp.where(core == 0, jnp.stack([keep, other]), jnp.stack([other, keep]))
    return jnp.stack([chip] + [lax.ppermute(chip, bond, shifts(side, k, True)) for k in range(1, side)])


def second_ring(row, side):
    bond = ("half", "member")
    return [row] + [lax.ppermute(row, bond, shifts(side, m, False)) for m in range(1, side)]


def swap_cores(pieces, side):
    return [lax.ppermute(p, ("half", "member"), twins(side)) for p in pieces]


def twins(side):
    return [(i, i ^ 1) for i in range(2 * side * side)]


def on_device(site_tensors, start_env, operators, op_site, op_kind, probe):
    fronts, panel, width = start_env.shape
    phys = site_tensors.shape[2]
    kinds = operators.shape[0]
    pairs = lax.axis_size("pair")
    pair = lax.axis_index("pair")
    parity = lax.axis_index("parity")
    half = lax.axis_index("half")
    member = lax.axis_index("member")
    members = lax.axis_size("member")
    side = math.isqrt(members)
    rows = 2 * panel
    lanes = 2 * phys * panel
    f32 = jnp.float32
    bf16 = jnp.bfloat16
    core = member % 2
    chip = half * (members // 2) + member // 2
    front = 2 * parity + half
    where = jnp.stack([member, pair, chip // side, chip % side, core, half, front, parity]).astype(jnp.int32)

    mine = jnp.swapaxes(site_tensors[0], 0, 1)
    near = lax.ppermute(mine, "parity", [(0, 1), (1, 0)])
    given = lax.dynamic_index_in_dim(start_env, 2 * parity + 1 - half, 0, keepdims=False)
    other = lax.ppermute(given, "half", [(0, 1), (1, 0)])
    env_shape = jax.ShapeDtypeStruct((rows, width), bf16)
    square = jax.ShapeDtypeStruct((2, phys, phys), f32)
    part = jax.ShapeDtypeStruct((phys, panel, width // 2), bf16)
    bond = ("half", "member")
    mixes, looks = pl.pallas_call(
        functools.partial(mix_kernel, width),
        in_specs=[SMEM] * 5,
        out_specs=[SMEM] * 2,
        out_shape=[square, square],
        compiler_params=params(),
    )(where, op_site, op_kind, operators, probe)
    where, other, mine, near, mixes, looks = lax.optimization_barrier(
        (where, other, mine, near, mixes, looks)
    )
    small = (where, mixes, looks)
    later, keep, give, env = pl.pallas_call(
        cut_kernel,
        in_specs=[SMEM] + [VMEM] * 2 + [ANY, VMEM],
        out_specs=[VMEM] * 4,
        out_shape=[jax.ShapeDtypeStruct(mine.shape, bf16), part, part, env_shape],
        scratch_shapes=[pltpu.SemaphoreType.DMA((1,))],
        compiler_params=params(),
    )(where, mine, near, start_env, other)
    after = lax.all_gather(later, bond, axis=0)
    twin = lax.ppermute(env, bond, twins(side))
    row = first_ring(keep, give, core, side)
    row, twin = lax.optimization_barrier((row, twin))
    pieces = second_ring(row, side)
    swapped = swap_cores(pieces, side)

    def sent_shape(extra):
        return jax.ShapeDtypeStruct((members, rows + extra, lanes), bf16)

    seen_shape = jax.ShapeDtypeStruct((2, 8, 128), f32)

    def exchange(sent):
        return lax.all_to_all(sent, "member", 0, 0, tiled=True)

    sent, seen = pl.pallas_call(
        functools.partial(start_kernel, side),
        in_specs=[SMEM] * 3 + [VMEM] * 2 + [HBM] * side,
        out_specs=[VMEM] * 2,
        out_shape=[jax.ShapeDtypeStruct((members, panel, 2 * lanes), bf16), seen_shape],
        scratch_shapes=[
            pltpu.VMEM((side * side, 2, phys, panel, width // 2), bf16),
            pltpu.SemaphoreType.DMA((side, side)),
        ],
        compiler_params=params(),
    )(*small, env, twin, *in_hbm(pieces))
    moved = exchange(sent)
    whole = (side * side, 2, 2, phys, panel, width // 2)
    lay_sems = pltpu.SemaphoreType.DMA((2 * side, side))
    everything = pieces + swapped
    env = pl.pallas_call(
        functools.partial(pieces_kernel, side),
        in_specs=[SMEM, VMEM] + [HBM] * (2 * side),
        out_specs=VMEM,
        out_shape=env_shape,
        scratch_shapes=[pltpu.VMEM(whole, bf16), lay_sems],
        compiler_params=params(),
    )(where, moved, *in_hbm(everything))
    evens, odds = [env], []
    env, after = lax.optimization_barrier((env, after))
    sent, seen = pl.pallas_call(
        functools.partial(stream_kernel, 0),
        in_specs=[SMEM] * 3 + [VMEM, HBM, VMEM],
        out_specs=[VMEM] * 2,
        out_shape=[sent_shape(0), seen_shape],
        scratch_shapes=[
            pltpu.VMEM(after.shape, bf16),
            pltpu.SemaphoreType.DMA((width // COLS,)),
        ],
        compiler_params=params(),
    )(*small, env, *in_hbm([after]), seen)
    after = pltpu.with_memory_space_constraint(after, pltpu.VMEM)
    before = None
    for now in range(pairs - 1):
        if now > 0:
            sent, seen, env = pl.pallas_call(
                functools.partial(middle_kernel, now),
                in_specs=[SMEM] * 3 + [VMEM] * 4,
                out_specs=[VMEM] * 3,
                out_shape=[sent_shape(0), seen_shape, env_shape],
                compiler_params=params(),
            )(*small, exchange(sent), before, after, seen)
            evens.append(env)
        env = pl.pallas_call(
            second_kernel,
            in_specs=[VMEM] * 2,
            out_specs=VMEM,
            out_shape=env_shape,
            compiler_params=params(),
        )(exchange(sent), after)
        odds.append(env)
        if now == 0:
            env, everything = lax.optimization_barrier((env, everything))
            before = pl.pallas_call(
                functools.partial(lay_kernel, side),
                in_specs=[SMEM] + [HBM] * (2 * side),
                out_specs=ANY,
                out_shape=jax.ShapeDtypeStruct(whole, bf16),
                scratch_shapes=[lay_sems],
                compiler_params=params(),
            )(where, *in_hbm(everything))
            before = pltpu.with_memory_space_constraint(before, pltpu.VMEM)
        env = lax.ppermute(env, "pair", [(now, now + 1)])
        sent, seen = pl.pallas_call(
            functools.partial(first_kernel, now + 1),
            in_specs=[SMEM] * 3 + [VMEM] * 3,
            out_specs=[VMEM] * 2,
            out_shape=[sent_shape(0), seen_shape],
            compiler_params=params(),
        )(*small, env, before, seen)
    moved = exchange(sent)
    sent, env = pl.pallas_call(
        functools.partial(end_kernel, pairs - 1),
        in_specs=[SMEM] * 3 + [VMEM] * 4,
        out_specs=[VMEM] * 2,
        out_shape=[sent_shape(EXTRA), env_shape],
        compiler_params=params(),
    )(*small, moved, before, after, seen)
    evens.append(env)
    kept = evens + odds
    homeward = pl.pallas_call(
        home_kernel,
        in_specs=[SMEM] + [VMEM] * 2 + [ANY] * len(kept),
        out_specs=VMEM,
        out_shape=jax.ShapeDtypeStruct((fronts, panel + EXTRA, width), bf16),
        scratch_shapes=[
            pltpu.VMEM((rows, width), bf16),
            pltpu.VMEM((2, rows, width), bf16),
            pltpu.SemaphoreType.DMA((2,)),
        ],
        compiler_params=params(),
    )(where, exchange(sent), after, *kept)
    home = lax.all_to_all(homeward, ("parity", "half"), 0, 0, tiled=True)
    values = jnp.sum(home[:, panel : panel + 3, 0].astype(f32), axis=1)
    return home[None, :, :panel], values[:, None]


def solution(mesh):
    links, peers = mesh.devices.shape
    devices = mesh.devices.reshape(links // 2, 2, 2, peers // 2)
    chain, bond = ("pair", "parity"), ("half", "member")
    placed = (P(chain, bond, None, None), P(None, bond, None), P(), P(), P(), P())
    return jax.shard_map(
        on_device,
        mesh=Mesh(devices, chain + bond),
        in_specs=placed,
        out_specs=(P(chain, None, bond, None), P(None, chain)),
        check_vma=False,
    )
```

time: 1080 us -> 277 us (0.26); the launches traced: 1070 us -> 276 us
  blocking collectives: 608 us -> 113 us
  local copies, waits for them, and re-layouts: 154 us -> 6.63 us
  matrix products: 125 us -> 0 us
  Pallas kernels: 0 us -> 51.3 us
  waiting for transfers between devices: 106 us -> 67.2 us
  starting transfers between devices: 56.4 us -> 22.3 us
    psum x9 -> x0, blocking collectives: 608 us -> none  [advance(): summed = lax.psum(partial_value, 'bond')]
    dot_general x37 -> x0, matrix products: 125 us -> none  [the longest x9 55.1 us: advance(): jnp.dot(current.reshape(group * panel, width), flat_right, preferred_elem...]
    all_to_all x0 -> x8, blocking collectives: none -> 113 us  [the longest x7 97 us: exchange(): return lax.all_to_all(sent, 'member', 0, 0, tiled=True)]
    all_to_all x18 -> x0, local copies, waits for them, and re-layouts: 65.8 us -> none  [advance(): lax.all_to_all(prod32.astype(jnp.bfloat16), 'bond', split_axis=3, concat_...]
    all_gather x1, waiting for transfers between devices: 57.6 us -> 5.97 us  [on_device(): after = lax.all_gather(later, bond, axis=0)]
    pallas_call x0 -> x16, Pallas kernels: none -> 51.3 us  [the longest x2 8.57 us: on_device(): pl.pallas_call(functools.partial(middle_kernel, now), in_specs=[SMEM] * 3...]
    while x19 -> x0, local copies, waits for them, and re-layouts: 47.8 us -> none
    all_to_all x9 -> x1, starting transfers between devices: 36.6 us -> 4.55 us  [exchange(): return lax.all_to_all(sent, 'member', 0, 0, tiled=True)]
  transfers between devices with their start and end apart: 19 -> 19, of which waited for: 10 -> 8; matrix products, arithmetic and copies ran while one was open for 2% -> 1% of each run, Pallas kernels for 0% -> 6%
where the time goes in v2:
time: 277 us; the launch traced here: 276 us
  blocking collectives  113 us (41%)
  waiting for transfers between devices  67.2 us (24%)
  Pallas kernels  51.3 us (19%)
  starting transfers between devices  22.3 us (8%)
  between operations  14.3 us (5%)
  local copies, waits for them, and re-layouts  6.63 us (2%)
    all_to_all x7, blocking collectives, exchange(): return lax.all_to_all(sent, 'member', 0, 0, tiled=True)  97 us
    ppermute x3, waiting for transfers between devices, second_ring(): lax.ppermute(row, bond, shifts(side, m, False))  26 us
    all_to_all x1, blocking collectives, on_device(): home = lax.all_to_all(homeward, ('parity', 'half'), 0, 0, tiled=True)  16.4 us
    all_to_all x1, waiting for transfers between devices, exchange(): return lax.all_to_all(sent, 'member', 0, 0, tiled=True)  14.2 us
    ppermute x3, waiting for transfers between devices, on_device(): env = lax.ppermute(env, 'pair', [(now, now + 1)])  13.9 us
    pallas_call x2, Pallas kernels, on_device(): pl.pallas_call(functools.partial(middle_kernel, now), in_specs=[SMEM] * 3...  8.57 us
    pallas_call x3, Pallas kernels, on_device(): pl.pallas_call(functools.partial(first_kernel, now + 1), in_specs=[SMEM]...  7.73 us
    pallas_call x1, Pallas kernels, on_device(): pl.pallas_call(functools.partial(pieces_kernel, side), in_specs=[SMEM, VM...  6.14 us
  transfers between devices with their start and end apart: 19, of which 8 were waited for; matrix products, arithmetic and copies ran while one was open for 1% of the time, Pallas kernels for 6%

profile of v2, /device:TPU:192, one launch (start us, length us, event | category | flops | bytes accessed | tf_op | source)
XLA Modules:
  0.0 275.9 jit_solution(4680499830197576050)
XLA Ops:
  7.2 0.0 all-gather.3.cloned.1.call-start
  7.2 1.0 copy.13
  8.2 1.1 collective-permute-start.1
  9.3 0.8 dynamic-slice_bitcast_fusion
  10.2 3.2 %collective-permute-start = (bf16[32,1024]{1,0:T(8,128)(2,1)S(1)}, bf16[32,1024]{1,0:T(8,128)(2,1)S(1)}, u32[]{:S(2)}, u32[]{:S(2)}) collective-permute-start(bf16[32,1024]{1,0:T(8,128)(2,1)S(1)} %dynamic-slice_bitcast_fusion), channel_id=1, source_target_pairs={{0,16},{16,0},{1,17},{17,1},{2,18},{18,2},{3,19},{19,3},{4,20},{20... | collective-permute-start | bytes 196616 | tf_op jit(solution)/shard_map/ppermute | solution.py:352
  13.4 0.8 copy.11.operators_ref
  14.2 0.1 stack.70.where_ref
  14.3 0.7 copy-done.2
  15.0 0.7 copy-done.3
  15.6 0.7 copy-done.4
  16.3 1.5 shard_map.77
  17.8 0.0 collective-permute-done.other_ref
  17.8 0.0 collective-permute-done.1.near_ref
  17.8 0.0 copy-start.1
  17.9 0.9 copy-done.1
  18.8 1.4 shard_map.78
  20.2 0.0 all-gather.3.cloned.1.call-update
  20.2 0.1 collective-permute-start.2
  20.3 1.3 collective-permute-done.2
  21.7 1.6 collective-permute-start.3
  23.3 2.7 collective-permute-start.4
  26.0 1.4 collective-permute-start.5
  27.4 0.0 collective-permute-start.6
  27.5 1.9 collective-permute-done.3
  29.3 3.8 %collective-permute-done.4 = bf16[2,4,32,512]{3,2,1,0:T(8,128)(2,1)S(1)} collective-permute-done((bf16[2,4,32,512]{3,2,1,0:T(8,128)(2,1)S(1)}, bf16[2,4,32,512]{3,2,1,0:T(8,128)(2,1)S(1)}, u32[]{:S(2)}, u32[]{:S(2)}) %collective-permute-start.4) | collective-permute-done | bytes 262176 | tf_op jit(solution)/shard_map/ppermute | solution.py:313
  33.1 0.1 pad_maximum_fusion.refs_0_
  33.3 0.8 collective-permute-start.7
  34.1 2.3 collective-permute-start.8
  36.4 1.3 collective-permute-start.9
  37.7 25.7 %collective-permute-done.7.refs_1_ = bf16[4,2,4,32,512]{4,3,2,1,0:T(8,128)(2,1)S(1)} collective-permute-done((bf16[4,2,4,32,512]{4,3,2,1,0:T(8,128)(2,1)S(1)}, bf16[4,2,4,32,512]{4,3,2,1,0:T(8,128)(2,1)S(1)}, u32[]{:S(2)}, u32[]{:S(2)}) %collective-permute-start.7) | collective-permute-done | bytes 1048608 | tf_op jit(solution)/shard_map/ppermute | solution.py:318
  63.4 0.5 collective-permute-start.12
  63.9 0.3 collective-permute-done.9.refs_3_
  64.2 0.2 copy-done.6
  64.4 4.9 %shard_map.79 = (bf16[16,32,512]{2,1,0:T(8,128)(2,1)}, f32[2,8,128]{2,1,0:T(8,128)S(1)}) custom-call(s32[8]{0:T(128)S(1)} %stack.70.where_ref, f32[2,4,4]{2,1,0:T(4,128)S(1)} %get-tuple-element.48.mix_ref, f32[2,4,4]{2,1,0:T(4,128)S(1)} %get-tuple-element.49.look_ref, bf16[64,1024]{1,0:T(8,128)(2,1)S(1)} %get-tuple-element.53.env_ref, ...), custom_call_target="tpu_custom_call" | custom-call | tf_op jit(solution)/shard_map/pallas_call | solution.py:391
  69.3 4.5 %all-to-all-start = ((bf16[16,32,512]{2,1,0:T(8,128)(2,1)}), bf16[16,32,512]{2,1,0:T(8,128)(2,1)S(1)}, u32[]{:S(2)}, u32[]{:S(2)}) async-start(bf16[16,32,512]{2,1,0:T(8,128)(2,1)} %get-tuple-element.58), calls=%async_computation | async-start | bytes 1048576 | tf_op jit(solution)/shard_map/all_to_all | solution.py:389
  73.9 14.2 %all-to-all-done.moved_ref = bf16[16,32,512]{2,1,0:T(8,128)(2,1)S(1)} async-done(((bf16[16,32,512]{2,1,0:T(8,128)(2,1)}), bf16[16,32,512]{2,1,0:T(8,128)(2,1)S(1)}, u32[]{:S(2)}, u32[]{:S(2)}) %all-to-all-start) | async-done | bytes 524320 | tf_op jit(solution)/shard_map/all_to_all | solution.py:389
  88.1 6.1 %shard_map.80.env_ref.refs_0_ = bf16[64,1024]{1,0:T(8,128)(2,1)S(1)} custom-call(s32[8]{0:T(128)S(1)} %stack.70.where_ref, bf16[16,32,512]{2,1,0:T(8,128)(2,1)S(1)} %all-to-all-done.moved_ref, bf16[4,2,4,32,512]{4,3,2,1,0:T(8,128)(2,1)} %copy-done.5, bf16[4,2,4,32,512]{4,3,2,1,0:T(8,128)(2,1)} %copy-done.6, ...), custom_call_target="tpu_custom_call" | custom-call | tf_op jit(solution)/shard_map/pallas_call | solution.py:406
  94.3 6.0 %all-gather.3.cloned.1.call-done = bf16[128,32,1024]{2,1,0:T(8,128)(2,1)} async-done(((bf16[4,32,1024]{2,1,0:T(8,128)(2,1)}), bf16[128,32,1024]{2,1,0:T(8,128)(2,1)}) %all-gather.3.cloned.1.call-update) | async-done | bytes 8388624 | tf_op jit(solution)/shard_map/all_gather | solution.py:376
  100.2 5.3 %shard_map.81 = (bf16[16,64,256]{2,1,0:T(8,128)(2,1)S(1)}, f32[2,8,128]{2,1,0:T(8,128)S(1)}) custom-call(s32[8]{0:T(128)S(1)} %stack.70.where_ref, f32[2,4,4]{2,1,0:T(4,128)S(1)} %get-tuple-element.48.mix_ref, f32[2,4,4]{2,1,0:T(4,128)S(1)} %get-tuple-element.49.look_ref, bf16[64,1024]{1,0:T(8,128)(2,1)S(1)} %shard_map.80.env_ref.refs_0_, ...), custom_call_target="tpu_custom_call" | custom-call | tf_op jit(solution)/shard_map/pallas_call | solution.py:416
  105.5 14.3 %all_to_all.45.moved_ref = bf16[16,64,256]{2,1,0:T(8,128)(2,1)S(1)} all-to-all(bf16[16,64,256]{2,1,0:T(8,128)(2,1)S(1)} %get-tuple-element.63), channel_id=1, replica_groups=mesh['pair'=4,'parity'=2,'half'=2,'member'=16] {'member'}, dimensions={0} | all-to-all | bytes 1048576 | tf_op jit(solution)/shard_map/all_to_all | solution.py:389
  119.9 1.6 shard_map.82.refs_4_
  121.5 0.7 collective-permute-start.14
  122.1 4.2 %shard_map.83.tensor_ref.old_ref = bf16[16,2,2,4,32,512]{5,4,3,2,1,0:T(8,128)(2,1)S(1)} custom-call(s32[8]{0:T(128)S(1)} %stack.70.where_ref, bf16[4,2,4,32,512]{4,3,2,1,0:T(8,128)(2,1)} %copy-done.5, bf16[4,2,4,32,512]{4,3,2,1,0:T(8,128)(2,1)} %copy-done.6, bf16[4,2,4,32,512]{4,3,2,1,0:T(8,128)(2,1)} %collective-permute-done.8.refs_2_, ...), custom_call_target="tpu_custom_call" | custom-call | tf_op jit(solution)/shard_map/pallas_call | solution.py:449
  126.4 2.6 shard_map.84
  129.0 13.5 %all_to_all.46.moved_ref = bf16[16,64,256]{2,1,0:T(8,128)(2,1)S(1)} all-to-all(bf16[16,64,256]{2,1,0:T(8,128)(2,1)S(1)} %get-tuple-element.74), channel_id=1, replica_groups=mesh['pair'=4,'parity'=2,'half'=2,'member'=16] {'member'}, dimensions={0} | all-to-all | bytes 1048576 | tf_op jit(solution)/shard_map/all_to_all | solution.py:389
  142.5 4.3 %shard_map.85 = (bf16[16,64,256]{2,1,0:T(8,128)(2,1)S(1)}, f32[2,8,128]{2,1,0:T(8,128)S(1)}, bf16[64,1024]{1,0:T(8,128)(2,1)S(1)}) custom-call(s32[8]{0:T(128)S(1)} %stack.70.where_ref, f32[2,4,4]{2,1,0:T(4,128)S(1)} %get-tuple-element.48.mix_ref, f32[2,4,4]{2,1,0:T(4,128)S(1)} %get-tuple-element.49.look_ref, bf16[16,64,256]{2,1,0:T(8,128)(2,1)S(1)} %all_to_all.46.moved_ref, ...), custom_call_target="tpu_custom_call" | custom-call | tf_op jit(solution)/shard_map/pallas_call | solution.py:431
  146.8 13.5 %all_to_all.47.moved_ref = bf16[16,64,256]{2,1,0:T(8,128)(2,1)S(1)} all-to-all(bf16[16,64,256]{2,1,0:T(8,128)(2,1)S(1)} %get-tuple-element.76), channel_id=1, replica_groups=mesh['pair'=4,'parity'=2,'half'=2,'member'=16] {'member'}, dimensions={0} | all-to-all | bytes 1048576 | tf_op jit(solution)/shard_map/all_to_all | solution.py:389
  160.2 1.6 shard_map.86.refs_5_
  161.8 0.7 collective-permute-start.15
  162.5 2.6 shard_map.87
  165.1 13.7 %all_to_all.48.moved_ref = bf16[16,64,256]{2,1,0:T(8,128)(2,1)S(1)} all-to-all(bf16[16,64,256]{2,1,0:T(8,128)(2,1)S(1)} %get-tuple-element.78), channel_id=1, replica_groups=mesh['pair'=4,'parity'=2,'half'=2,'member'=16] {'member'}, dimensions={0} | all-to-all | bytes 1048576 | tf_op jit(solution)/shard_map/all_to_all | solution.py:389
  178.8 4.3 %shard_map.88 = (bf16[16,64,256]{2,1,0:T(8,128)(2,1)S(1)}, f32[2,8,128]{2,1,0:T(8,128)S(1)}, bf16[64,1024]{1,0:T(8,128)(2,1)S(1)}) custom-call(s32[8]{0:T(128)S(1)} %stack.70.where_ref, f32[2,4,4]{2,1,0:T(4,128)S(1)} %get-tuple-element.48.mix_ref, f32[2,4,4]{2,1,0:T(4,128)S(1)} %get-tuple-element.49.look_ref, bf16[16,64,256]{2,1,0:T(8,128)(2,1)S(1)} %all_to_all.48.moved_ref, ...), custom_call_target="tpu_custom_call" | custom-call | tf_op jit(solution)/shard_map/pallas_call | solution.py:431
  183.1 13.5 %all_to_all.49.moved_ref = bf16[16,64,256]{2,1,0:T(8,128)(2,1)S(1)} all-to-all(bf16[16,64,256]{2,1,0:T(8,128)(2,1)S(1)} %get-tuple-element.80), channel_id=1, replica_groups=mesh['pair'=4,'parity'=2,'half'=2,'member'=16] {'member'}, dimensions={0} | all-to-all | bytes 1048576 | tf_op jit(solution)/shard_map/all_to_all | solution.py:389
  196.6 1.6 shard_map.89.refs_6_
  198.2 1.3 collective-permute-start.16
  199.5 13.9 %collective-permute-done.16.env_ref = bf16[64,1024]{1,0:T(8,128)(2,1)S(1)} collective-permute-done((bf16[64,1024]{1,0:T(8,128)(2,1)S(1)}, bf16[64,1024]{1,0:T(8,128)(2,1)S(1)}, u32[]{:S(2)}, u32[]{:S(2)}) %collective-permute-start.16) | collective-permute-done | bytes 131104 | tf_op jit(solution)/shard_map/ppermute | solution.py:458
  213.4 2.6 shard_map.90
  216.0 13.9 %all_to_all.50.moved_ref = bf16[16,64,256]{2,1,0:T(8,128)(2,1)S(1)} all-to-all(bf16[16,64,256]{2,1,0:T(8,128)(2,1)S(1)} %get-tuple-element.82), channel_id=1, replica_groups=mesh['pair'=4,'parity'=2,'half'=2,'member'=16] {'member'}, dimensions={0} | all-to-all | bytes 1048576 | tf_op jit(solution)/shard_map/all_to_all | solution.py:389
  229.8 4.3 %shard_map.91 = (bf16[16,80,256]{2,1,0:T(8,128)(2,1)S(1)}, bf16[64,1024]{1,0:T(8,128)(2,1)S(1)}) custom-call(s32[8]{0:T(128)S(1)} %stack.70.where_ref, f32[2,4,4]{2,1,0:T(4,128)S(1)} %get-tuple-element.48.mix_ref, f32[2,4,4]{2,1,0:T(4,128)S(1)} %get-tuple-element.49.look_ref, bf16[16,64,256]{2,1,0:T(8,128)(2,1)S(1)} %all_to_all.50.moved_ref, ...), custom_call_target="tpu_custom_call" | custom-call | tf_op jit(solution)/shard_map/pallas_call | solution.py:467
  234.2 14.6 %all_to_all.51.moved_ref = bf16[16,80,256]{2,1,0:T(8,128)(2,1)S(1)} all-to-all(bf16[16,80,256]{2,1,0:T(8,128)(2,1)S(1)} %get-tuple-element.84), channel_id=1, replica_groups=mesh['pair'=4,'parity'=2,'half'=2,'member'=16] {'member'}, dimensions={0} | all-to-all | bytes 1310720 | tf_op jit(solution)/shard_map/all_to_all | solution.py:389
  248.8 2.5 shard_map.92
  251.3 16.4 %all_to_all.52 = bf16[4,48,1024]{2,1,0:T(8,128)(2,1)S(1)} all-to-all(bf16[4,48,1024]{2,1,0:T(8,128)(2,1)S(1)} %shard_map.92), channel_id=1, replica_groups=mesh['pair'=4,'parity'=2,'half'=2,'member'=16] {'parity','half'}, dimensions={0} | all-to-all | bytes 786432 | tf_op jit(solution)/shard_map/all_to_all | solution.py:488
  267.7 0.7 slice_bitcast_fusion
  268.4 0.6 convert_reduce_fusion
  (22 shorter events, 0.1 us)
Async XLA Ops:
  7.2 93.1 %all-gather.3.cloned.1.call-start = ((), (), s32[]{:S(2)}) async-start(), calls=%async_computation.9 | async-start | bytes 8650752 | tf_op jit(solution)/shard_map/all_gather | solution.py:376
  8.2 9.6 %collective-permute-start.1 = (bf16[4,32,1024]{2,1,0:T(8,128)(2,1)S(1)}, bf16[4,32,1024]{2,1,0:T(8,128)(2,1)S(1)}, u32[]{:S(2)}, u32[]{:S(2)}) collective-permute-start(bf16[4,32,1024]{2,1,0:T(8,128)(2,1)S(1)} %bitcast.34), channel_id=1, source_target_pairs={{0,32},{32,0},{1,33},{33,1},{2,34},{34,2},{3,35},{35,3},{4,36},{36... | collective-permute-start | bytes 786440 | tf_op jit(solution)/shard_map/ppermute | solution.py:350
  10.2 7.6 %collective-permute-start = (bf16[32,1024]{1,0:T(8,128)(2,1)S(1)}, bf16[32,1024]{1,0:T(8,128)(2,1)S(1)}, u32[]{:S(2)}, u32[]{:S(2)}) collective-permute-start(bf16[32,1024]{1,0:T(8,128)(2,1)S(1)} %dynamic-slice_bitcast_fusion), channel_id=1, source_target_pairs={{0,16},{16,0},{1,17},{17,1},{2,18},{18,2},{3,19},{19,3},{4,20},{20... | collective-permute-start | bytes 196616 | tf_op jit(solution)/shard_map/ppermute | solution.py:352
  14.3 0.7 copy-start.2
  15.0 0.7 copy-start.3
  15.6 0.7 copy-start.4
  17.8 1.0 copy-start.1
  20.2 1.4 collective-permute-start.2
  21.7 7.7 %collective-permute-start.3 = (bf16[2,4,32,512]{3,2,1,0:T(8,128)(2,1)S(1)}, bf16[2,4,32,512]{3,2,1,0:T(8,128)(2,1)S(1)}, u32[]{:S(2)}, u32[]{:S(2)}) collective-permute-start(bf16[2,4,32,512]{3,2,1,0:T(8,128)(2,1)S(1)} %maximum_select_fusion.1), channel_id=1, source_target_pairs={{0,2},{1,9},{2,4},{3,11},{4,6},{5,13},{6,0},{7,15},{8,10},{9,17},{... | collective-permute-start | bytes 786440 | tf_op jit(solution)/shard_map/ppermute | solution.py:313
  23.3 9.9 %collective-permute-start.4 = (bf16[2,4,32,512]{3,2,1,0:T(8,128)(2,1)S(1)}, bf16[2,4,32,512]{3,2,1,0:T(8,128)(2,1)S(1)}, u32[]{:S(2)}, u32[]{:S(2)}) collective-permute-start(bf16[2,4,32,512]{3,2,1,0:T(8,128)(2,1)S(1)} %maximum_select_fusion.1), channel_id=1, source_target_pairs={{0,4},{1,17},{2,6},{3,19},{4,0},{5,21},{6,2},{7,23},{8,12},{9,25},... | collective-permute-start | bytes 786440 | tf_op jit(solution)/shard_map/ppermute | solution.py:313
  26.0 7.2 %collective-permute-start.5 = (bf16[2,4,32,512]{3,2,1,0:T(8,128)(2,1)S(1)}, bf16[2,4,32,512]{3,2,1,0:T(8,128)(2,1)S(1)}, u32[]{:S(2)}, u32[]{:S(2)}) collective-permute-start(bf16[2,4,32,512]{3,2,1,0:T(8,128)(2,1)S(1)} %maximum_select_fusion.1), channel_id=1, source_target_pairs={{0,6},{1,25},{2,0},{3,27},{4,2},{5,29},{6,4},{7,31},{8,14},{9,1},{... | collective-permute-start | bytes 786440 | tf_op jit(solution)/shard_map/ppermute | solution.py:313
  27.4 5.9 %collective-permute-start.6 = (bf16[64,1024]{1,0:T(8,128)(2,1)S(1)}, bf16[64,1024]{1,0:T(8,128)(2,1)S(1)}, u32[]{:S(2)}, u32[]{:S(2)}) collective-permute-start(bf16[64,1024]{1,0:T(8,128)(2,1)S(1)} %get-tuple-element.53.env_ref), channel_id=1, source_target_pairs={{0,1},{1,0},{2,3},{3,2},{4,5},{5,4},{6,7},{7,6},{8,9},{9,8},{10,11... | collective-permute-start | bytes 393224 | tf_op jit(solution)/shard_map/ppermute | solution.py:377
  33.3 30.9 %copy-start.5 = (bf16[4,2,4,32,512]{4,3,2,1,0:T(8,128)(2,1)}, bf16[4,2,4,32,512]{4,3,2,1,0:T(8,128)(2,1)S(1)}, u32[]{:S(2)}) copy-start(bf16[4,2,4,32,512]{4,3,2,1,0:T(8,128)(2,1)S(1)} %pad_maximum_fusion.refs_0_) | copy-start | bytes 3145732
  33.3 30.1 %collective-permute-start.7 = (bf16[4,2,4,32,512]{4,3,2,1,0:T(8,128)(2,1)S(1)}, bf16[4,2,4,32,512]{4,3,2,1,0:T(8,128)(2,1)S(1)}, u32[]{:S(2)}, u32[]{:S(2)}) collective-permute-start(bf16[4,2,4,32,512]{4,3,2,1,0:T(8,128)(2,1)S(1)} %pad_maximum_fusion.refs_0_), channel_id=1, source_target_pairs={{0,8},{1,3},{2,10},{3,5},{4,12},{5,7},{6,14},{7,1},{8,16},{9,11},{... | collective-permute-start | bytes 3145736 | tf_op jit(solution)/shard_map/ppermute | solution.py:318
  34.1 29.4 %collective-permute-start.8 = (bf16[4,2,4,32,512]{4,3,2,1,0:T(8,128)(2,1)S(1)}, bf16[4,2,4,32,512]{4,3,2,1,0:T(8,128)(2,1)}, u32[]{:S(2)}, u32[]{:S(2)}) collective-permute-start(bf16[4,2,4,32,512]{4,3,2,1,0:T(8,128)(2,1)S(1)} %pad_maximum_fusion.refs_0_), channel_id=1, source_target_pairs={{0,16},{1,5},{2,18},{3,7},{4,20},{5,1},{6,22},{7,3},{8,24},{9,13},... | collective-permute-start | bytes 3145736 | tf_op jit(solution)/shard_map/ppermute | solution.py:318
  36.4 27.8 %collective-permute-start.9 = (bf16[4,2,4,32,512]{4,3,2,1,0:T(8,128)(2,1)S(1)}, bf16[4,2,4,32,512]{4,3,2,1,0:T(8,128)(2,1)}, u32[]{:S(2)}, u32[]{:S(2)}) collective-permute-start(bf16[4,2,4,32,512]{4,3,2,1,0:T(8,128)(2,1)S(1)} %pad_maximum_fusion.refs_0_), channel_id=1, source_target_pairs={{0,24},{1,7},{2,26},{3,1},{4,28},{5,3},{6,30},{7,5},{8,0},{9,15},{... | collective-permute-start | bytes 3145736 | tf_op jit(solution)/shard_map/ppermute | solution.py:318
  37.7 36.1 %collective-permute-start.10 = (bf16[4,2,4,32,512]{4,3,2,1,0:T(8,128)(2,1)S(1)}, bf16[4,2,4,32,512]{4,3,2,1,0:T(8,128)(2,1)}, u32[]{:S(2)}, u32[]{:S(2)}) collective-permute-start(bf16[4,2,4,32,512]{4,3,2,1,0:T(8,128)(2,1)S(1)} %pad_maximum_fusion.refs_0_), channel_id=1, source_target_pairs={{0,1},{1,0},{2,3},{3,2},{4,5},{5,4},{6,7},{7,6},{8,9},{9,8},{10,11... | collective-permute-start | bytes 3145736 | tf_op jit(solution)/shard_map/ppermute | solution.py:322
  63.4 1.0 copy-start.6
  63.4 24.7 %collective-permute-start.11 = (bf16[4,2,4,32,512]{4,3,2,1,0:T(8,128)(2,1)S(1)}, bf16[4,2,4,32,512]{4,3,2,1,0:T(8,128)(2,1)}, u32[]{:S(2)}, u32[]{:S(2)}) collective-permute-start(bf16[4,2,4,32,512]{4,3,2,1,0:T(8,128)(2,1)S(1)} %collective-permute-done.7.refs_1_), channel_id=1, source_target_pairs={{0,1},{1,0},{2,3},{3,2},{4,5},{5,4},{6,7},{7,6},{8,9},{9,8},{10,11... | collective-permute-start | bytes 3145736 | tf_op jit(solution)/shard_map/ppermute | solution.py:322
  63.4 24.7 %collective-permute-start.12 = (bf16[4,2,4,32,512]{4,3,2,1,0:T(8,128)(2,1)}, bf16[4,2,4,32,512]{4,3,2,1,0:T(8,128)(2,1)}, u32[]{:S(2)}, u32[]{:S(2)}) collective-permute-start(bf16[4,2,4,32,512]{4,3,2,1,0:T(8,128)(2,1)} %collective-permute-done.8.refs_2_), channel_id=1, source_target_pairs={{0,1},{1,0},{2,3},{3,2},{4,5},{5,4},{6,7},{7,6},{8,9},{9,8},{10,11... | collective-permute-start | bytes 3145736 | tf_op jit(solution)/shard_map/ppermute | solution.py:322
  64.2 23.9 %collective-permute-start.13 = (bf16[4,2,4,32,512]{4,3,2,1,0:T(8,128)(2,1)}, bf16[4,2,4,32,512]{4,3,2,1,0:T(8,128)(2,1)}, u32[]{:S(2)}, u32[]{:S(2)}) collective-permute-start(bf16[4,2,4,32,512]{4,3,2,1,0:T(8,128)(2,1)} %collective-permute-done.9.refs_3_), channel_id=1, source_target_pairs={{0,1},{1,0},{2,3},{3,2},{4,5},{5,4},{6,7},{7,6},{8,9},{9,8},{10,11... | collective-permute-start | bytes 3145736 | tf_op jit(solution)/shard_map/ppermute | solution.py:322
  69.3 18.8 %all-to-all-start = ((bf16[16,32,512]{2,1,0:T(8,128)(2,1)}), bf16[16,32,512]{2,1,0:T(8,128)(2,1)S(1)}, u32[]{:S(2)}, u32[]{:S(2)}) async-start(bf16[16,32,512]{2,1,0:T(8,128)(2,1)} %get-tuple-element.58), calls=%async_computation | async-start | bytes 1048576 | tf_op jit(solution)/shard_map/all_to_all | solution.py:389
  100.2 19.6 %copy-start = (bf16[128,32,1024]{2,1,0:T(8,128)(2,1)S(1)}, bf16[128,32,1024]{2,1,0:T(8,128)(2,1)}, u32[]{:S(2)}) copy-start(bf16[128,32,1024]{2,1,0:T(8,128)(2,1)} %all-gather.3.cloned.1.call-done) | copy-start | bytes 25165828
  121.5 4.9 %collective-permute-start.14 = (bf16[64,1024]{1,0:T(8,128)(2,1)S(1)}, bf16[64,1024]{1,0:T(8,128)(2,1)S(1)}, u32[]{:S(2)}, u32[]{:S(2)}) collective-permute-start(bf16[64,1024]{1,0:T(8,128)(2,1)S(1)} %shard_map.82.refs_4_), channel_id=1, source_target_pairs={{0,64},{1,65},{2,66},{3,67},{4,68},{5,69},{6,70},{7,71},{8,72},{9,... | collective-permute-start | bytes 393224 | tf_op jit(solution)/shard_map/ppermute | solution.py:458
  161.8 0.7 collective-permute-start.15
  198.2 15.2 %collective-permute-start.16 = (bf16[64,1024]{1,0:T(8,128)(2,1)S(1)}, bf16[64,1024]{1,0:T(8,128)(2,1)S(1)}, u32[]{:S(2)}, u32[]{:S(2)}) collective-permute-start(bf16[64,1024]{1,0:T(8,128)(2,1)S(1)} %shard_map.89.refs_6_), channel_id=1, source_target_pairs={{128,192},{129,193},{130,194},{131,195},{132,196},{133,197},{134,1... | collective-permute-start | bytes 393224 | tf_op jit(solution)/shard_map/ppermute | solution.py:458
Sparse Core Ops, SparseCore 0:
  20.3 79.8 all-gather.2

commit v3 on v2

--- a/solution.py
+++ b/solution.py
@@ -14,17 +14,9 @@
 COLS = 256
 
 
-def split3(value):
+def two_parts(value):
     high = value.astype(jnp.bfloat16).astype(jnp.float32)
-    rest = value - high
-    mid = rest.astype(jnp.bfloat16).astype(jnp.float32)
-    return high, mid, rest - mid
-
-
-def parts_of(value, lanes):
-    rows = [jnp.broadcast_to(p, (1, lanes)) for p in split3(value)]
-    rows.append(jnp.zeros((EXTRA - 3, lanes), jnp.float32))
-    return jnp.concatenate(rows, axis=0).astype(jnp.bfloat16)
+    return jnp.concatenate([high, value - high], axis=0).astype(jnp.bfloat16)
 
 
 def columns(tensor_ref, t, c):
@@ -72,7 +64,7 @@
         first = c * (COLS // panel)
         h, first = first // half, first % half
         out_ref[first : first + COLS // panel, h * panel : (h + 1) * panel, :] = turned
-    return jnp.sum(total, axis=1, keepdims=True)
+    return total
 
 
 def gather(moved_ref, tensor_ref, env_ref):
@@ -115,18 +107,42 @@
             copies.append(pltpu.make_async_copy(ref.at[k], place, sems.at[i, k]))
     for copy in copies:
         copy.start()
-    for copy in copies:
+    return copies
+
+
+def lay_kernel(side, where_ref, *refs):
+    for copy in lay(side, where_ref, refs[:-2], refs[-2], refs[-1]):
         copy.wait()
-
-
-def lay_kernel(side, where_ref, *refs):
-    lay(side, where_ref, refs[:-2], refs[-2], refs[-1])
 
 
 def pieces_kernel(side, where_ref, moved_ref, *refs):
     pieces, (env_ref, tensor, sems) = refs[:-3], refs[-3:]
-    lay(side, where_ref, pieces, tensor, sems)
-    gather(moved_ref, tensor, env_ref)
+    copies = lay(side, where_ref, pieces, tensor, sems)
+    chips, wide = tensor.shape[0], tensor.shape[5]
+    left = jnp.concatenate(
+        [
+            jnp.concatenate([moved_ref[g], moved_ref[g + 1]], axis=0) for g in range(0, chips, 2)
+        ],
+        axis=1,
+    )
+    for part in range(2):
+        at = where_ref[4] if part == 0 else 1 - where_ref[4]
+        for copy in copies[part * side * side : (part + 1) * side * side]:
+            copy.wait()
+        for c in range(wide // COLS):
+            cols = slice(c * COLS, (c + 1) * COLS)
+            right = jnp.concatenate(
+                [
+                    tensor[(h * chips + g) // 2, at, g % 2, :, :, cols].reshape(-1, COLS)
+                    for g in range(chips)
+                    for h in range(2)
+                ],
+                axis=0,
+            )
+            place = pl.ds(pl.multiple_of(at * wide + c * COLS, COLS), COLS)
+            env_ref[:, place] = jnp.dot(
+                left, right, preferred_element_type=jnp.float32
+            ).astype(jnp.bfloat16)
 
 
 def stream_kernel(
@@ -142,31 +158,45 @@
         )
         copies[-1].start()
     arrived = [copy.wait for copy in copies]
-    value = spread(1, where_ref, mix_ref, look_ref, env_ref[...], held, out_ref, arrived)
+    total = spread(1, where_ref, mix_ref, look_ref, env_ref[...], held, out_ref, arrived)
     new_ref[0] = seen_ref[0]
-    new_ref[1] = jnp.broadcast_to(value, new_ref.shape[1:])
+    first_row = lax.broadcasted_iota(jnp.int32, new_ref.shape[1:], 0) == 0
+    new_ref[1] = jnp.where(first_row, jnp.broadcast_to(total, new_ref.shape[1:]), 0.0)
+
+
+def load(side, where_ref, pieces, tensor_ref, sems):
+    blocks = []
+    for c in range(tensor_ref.shape[4] // COLS):
+        cols = pl.ds(c * COLS, COLS)
+        copies = []
+        for m, ref in enumerate(pieces):
+            for k in range(side):
+                chip = chip_of(side, where_ref, where_ref[4], m, k)
+                copies.append(
+                    pltpu.make_async_copy(
+                        ref.at[k, :, :, :, cols], tensor_ref.at[chip, :, :, :, cols], sems.at[c, m, k]
+                    )
+                )
+        for copy in copies:
+            copy.start()
+        blocks.append(copies)
+    return blocks
 
 
 def start_kernel(side, where_ref, mix_ref, look_ref, env_ref, twin_ref, *refs):
     pieces, (out_ref, new_ref, tensor, sems) = refs[:-4], refs[-4:]
     core = where_ref[4]
-    copies = []
-    for m, ref in enumerate(pieces):
-        for k in range(side):
-            place = tensor.at[chip_of(side, where_ref, core, m, k)]
-            copies.append(pltpu.make_async_copy(ref.at[k], place, sems.at[m, k]))
-    for copy in copies:
-        copy.start()
+    blocks = load(side, where_ref, pieces, tensor, sems)
     own, twin = env_ref[...], twin_ref[...]
     env = jnp.concatenate(
         [jnp.where(core == 0, own, twin), jnp.where(core == 0, twin, own)], axis=0
     )
-    for copy in copies:
-        copy.wait()
     chips, _, phys, panel, wide = tensor.shape
     mem = where_ref[0] // 2
     total = jnp.zeros((1, 128), jnp.float32)
-    for c in range(wide // COLS):
+    for c, copies in enumerate(blocks):
+        for copy in copies:
+            copy.wait()
         cols = slice(c * COLS, (c + 1) * COLS)
         prods = [
             jnp.dot(
@@ -185,68 +215,121 @@
         turned = jnp.concatenate(tall, axis=0).astype(jnp.bfloat16).T
         per = COLS // panel
         out_ref[c * per : (c + 1) * per] = turned.reshape(per, panel, 4 * phys * panel)
-    value = jnp.sum(total, axis=1, keepdims=True)
-    new_ref[...] = jnp.broadcast_to(value, new_ref.shape)
-
-
-def first_kernel(now, where_ref, mix_ref, look_ref, env_ref, tensor_ref, seen_ref, out_ref, new_ref):
-    value = spread(0, where_ref, mix_ref, look_ref, env_ref[...], tensor_ref, out_ref)
-    new_ref[0] = jnp.where(where_ref[1] == now, value, seen_ref[0])
+    first_row = lax.broadcasted_iota(jnp.int32, new_ref.shape[1:], 0) == 0
+    total = jnp.where(first_row, jnp.broadcast_to(total, new_ref.shape[1:]), 0.0)
+    new_ref[...] = jnp.broadcast_to(total[None], new_ref.shape)
+
+
+def spread_plain(slot, mix_ref, bank_ref, env, tensor_ref, out_ref):
+    width = env.shape[1]
+    phys = bank_ref.shape[1]
+    panel = env.shape[0] // 2
+    half = width // panel // 2
+    total = jnp.zeros((8, 128), jnp.float32)
+    for c in range(width // COLS):
+        prods = [
+            jnp.dot(env, columns(tensor_ref, t, c), preferred_element_type=jnp.float32)
+            for t in range(phys)
+        ]
+        seen = sum(bank_ref[slot, t, :, c * COLS : (c + 1) * COLS] * prods[t] for t in range(phys))
+        seen = jnp.sum(seen.reshape(-1, 8, COLS), axis=0)
+        total += sum(seen[:, b : b + 128] for b in range(0, COLS, 128))
+
+        def factor(s, t):
+            row = slot * phys * phys + s * phys + t
+            return mix_ref[row : row + 1]
+
+        mixed = [sum(factor(s, t) * prods[t] for t in range(phys)) for s in range(phys)]
+        tall = jnp.concatenate(
+            [mixed[s][h * panel : (h + 1) * panel] for h in range(2) for s in range(phys)], axis=0
+        )
+        turned = tall.astype(jnp.bfloat16).T.reshape(COLS // panel, panel, 2 * phys * panel)
+        first = c * (COLS // panel)
+        h, first = first // half, first % half
+        out_ref[first : first + COLS // panel, h * panel : (h + 1) * panel, :] = turned
+    return total
+
+
+def first_kernel(now, pair_ref, mix_ref, bank_ref, env_ref, tensor_ref, seen_ref, out_ref, new_ref):
+    total = spread_plain(0, mix_ref, bank_ref, env_ref[...], tensor_ref, out_ref)
+    new_ref[0] = jnp.where(pair_ref[...] == now, total, seen_ref[0])
     new_ref[1] = seen_ref[1]
 
 
 def middle_kernel(
-    now, where_ref, mix_ref, look_ref, moved_ref, old_ref, tensor_ref, seen_ref, out_ref, new_ref, env_ref
+    now, pair_ref, mix_ref, bank_ref, moved_ref, old_ref, tensor_ref, seen_ref, out_ref, new_ref, env_ref
 ):
     gather(moved_ref, old_ref, env_ref)
-    value = spread(1, where_ref, mix_ref, look_ref, env_ref[...], tensor_ref, out_ref)
+    total = spread_plain(1, mix_ref, bank_ref, env_ref[...], tensor_ref, out_ref)
     new_ref[0] = seen_ref[0]
-    new_ref[1] = jnp.where(where_ref[1] == now, value, seen_ref[1])
+    new_ref[1] = jnp.where(pair_ref[...] == now, total, seen_ref[1])
 
 
 def end_kernel(
-    now, where_ref, mix_ref, look_ref, moved_ref, old_ref, tensor_ref, seen_ref, out_ref, env_ref
+    now, pair_ref, mix_ref, bank_ref, moved_ref, old_ref, tensor_ref, seen_ref, out_ref, env_ref
 ):
     gather(moved_ref, old_ref, env_ref)
-    value = spread(1, where_ref, mix_ref, look_ref, env_ref[...], tensor_ref, out_ref)
+    total = spread_plain(1, mix_ref, bank_ref, env_ref[...], tensor_ref, out_ref)
     rows, lanes = env_ref.shape[0], out_ref.shape[2]
-    odd = jnp.where(where_ref[1] == now, value, seen_ref[1][:1, :1])
-    extra = jnp.concatenate([parts_of(v, lanes // 2) for v in (seen_ref[0][:1, :1], odd)], axis=1)
+    odd = jnp.where(pair_ref[...] == now, total, seen_ref[1])
+    extra = jnp.concatenate([two_parts(v) for v in (seen_ref[0], odd)], axis=1)
     out_ref[:, rows:, :] = jnp.broadcast_to(extra[None], (out_ref.shape[0], EXTRA, lanes))
+
+
+def bank_kernel(where_ref, look_ref, *refs):
+    tensors, bank_ref = refs[:-1], refs[-1]
+    slots, phys, rows, width = bank_ref.shape
+    half = width // rows
+    for slot, ref in enumerate(tensors):
+        for c in range(width // COLS):
+            own = [
+                jnp.concatenate(
+                    [block(ref, h * half + where_ref[0], s, c) for h in range(2)], axis=0
+                ).astype(jnp.float32)
+                for s in range(phys)
+            ]
+            for t in range(phys):
+                bank_ref[slot, t, :, c * COLS : (c + 1) * COLS] = sum(
+                    look_ref[slot, s, t] * own[s] for s in range(phys)
+                )
+
+
+def pick_kernel(pair_ref, *refs):
+    kept, outs = refs[:-2], refs[-2:]
+    count = len(kept) // 2
+    pair = pair_ref[:1, :1]
+    for q in range(2):
+        value = kept[q * count][...]
+        for p in range(1, count):
+            value = jnp.where(pair == p, kept[q * count + p][...], value)
+        outs[q][...] = value
 
 
 def second_kernel(moved_ref, tensor_ref, env_ref):
     gather(moved_ref, tensor_ref, env_ref)
 
 
-def home_kernel(where_ref, moved_ref, tensor_ref, *refs):
-    kept, (out_ref, env, picked, sems) = refs[:-4], refs[-4:]
-    count = (len(kept) + 1) // 2
+def home_kernel(now, pair_ref, moved_ref, tensor_ref, even_ref, odd_ref, six_ref, out_ref, env):
+    gather(moved_ref, tensor_ref, env)
     rows = env.shape[0]
     panel = rows // 2
-
-    def each(act):
-        for i, ref in enumerate(kept):
-            q, p = i // count, i % count
-            copy = pltpu.make_async_copy(ref, picked.at[q], sems.at[q])
-            pl.when(where_ref[1] == p)(getattr(copy, act))
-
-    each("start")
-    gather(moved_ref, tensor_ref, env)
-    each("wait")
-    now = where_ref[1] == count - 1
+    here = pair_ref[:1, :1] == now
     values = jnp.sum(moved_ref[:, rows:].astype(jnp.float32), axis=0)
-    for q in range(2):
-        result = picked[0] if q == 0 else jnp.where(now, env[...], picked[1])
-        value = jnp.sum(values[:, q * 128 : q * 128 + 1], axis=0, keepdims=True)
-        extra = parts_of(value, out_ref.shape[2])
+    for q, (kept, last) in enumerate(((even_ref, six_ref), (odd_ref, env))):
+        result = jnp.where(here, last[...], kept[...])
+        value = values[:, q * 128 : (q + 1) * 128]
+        extra = two_parts(value[:8] + value[8:])
         for h in range(2):
             out_ref[2 * q + h, :panel] = result[h * panel : (h + 1) * panel]
-            out_ref[2 * q + h, panel:] = extra
-
-
-def mix_kernel(width, where_ref, site_ref, kind_ref, operators_ref, probe_ref, mix_ref, look_ref):
+            out_ref[2 * q + h, panel:] = jnp.zeros_like(out_ref[0, panel:])
+            out_ref[2 * q + h, panel:, :128] = extra
+
+
+def mix_kernel(
+    width, where_ref, site_ref, kind_ref, operators_ref, probe_ref, mix_ref, look_ref, factor_ref, pair_ref
+):
     pair, front = where_ref[1], where_ref[6]
+    pair_ref[...] = jnp.zeros_like(pair_ref) + pair
     kind, site = kind_ref[front], site_ref[front]
     phys = probe_ref.shape[0]
     scale = 1.0 / math.sqrt(width)
@@ -255,14 +338,15 @@
             for t in range(phys):
                 row, col = (s, t) if slot == 0 else (t, s)
                 own = 1.0 if s == t else 0.0
-                mix_ref[slot, s, t] = jnp.where(
-                    site == 2 * pair + slot, operators_ref[kind, row, col], own
-                )
+                factor = jnp.where(site == 2 * pair + slot, operators_ref[kind, row, col], own)
+                mix_ref[slot, s, t] = factor
+                line = (slot * phys + s) * phys + t
+                factor_ref[line : line + 1] = jnp.zeros((1, factor_ref.shape[1]), jnp.float32) + factor
                 look_ref[slot, s, t] = probe_ref[row, col] * scale
 
 
 def cut_kernel(
-    where_ref, mine_ref, near_ref, start_ref, other_ref, later_ref, keep_ref, give_ref, env_ref, sem
+    where_ref, mine_ref, near_ref, start_ref, other_ref, keep_ref, give_ref, env_ref, sem
 ):
     core, half, front, parity = where_ref[4], where_ref[5], where_ref[6], where_ref[7]
     panel = other_ref.shape[0]
@@ -273,7 +357,6 @@
     env_ref[pl.ds(pl.multiple_of((1 - half) * panel, panel), panel)] = other_ref[...]
     wide = keep_ref.shape[2]
     mine, near = mine_ref[...], near_ref[...]
-    later_ref[...] = jnp.where(parity == 0, near, mine)
     begun = jnp.where(parity == 0, mine, near)
     low, high = begun[..., :wide], begun[..., wide:]
     keep_ref[...] = jnp.where(core == 0, low, high)
@@ -354,26 +437,31 @@
     square = jax.ShapeDtypeStruct((2, phys, phys), f32)
     part = jax.ShapeDtypeStruct((phys, panel, width // 2), bf16)
     bond = ("half", "member")
-    mixes, looks = pl.pallas_call(
+    mixes, looks, factors, pairs_here = pl.pallas_call(
         functools.partial(mix_kernel, width),
         in_specs=[SMEM] * 5,
-        out_specs=[SMEM] * 2,
-        out_shape=[square, square],
+        out_specs=[SMEM] * 2 + [VMEM] * 2,
+        out_shape=[
+            square,
+            square,
+            jax.ShapeDtypeStruct((2 * phys * phys, COLS), f32),
+            jax.ShapeDtypeStruct((8, 128), jnp.int32),
+        ],
         compiler_params=params(),
     )(where, op_site, op_kind, operators, probe)
-    where, other, mine, near, mixes, looks = lax.optimization_barrier(
-        (where, other, mine, near, mixes, looks)
+    where, other, mine, near, mixes, looks, factors, pairs_here = lax.optimization_barrier(
+        (where, other, mine, near, mixes, looks, factors, pairs_here)
     )
     small = (where, mixes, looks)
-    later, keep, give, env = pl.pallas_call(
+    after = lax.all_gather(jnp.where(parity == 0, near, mine), bond, axis=0)
+    keep, give, env = pl.pallas_call(
         cut_kernel,
         in_specs=[SMEM] + [VMEM] * 2 + [ANY, VMEM],
-        out_specs=[VMEM] * 4,
-        out_shape=[jax.ShapeDtypeStruct(mine.shape, bf16), part, part, env_shape],
+        out_specs=[VMEM] * 3,
+        out_shape=[part, part, env_shape],
         scratch_shapes=[pltpu.SemaphoreType.DMA((1,))],
         compiler_params=params(),
     )(where, mine, near, start_env, other)
-    after = lax.all_gather(later, bond, axis=0)
     twin = lax.ppermute(env, bond, twins(side))
     row = first_ring(keep, give, core, side)
     row, twin = lax.optimization_barrier((row, twin))
@@ -395,7 +483,7 @@
         out_shape=[jax.ShapeDtypeStruct((members, panel, 2 * lanes), bf16), seen_shape],
         scratch_shapes=[
             pltpu.VMEM((side * side, 2, phys, panel, width // 2), bf16),
-            pltpu.SemaphoreType.DMA((side, side)),
+            pltpu.SemaphoreType.DMA((width // 2 // COLS, side, side)),
         ],
         compiler_params=params(),
     )(*small, env, twin, *in_hbm(pieces))
@@ -430,11 +518,11 @@
         if now > 0:
             sent, seen, env = pl.pallas_call(
                 functools.partial(middle_kernel, now),
-                in_specs=[SMEM] * 3 + [VMEM] * 4,
+                in_specs=[VMEM] * 7,
                 out_specs=[VMEM] * 3,
                 out_shape=[sent_shape(0), seen_shape, env_shape],
                 compiler_params=params(),
-            )(*small, exchange(sent), before, after, seen)
+            )(*vectors, exchange(sent), before, after, seen)
             evens.append(env)
         env = pl.pallas_call(
             second_kernel,
@@ -455,38 +543,51 @@
                 compiler_params=params(),
             )(where, *in_hbm(everything))
             before = pltpu.with_memory_space_constraint(before, pltpu.VMEM)
+            bank = pl.pallas_call(
+                bank_kernel,
+                in_specs=[SMEM] * 2 + [VMEM] * 2,
+                out_specs=VMEM,
+                out_shape=jax.ShapeDtypeStruct((2, phys, rows, width), f32),
+                compiler_params=params(),
+            )(where, looks, before, after)
+            vectors = (pairs_here, factors, bank)
+        if now == pairs - 2:
+            env, *kept = lax.optimization_barrier((env, *evens, *odds))
+            picked = pl.pallas_call(
+                pick_kernel,
+                in_specs=[VMEM] * (1 + len(kept)),
+                out_specs=[VMEM] * 2,
+                out_shape=[env_shape] * 2,
+                compiler_params=params(),
+            )(pairs_here, *kept)
         env = lax.ppermute(env, "pair", [(now, now + 1)])
+        if now == pairs - 2:
+            env, picked = lax.optimization_barrier((env, picked))
         sent, seen = pl.pallas_call(
             functools.partial(first_kernel, now + 1),
-            in_specs=[SMEM] * 3 + [VMEM] * 3,
+            in_specs=[VMEM] * 6,
             out_specs=[VMEM] * 2,
             out_shape=[sent_shape(0), seen_shape],
             compiler_params=params(),
-        )(*small, env, before, seen)
+        )(*vectors, env, before, seen)
     moved = exchange(sent)
     sent, env = pl.pallas_call(
         functools.partial(end_kernel, pairs - 1),
-        in_specs=[SMEM] * 3 + [VMEM] * 4,
+        in_specs=[VMEM] * 7,
         out_specs=[VMEM] * 2,
         out_shape=[sent_shape(EXTRA), env_shape],
         compiler_params=params(),
-    )(*small, moved, before, after, seen)
-    evens.append(env)
-    kept = evens + odds
+    )(*vectors, moved, before, after, seen)
     homeward = pl.pallas_call(
-        home_kernel,
-        in_specs=[SMEM] + [VMEM] * 2 + [ANY] * len(kept),
+        functools.partial(home_kernel, pairs - 1),
+        in_specs=[VMEM] * 6,
         out_specs=VMEM,
         out_shape=jax.ShapeDtypeStruct((fronts, panel + EXTRA, width), bf16),
-        scratch_shapes=[
-            pltpu.VMEM((rows, width), bf16),
-            pltpu.VMEM((2, rows, width), bf16),
-            pltpu.SemaphoreType.DMA((2,)),
-        ],
+        scratch_shapes=[pltpu.VMEM((rows, width), bf16)],
         compiler_params=params(),
-    )(where, exchange(sent), after, *kept)
+    )(pairs_here, exchange(sent), after, *picked, env)
     home = lax.all_to_all(homeward, ("parity", "half"), 0, 0, tiled=True)
-    values = jnp.sum(home[:, panel : panel + 3, 0].astype(f32), axis=1)
+    values = jnp.sum(home[:, panel:, :128].astype(f32), axis=(1, 2))
     return home[None, :, :panel], values[:, None]
 
 

time: 277 us -> 265 us (0.957)
  waiting for transfers between devices: 67.2 us -> 57.6 us
  Pallas kernels: 51.3 us -> 45.3 us
  starting transfers between devices: 22.3 us -> 26.3 us
    ppermute x4, starting transfers between devices: 0.51 us -> 8.65 us  [swap_cores(): return [lax.ppermute(p, ('half', 'member'), twins(side)) for p in pieces]]
    ppermute x3, waiting for transfers between devices: 26 us -> 18.3 us  [second_ring(): lax.ppermute(row, bond, shifts(side, m, False))]
    all_gather x1, waiting for transfers between devices: 5.97 us -> 0.02 us  [on_device(): after = lax.all_gather(jnp.where(parity == 0, near, mine), bond, axis=0)]
    ppermute x3, waiting for transfers between devices: 5.69 us -> 10.4 us  [first_ring(): lax.ppermute(chip, bond, shifts(side, k, True))]
    pallas_call x7 -> x9, Pallas kernels: 23.1 us -> 18.8 us  [the longest x2 6.99 us: on_device(): pl.pallas_call(functools.partial(middle_kernel, now), in_specs=[VMEM] * 7...]
  transfers between devices with their start and end apart: 19 -> 19, of which waited for: 8 -> 8; matrix products, arithmetic and copies ran while one was open for 1% -> 1% of each run, Pallas kernels for 6% -> 7%
where the time goes in v3:
time: 265 us
  blocking collectives  113 us (43%)
  waiting for transfers between devices  57.6 us (22%)
  Pallas kernels  45.3 us (17%)
  starting transfers between devices  26.3 us (10%)
  between operations  14.3 us (5%)
  local copies, waits for them, and re-layouts  6.43 us (2%)
    all_to_all x7, blocking collectives, exchange(): return lax.all_to_all(sent, 'member', 0, 0, tiled=True)  98.2 us
    ppermute x3, waiting for transfers between devices, second_ring(): lax.ppermute(row, bond, shifts(side, m, False))  18.3 us
    all_to_all x1, blocking collectives, on_device(): home = lax.all_to_all(homeward, ('parity', 'half'), 0, 0, tiled=True)  14.9 us
    all_to_all x1, waiting for transfers between devices, exchange(): return lax.all_to_all(sent, 'member', 0, 0, tiled=True)  14 us
    ppermute x3, waiting for transfers between devices, on_device(): env = lax.ppermute(env, 'pair', [(now, now + 1)])  13.5 us
    ppermute x3, waiting for transfers between devices, first_ring(): lax.ppermute(chip, bond, shifts(side, k, True))  10.4 us
    ppermute x4, starting transfers between devices, swap_cores(): return [lax.ppermute(p, ('half', 'member'), twins(side)) for p in pieces]  8.65 us
    pallas_call x2, Pallas kernels, on_device(): pl.pallas_call(functools.partial(middle_kernel, now), in_specs=[VMEM] * 7...  6.99 us
  transfers between devices with their start and end apart: 19, of which 8 were waited for; matrix products, arithmetic and copies ran while one was open for 1% of the time, Pallas kernels for 7%

profile of v3, /device:TPU:192, one launch (start us, length us, event | category | flops | bytes accessed | tf_op | source)
XLA Modules:
  0.0 264.6 jit_solution(7170353473208496688)
XLA Ops:
  7.2 0.0 all-gather.3.cloned.1.call-start
  7.2 1.0 copy.13
  8.2 1.1 collective-permute-start.1
  9.3 0.8 dynamic-slice_bitcast_fusion
  10.2 3.2 %collective-permute-start = (bf16[32,1024]{1,0:T(8,128)(2,1)S(1)}, bf16[32,1024]{1,0:T(8,128)(2,1)S(1)}, u32[]{:S(2)}, u32[]{:S(2)}) collective-permute-start(bf16[32,1024]{1,0:T(8,128)(2,1)S(1)} %dynamic-slice_bitcast_fusion), channel_id=1, source_target_pairs={{0,16},{16,0},{1,17},{17,1},{2,18},{18,2},{3,19},{19,3},{4,20},{20... | collective-permute-start | bytes 196616 | tf_op jit(solution)/shard_map/ppermute | solution.py:435
  13.4 0.8 copy.11.operators_ref
  14.2 0.1 stack.70.where_ref
  14.3 0.7 copy-done.2
  15.0 0.7 copy-done.3
  15.6 0.7 copy-done.4
  16.3 1.5 shard_map.77
  17.8 0.7 broadcast_select_fusion
  18.6 0.0 all-gather.3.cloned.1.call-update
  18.6 0.9 copy-done.1
  19.6 0.7 shard_map.78
  20.2 0.1 collective-permute-start.2
  20.3 1.3 collective-permute-done.2
  21.7 2.8 %collective-permute-start.5 = (bf16[2,4,32,512]{3,2,1,0:T(8,128)(2,1)S(1)}, bf16[2,4,32,512]{3,2,1,0:T(8,128)(2,1)S(1)}, u32[]{:S(2)}, u32[]{:S(2)}) collective-permute-start(bf16[2,4,32,512]{3,2,1,0:T(8,128)(2,1)S(1)} %maximum_select_fusion.1), channel_id=1, source_target_pairs={{0,6},{1,25},{2,0},{3,27},{4,2},{5,29},{6,4},{7,31},{8,14},{9,1},{... | collective-permute-start | bytes 786440 | tf_op jit(solution)/shard_map/ppermute | solution.py:396
  24.5 0.8 collective-permute-start.4
  25.3 0.9 collective-permute-start.3
  26.3 5.0 %collective-permute-done.5 = bf16[2,4,32,512]{3,2,1,0:T(8,128)(2,1)S(1)} collective-permute-done((bf16[2,4,32,512]{3,2,1,0:T(8,128)(2,1)S(1)}, bf16[2,4,32,512]{3,2,1,0:T(8,128)(2,1)S(1)}, u32[]{:S(2)}, u32[]{:S(2)}) %collective-permute-start.5) | collective-permute-done | bytes 262176 | tf_op jit(solution)/shard_map/ppermute | solution.py:396
  31.3 1.2 collective-permute-done.4
  32.5 4.1 %collective-permute-done.3 = bf16[2,4,32,512]{3,2,1,0:T(8,128)(2,1)S(1)} collective-permute-done((bf16[2,4,32,512]{3,2,1,0:T(8,128)(2,1)S(1)}, bf16[2,4,32,512]{3,2,1,0:T(8,128)(2,1)S(1)}, u32[]{:S(2)}, u32[]{:S(2)}) %collective-permute-start.3) | collective-permute-done | bytes 262176 | tf_op jit(solution)/shard_map/ppermute | solution.py:396
  36.6 0.1 pad_maximum_fusion.refs_0_
  36.8 0.2 collective-permute-start.9
  37.0 1.2 collective-permute-start.8
  38.2 0.7 collective-permute-start.7
  38.9 14.0 %collective-permute-done.9.refs_3_ = bf16[4,2,4,32,512]{4,3,2,1,0:T(8,128)(2,1)S(1)} collective-permute-done((bf16[4,2,4,32,512]{4,3,2,1,0:T(8,128)(2,1)S(1)}, bf16[4,2,4,32,512]{4,3,2,1,0:T(8,128)(2,1)S(1)}, u32[]{:S(2)}, u32[]{:S(2)}) %collective-permute-start.9) | collective-permute-done | bytes 1048608 | tf_op jit(solution)/shard_map/ppermute | solution.py:401
  52.9 8.6 %collective-permute-start.13 = (bf16[4,2,4,32,512]{4,3,2,1,0:T(8,128)(2,1)S(1)}, bf16[4,2,4,32,512]{4,3,2,1,0:T(8,128)(2,1)}, u32[]{:S(2)}, u32[]{:S(2)}) collective-permute-start(bf16[4,2,4,32,512]{4,3,2,1,0:T(8,128)(2,1)S(1)} %collective-permute-done.9.refs_3_), channel_id=1, source_target_pairs={{0,1},{1,0},{2,3},{3,2},{4,5},{5,4},{6,7},{7,6},{8,9},{9,8},{10,11... | collective-permute-start | bytes 3145736 | tf_op jit(solution)/shard_map/ppermute | solution.py:405
  61.5 0.1 collective-permute-start.12
  61.5 4.3 %collective-permute-done.7.refs_1_ = bf16[4,2,4,32,512]{4,3,2,1,0:T(8,128)(2,1)} collective-permute-done((bf16[4,2,4,32,512]{4,3,2,1,0:T(8,128)(2,1)S(1)}, bf16[4,2,4,32,512]{4,3,2,1,0:T(8,128)(2,1)}, u32[]{:S(2)}, u32[]{:S(2)}) %collective-permute-start.7) | collective-permute-done | bytes 1048608 | tf_op jit(solution)/shard_map/ppermute | solution.py:401
  65.9 4.8 %shard_map.79 = (bf16[16,32,512]{2,1,0:T(8,128)(2,1)}, f32[2,8,128]{2,1,0:T(8,128)S(1)}) custom-call(s32[8]{0:T(128)S(1)} %stack.70.where_ref, f32[2,4,4]{2,1,0:T(4,128)S(1)} %get-tuple-element.68.mix_ref, f32[2,4,4]{2,1,0:T(4,128)S(1)} %get-tuple-element.67.look_ref, bf16[64,1024]{1,0:T(8,128)(2,1)S(1)} %get-tuple-element.72.env_ref, ...), custom_call_target="tpu_custom_call" | custom-call | tf_op jit(solution)/shard_map/pallas_call | solution.py:479
  70.7 3.8 %all-to-all-start = ((bf16[16,32,512]{2,1,0:T(8,128)(2,1)}), bf16[16,32,512]{2,1,0:T(8,128)(2,1)S(1)}, u32[]{:S(2)}, u32[]{:S(2)}) async-start(bf16[16,32,512]{2,1,0:T(8,128)(2,1)} %get-tuple-element.77), calls=%async_computation | async-start | bytes 1048576 | tf_op jit(solution)/shard_map/all_to_all | solution.py:477
  74.4 14.0 %all-to-all-done.moved_ref = bf16[16,32,512]{2,1,0:T(8,128)(2,1)S(1)} async-done(((bf16[16,32,512]{2,1,0:T(8,128)(2,1)}), bf16[16,32,512]{2,1,0:T(8,128)(2,1)S(1)}, u32[]{:S(2)}, u32[]{:S(2)}) %all-to-all-start) | async-done | bytes 524320 | tf_op jit(solution)/shard_map/all_to_all | solution.py:477
  88.4 5.3 %shard_map.80.env_ref.refs_0_ = bf16[64,1024]{1,0:T(8,128)(2,1)S(1)} custom-call(s32[8]{0:T(128)S(1)} %stack.70.where_ref, bf16[16,32,512]{2,1,0:T(8,128)(2,1)S(1)} %all-to-all-done.moved_ref, bf16[4,2,4,32,512]{4,3,2,1,0:T(8,128)(2,1)} %copy-done.5, bf16[4,2,4,32,512]{4,3,2,1,0:T(8,128)(2,1)} %collective-permute-done.7.refs_1_, ...), custom_call_target="tpu_custom_call" | custom-call | tf_op jit(solution)/shard_map/pallas_call | solution.py:494
  93.7 0.0 all-gather.3.cloned.1.call-done
  93.8 5.3 %shard_map.81 = (bf16[16,64,256]{2,1,0:T(8,128)(2,1)S(1)}, f32[2,8,128]{2,1,0:T(8,128)S(1)}) custom-call(s32[8]{0:T(128)S(1)} %stack.70.where_ref, f32[2,4,4]{2,1,0:T(4,128)S(1)} %get-tuple-element.68.mix_ref, f32[2,4,4]{2,1,0:T(4,128)S(1)} %get-tuple-element.67.look_ref, bf16[64,1024]{1,0:T(8,128)(2,1)S(1)} %shard_map.80.env_ref.refs_0_, ...), custom_call_target="tpu_custom_call" | custom-call | tf_op jit(solution)/shard_map/pallas_call | solution.py:504
  99.0 15.8 %all_to_all.45.moved_ref = bf16[16,64,256]{2,1,0:T(8,128)(2,1)S(1)} all-to-all(bf16[16,64,256]{2,1,0:T(8,128)(2,1)S(1)} %get-tuple-element.81), channel_id=1, replica_groups=mesh['pair'=4,'parity'=2,'half'=2,'member'=16] {'member'}, dimensions={0} | all-to-all | bytes 1048576 | tf_op jit(solution)/shard_map/all_to_all | solution.py:477
  114.8 1.6 shard_map.82.refs_3_
  116.4 0.7 collective-permute-start.14
  117.1 4.2 %shard_map.83.refs_0_.tensor_ref.old_ref = bf16[16,2,2,4,32,512]{5,4,3,2,1,0:T(8,128)(2,1)S(1)} custom-call(s32[8]{0:T(128)S(1)} %stack.70.where_ref, bf16[4,2,4,32,512]{4,3,2,1,0:T(8,128)(2,1)} %copy-done.5, bf16[4,2,4,32,512]{4,3,2,1,0:T(8,128)(2,1)} %collective-permute-done.7.refs_1_, bf16[4,2,4,32,512]{4,3,2,1,0:T(8,128)(2,1)} %collective-permute-done.8.refs_2_, ...), custom_call_target="tpu_custom_call" | custom-call | tf_op jit(solution)/shard_map/pallas_call | solution.py:537
  121.4 1.2 shard_map.84.bank_ref
  122.6 1.8 shard_map.85
  124.4 13.5 %all_to_all.46.moved_ref = bf16[16,64,256]{2,1,0:T(8,128)(2,1)S(1)} all-to-all(bf16[16,64,256]{2,1,0:T(8,128)(2,1)S(1)} %get-tuple-element.92), channel_id=1, replica_groups=mesh['pair'=4,'parity'=2,'half'=2,'member'=16] {'member'}, dimensions={0} | all-to-all | bytes 1048576 | tf_op jit(solution)/shard_map/all_to_all | solution.py:477
  137.9 3.5 %shard_map.86 = (bf16[16,64,256]{2,1,0:T(8,128)(2,1)S(1)}, f32[2,8,128]{2,1,0:T(8,128)S(1)}, bf16[64,1024]{1,0:T(8,128)(2,1)S(1)}) custom-call(s32[8,128]{1,0:T(8,128)S(1)} %get-tuple-element.64.pair_ref, f32[32,256]{1,0:T(8,128)S(1)} %get-tuple-element.65.mix_ref, f32[2,4,64,1024]{3,2,1,0:T(8,128)S(1)} %shard_map.84.bank_ref, ...), custom_call_target="tpu_custom_call" | custom-call | tf_op jit(solution)/shard_map/pallas_call | solution.py:519
  141.4 13.5 %all_to_all.47.moved_ref = bf16[16,64,256]{2,1,0:T(8,128)(2,1)S(1)} all-to-all(bf16[16,64,256]{2,1,0:T(8,128)(2,1)S(1)} %get-tuple-element.94), channel_id=1, replica_groups=mesh['pair'=4,'parity'=2,'half'=2,'member'=16] {'member'}, dimensions={0} | all-to-all | bytes 1048576 | tf_op jit(solution)/shard_map/all_to_all | solution.py:477
  154.8 1.6 shard_map.87.refs_4_
  156.4 0.9 collective-permute-start.15
  157.3 1.8 shard_map.88
  159.1 13.5 %all_to_all.48.moved_ref = bf16[16,64,256]{2,1,0:T(8,128)(2,1)S(1)} all-to-all(bf16[16,64,256]{2,1,0:T(8,128)(2,1)S(1)} %get-tuple-element.96), channel_id=1, replica_groups=mesh['pair'=4,'parity'=2,'half'=2,'member'=16] {'member'}, dimensions={0} | all-to-all | bytes 1048576 | tf_op jit(solution)/shard_map/all_to_all | solution.py:477
  172.6 3.5 %shard_map.89 = (bf16[16,64,256]{2,1,0:T(8,128)(2,1)S(1)}, f32[2,8,128]{2,1,0:T(8,128)S(1)}, bf16[64,1024]{1,0:T(8,128)(2,1)S(1)}) custom-call(s32[8,128]{1,0:T(8,128)S(1)} %get-tuple-element.64.pair_ref, f32[32,256]{1,0:T(8,128)S(1)} %get-tuple-element.65.mix_ref, f32[2,4,64,1024]{3,2,1,0:T(8,128)S(1)} %shard_map.84.bank_ref, ...), custom_call_target="tpu_custom_call" | custom-call | tf_op jit(solution)/shard_map/pallas_call | solution.py:519
  176.1 13.5 %all_to_all.49.moved_ref = bf16[16,64,256]{2,1,0:T(8,128)(2,1)S(1)} all-to-all(bf16[16,64,256]{2,1,0:T(8,128)(2,1)S(1)} %get-tuple-element.98), channel_id=1, replica_groups=mesh['pair'=4,'parity'=2,'half'=2,'member'=16] {'member'}, dimensions={0} | all-to-all | bytes 1048576 | tf_op jit(solution)/shard_map/all_to_all | solution.py:477
  189.6 1.6 shard_map.90.refs_5_
  191.2 1.3 collective-permute-start.16
  192.5 0.1 shard_map.91
  192.6 13.5 %collective-permute-done.16.env_ref = bf16[64,1024]{1,0:T(8,128)(2,1)S(1)} collective-permute-done((bf16[64,1024]{1,0:T(8,128)(2,1)S(1)}, bf16[64,1024]{1,0:T(8,128)(2,1)S(1)}, u32[]{:S(2)}, u32[]{:S(2)}) %collective-permute-start.16) | collective-permute-done | bytes 131104 | tf_op jit(solution)/shard_map/ppermute | solution.py:563
  206.1 1.8 shard_map.92
  207.9 13.9 %all_to_all.50.moved_ref = bf16[16,64,256]{2,1,0:T(8,128)(2,1)S(1)} all-to-all(bf16[16,64,256]{2,1,0:T(8,128)(2,1)S(1)} %get-tuple-element.112), channel_id=1, replica_groups=mesh['pair'=4,'parity'=2,'half'=2,'member'=16] {'member'}, dimensions={0} | all-to-all | bytes 1048576 | tf_op jit(solution)/shard_map/all_to_all | solution.py:477
  221.8 3.5 %shard_map.93 = (bf16[16,80,256]{2,1,0:T(8,128)(2,1)S(1)}, bf16[64,1024]{1,0:T(8,128)(2,1)S(1)}) custom-call(s32[8,128]{1,0:T(8,128)S(1)} %get-tuple-element.64.pair_ref, f32[32,256]{1,0:T(8,128)S(1)} %get-tuple-element.65.mix_ref, f32[2,4,64,1024]{3,2,1,0:T(8,128)S(1)} %shard_map.84.bank_ref, bf16[16,64,256]{2,1,0:T(8,128)(2,1)S(1)} %all_to_all.50.moved_ref, ...), custom_call_target="tpu_custom_call" | custom-call | tf_op jit(solution)/shard_map/pallas_call | solution.py:574
  225.3 14.6 %all_to_all.51.moved_ref = bf16[16,80,256]{2,1,0:T(8,128)(2,1)S(1)} all-to-all(bf16[16,80,256]{2,1,0:T(8,128)(2,1)S(1)} %get-tuple-element.114), channel_id=1, replica_groups=mesh['pair'=4,'parity'=2,'half'=2,'member'=16] {'member'}, dimensions={0} | all-to-all | bytes 1310720 | tf_op jit(solution)/shard_map/all_to_all | solution.py:477
  239.9 1.6 shard_map.94
  241.5 14.9 %all_to_all.52 = bf16[4,48,1024]{2,1,0:T(8,128)(2,1)S(1)} all-to-all(bf16[4,48,1024]{2,1,0:T(8,128)(2,1)S(1)} %shard_map.94), channel_id=1, replica_groups=mesh['pair'=4,'parity'=2,'half'=2,'member'=16] {'parity','half'}, dimensions={0} | all-to-all | bytes 786432 | tf_op jit(solution)/shard_map/all_to_all | solution.py:589
  256.4 0.6 convert_reduce_fusion
  257.0 0.7 slice_bitcast_fusion
  (25 shorter events, 0.1 us)
Async XLA Ops:
  7.2 86.6 %all-gather.3.cloned.1.call-start = ((), (), s32[]{:S(2)}) async-start(), calls=%async_computation.9 | async-start | bytes 8650752 | tf_op jit(solution)/shard_map/all_gather | solution.py:456
  8.2 9.6 %collective-permute-start.1 = (bf16[4,32,1024]{2,1,0:T(8,128)(2,1)S(1)}, bf16[4,32,1024]{2,1,0:T(8,128)(2,1)S(1)}, u32[]{:S(2)}, u32[]{:S(2)}) collective-permute-start(bf16[4,32,1024]{2,1,0:T(8,128)(2,1)S(1)} %bitcast.35), channel_id=1, source_target_pairs={{0,32},{32,0},{1,33},{33,1},{2,34},{34,2},{3,35},{35,3},{4,36},{36... | collective-permute-start | bytes 786440 | tf_op jit(solution)/shard_map/ppermute | solution.py:433
  10.2 7.6 %collective-permute-start = (bf16[32,1024]{1,0:T(8,128)(2,1)S(1)}, bf16[32,1024]{1,0:T(8,128)(2,1)S(1)}, u32[]{:S(2)}, u32[]{:S(2)}) collective-permute-start(bf16[32,1024]{1,0:T(8,128)(2,1)S(1)} %dynamic-slice_bitcast_fusion), channel_id=1, source_target_pairs={{0,16},{16,0},{1,17},{17,1},{2,18},{18,2},{3,19},{19,3},{4,20},{20... | collective-permute-start | bytes 196616 | tf_op jit(solution)/shard_map/ppermute | solution.py:435
  14.3 0.7 copy-start.2
  15.0 0.7 copy-start.3
  15.6 0.7 copy-start.4
  18.6 1.0 copy-start.1
  20.2 1.4 collective-permute-start.2
  21.7 9.6 %collective-permute-start.5 = (bf16[2,4,32,512]{3,2,1,0:T(8,128)(2,1)S(1)}, bf16[2,4,32,512]{3,2,1,0:T(8,128)(2,1)S(1)}, u32[]{:S(2)}, u32[]{:S(2)}) collective-permute-start(bf16[2,4,32,512]{3,2,1,0:T(8,128)(2,1)S(1)} %maximum_select_fusion.1), channel_id=1, source_target_pairs={{0,6},{1,25},{2,0},{3,27},{4,2},{5,29},{6,4},{7,31},{8,14},{9,1},{... | collective-permute-start | bytes 786440 | tf_op jit(solution)/shard_map/ppermute | solution.py:396
  24.5 8.0 %collective-permute-start.4 = (bf16[2,4,32,512]{3,2,1,0:T(8,128)(2,1)S(1)}, bf16[2,4,32,512]{3,2,1,0:T(8,128)(2,1)S(1)}, u32[]{:S(2)}, u32[]{:S(2)}) collective-permute-start(bf16[2,4,32,512]{3,2,1,0:T(8,128)(2,1)S(1)} %maximum_select_fusion.1), channel_id=1, source_target_pairs={{0,4},{1,17},{2,6},{3,19},{4,0},{5,21},{6,2},{7,23},{8,12},{9,25},... | collective-permute-start | bytes 786440 | tf_op jit(solution)/shard_map/ppermute | solution.py:396
  25.3 11.3 %collective-permute-start.3 = (bf16[2,4,32,512]{3,2,1,0:T(8,128)(2,1)S(1)}, bf16[2,4,32,512]{3,2,1,0:T(8,128)(2,1)S(1)}, u32[]{:S(2)}, u32[]{:S(2)}) collective-permute-start(bf16[2,4,32,512]{3,2,1,0:T(8,128)(2,1)S(1)} %maximum_select_fusion.1), channel_id=1, source_target_pairs={{0,2},{1,9},{2,4},{3,11},{4,6},{5,13},{6,0},{7,15},{8,10},{9,17},{... | collective-permute-start | bytes 786440 | tf_op jit(solution)/shard_map/ppermute | solution.py:396
  26.2 10.6 %collective-permute-start.6 = (bf16[64,1024]{1,0:T(8,128)(2,1)S(1)}, bf16[64,1024]{1,0:T(8,128)(2,1)S(1)}, u32[]{:S(2)}, u32[]{:S(2)}) collective-permute-start(bf16[64,1024]{1,0:T(8,128)(2,1)S(1)} %get-tuple-element.72.env_ref), channel_id=1, source_target_pairs={{0,1},{1,0},{2,3},{3,2},{4,5},{5,4},{6,7},{7,6},{8,9},{9,8},{10,11... | collective-permute-start | bytes 393224 | tf_op jit(solution)/shard_map/ppermute | solution.py:465
  36.8 29.1 %copy-start.5 = (bf16[4,2,4,32,512]{4,3,2,1,0:T(8,128)(2,1)}, bf16[4,2,4,32,512]{4,3,2,1,0:T(8,128)(2,1)S(1)}, u32[]{:S(2)}) copy-start(bf16[4,2,4,32,512]{4,3,2,1,0:T(8,128)(2,1)S(1)} %pad_maximum_fusion.refs_0_) | copy-start | bytes 3145732
  36.8 16.1 %collective-permute-start.9 = (bf16[4,2,4,32,512]{4,3,2,1,0:T(8,128)(2,1)S(1)}, bf16[4,2,4,32,512]{4,3,2,1,0:T(8,128)(2,1)S(1)}, u32[]{:S(2)}, u32[]{:S(2)}) collective-permute-start(bf16[4,2,4,32,512]{4,3,2,1,0:T(8,128)(2,1)S(1)} %pad_maximum_fusion.refs_0_), channel_id=1, source_target_pairs={{0,24},{1,7},{2,26},{3,1},{4,28},{5,3},{6,30},{7,5},{8,0},{9,15},{... | collective-permute-start | bytes 3145736 | tf_op jit(solution)/shard_map/ppermute | solution.py:401
  37.0 24.5 %collective-permute-start.8 = (bf16[4,2,4,32,512]{4,3,2,1,0:T(8,128)(2,1)S(1)}, bf16[4,2,4,32,512]{4,3,2,1,0:T(8,128)(2,1)}, u32[]{:S(2)}, u32[]{:S(2)}) collective-permute-start(bf16[4,2,4,32,512]{4,3,2,1,0:T(8,128)(2,1)S(1)} %pad_maximum_fusion.refs_0_), channel_id=1, source_target_pairs={{0,16},{1,5},{2,18},{3,7},{4,20},{5,1},{6,22},{7,3},{8,24},{9,13},... | collective-permute-start | bytes 3145736 | tf_op jit(solution)/shard_map/ppermute | solution.py:401
  38.2 27.7 %collective-permute-start.7 = (bf16[4,2,4,32,512]{4,3,2,1,0:T(8,128)(2,1)S(1)}, bf16[4,2,4,32,512]{4,3,2,1,0:T(8,128)(2,1)}, u32[]{:S(2)}, u32[]{:S(2)}) collective-permute-start(bf16[4,2,4,32,512]{4,3,2,1,0:T(8,128)(2,1)S(1)} %pad_maximum_fusion.refs_0_), channel_id=1, source_target_pairs={{0,8},{1,3},{2,10},{3,5},{4,12},{5,7},{6,14},{7,1},{8,16},{9,11},{... | collective-permute-start | bytes 3145736 | tf_op jit(solution)/shard_map/ppermute | solution.py:401
  38.9 35.5 %collective-permute-start.10 = (bf16[4,2,4,32,512]{4,3,2,1,0:T(8,128)(2,1)S(1)}, bf16[4,2,4,32,512]{4,3,2,1,0:T(8,128)(2,1)}, u32[]{:S(2)}, u32[]{:S(2)}) collective-permute-start(bf16[4,2,4,32,512]{4,3,2,1,0:T(8,128)(2,1)S(1)} %pad_maximum_fusion.refs_0_), channel_id=1, source_target_pairs={{0,1},{1,0},{2,3},{3,2},{4,5},{5,4},{6,7},{7,6},{8,9},{9,8},{10,11... | collective-permute-start | bytes 3145736 | tf_op jit(solution)/shard_map/ppermute | solution.py:405
  52.9 13.0 %copy-start.6 = (bf16[4,2,4,32,512]{4,3,2,1,0:T(8,128)(2,1)}, bf16[4,2,4,32,512]{4,3,2,1,0:T(8,128)(2,1)S(1)}, u32[]{:S(2)}) copy-start(bf16[4,2,4,32,512]{4,3,2,1,0:T(8,128)(2,1)S(1)} %collective-permute-done.9.refs_3_) | copy-start | bytes 3145732
  52.9 35.5 %collective-permute-start.13 = (bf16[4,2,4,32,512]{4,3,2,1,0:T(8,128)(2,1)S(1)}, bf16[4,2,4,32,512]{4,3,2,1,0:T(8,128)(2,1)}, u32[]{:S(2)}, u32[]{:S(2)}) collective-permute-start(bf16[4,2,4,32,512]{4,3,2,1,0:T(8,128)(2,1)S(1)} %collective-permute-done.9.refs_3_), channel_id=1, source_target_pairs={{0,1},{1,0},{2,3},{3,2},{4,5},{5,4},{6,7},{7,6},{8,9},{9,8},{10,11... | collective-permute-start | bytes 3145736 | tf_op jit(solution)/shard_map/ppermute | solution.py:405
  61.5 27.0 %collective-permute-start.12 = (bf16[4,2,4,32,512]{4,3,2,1,0:T(8,128)(2,1)}, bf16[4,2,4,32,512]{4,3,2,1,0:T(8,128)(2,1)}, u32[]{:S(2)}, u32[]{:S(2)}) collective-permute-start(bf16[4,2,4,32,512]{4,3,2,1,0:T(8,128)(2,1)} %collective-permute-done.8.refs_2_), channel_id=1, source_target_pairs={{0,1},{1,0},{2,3},{3,2},{4,5},{5,4},{6,7},{7,6},{8,9},{9,8},{10,11... | collective-permute-start | bytes 3145736 | tf_op jit(solution)/shard_map/ppermute | solution.py:405
  65.9 22.6 %collective-permute-start.11 = (bf16[4,2,4,32,512]{4,3,2,1,0:T(8,128)(2,1)}, bf16[4,2,4,32,512]{4,3,2,1,0:T(8,128)(2,1)}, u32[]{:S(2)}, u32[]{:S(2)}) collective-permute-start(bf16[4,2,4,32,512]{4,3,2,1,0:T(8,128)(2,1)} %collective-permute-done.7.refs_1_), channel_id=1, source_target_pairs={{0,1},{1,0},{2,3},{3,2},{4,5},{5,4},{6,7},{7,6},{8,9},{9,8},{10,11... | collective-permute-start | bytes 3145736 | tf_op jit(solution)/shard_map/ppermute | solution.py:405
  70.7 17.8 %all-to-all-start = ((bf16[16,32,512]{2,1,0:T(8,128)(2,1)}), bf16[16,32,512]{2,1,0:T(8,128)(2,1)S(1)}, u32[]{:S(2)}, u32[]{:S(2)}) async-start(bf16[16,32,512]{2,1,0:T(8,128)(2,1)} %get-tuple-element.77), calls=%async_computation | async-start | bytes 1048576 | tf_op jit(solution)/shard_map/all_to_all | solution.py:477
  93.7 21.1 %copy-start = (bf16[128,32,1024]{2,1,0:T(8,128)(2,1)S(1)}, bf16[128,32,1024]{2,1,0:T(8,128)(2,1)}, u32[]{:S(2)}) copy-start(bf16[128,32,1024]{2,1,0:T(8,128)(2,1)} %all-gather.3.cloned.1.call-done) | copy-start | bytes 25165828
  116.4 6.1 %collective-permute-start.14 = (bf16[64,1024]{1,0:T(8,128)(2,1)S(1)}, bf16[64,1024]{1,0:T(8,128)(2,1)S(1)}, u32[]{:S(2)}, u32[]{:S(2)}) collective-permute-start(bf16[64,1024]{1,0:T(8,128)(2,1)S(1)} %shard_map.82.refs_3_), channel_id=1, source_target_pairs={{0,64},{1,65},{2,66},{3,67},{4,68},{5,69},{6,70},{7,71},{8,72},{9,... | collective-permute-start | bytes 393224 | tf_op jit(solution)/shard_map/ppermute | solution.py:563
  156.4 0.9 collective-permute-start.15
  191.2 14.9 %collective-permute-start.16 = (bf16[64,1024]{1,0:T(8,128)(2,1)S(1)}, bf16[64,1024]{1,0:T(8,128)(2,1)S(1)}, u32[]{:S(2)}, u32[]{:S(2)}) collective-permute-start(bf16[64,1024]{1,0:T(8,128)(2,1)S(1)} %shard_map.90.refs_5_), channel_id=1, source_target_pairs={{128,192},{129,193},{130,194},{131,195},{132,196},{133,197},{134,1... | collective-permute-start | bytes 393224 | tf_op jit(solution)/shard_map/ppermute | solution.py:563
Sparse Core Ops, SparseCore 0:
  18.7 74.9 all-gather.2

commit v4 on v3

--- a/solution.py
+++ b/solution.py
@@ -319,10 +319,23 @@
         result = jnp.where(here, last[...], kept[...])
         value = values[:, q * 128 : (q + 1) * 128]
         extra = two_parts(value[:8] + value[8:])
+        extra = jnp.concatenate([extra, jnp.zeros_like(extra)], axis=0)
+        width = result.shape[1]
         for h in range(2):
-            out_ref[2 * q + h, :panel] = result[h * panel : (h + 1) * panel]
-            out_ref[2 * q + h, panel:] = jnp.zeros_like(out_ref[0, panel:])
-            out_ref[2 * q + h, panel:, :128] = extra
+            out_ref[2 * q + h, :, :width] = result[h * panel : (h + 1) * panel]
+            out_ref[2 * q + h, :, width:] = extra
+
+
+def out_kernel(home_ref, out_ref, value_ref):
+    fronts, width = out_ref.shape[1], out_ref.shape[3]
+    out_ref[0] = home_ref[:, :, :width]
+    lane = lax.broadcasted_iota(jnp.int32, (1, 128), 1)
+    values = jnp.zeros((1, 128), jnp.float32)
+    for f in range(fronts):
+        rows = home_ref[f, :, width:].astype(jnp.float32)
+        value = jnp.sum(jnp.sum(rows, axis=0, keepdims=True), axis=1, keepdims=True)
+        values = jnp.where(lane == f, value, values)
+    value_ref[...] = values[:, :fronts]
 
 
 def mix_kernel(
@@ -582,13 +595,22 @@
         functools.partial(home_kernel, pairs - 1),
         in_specs=[VMEM] * 6,
         out_specs=VMEM,
-        out_shape=jax.ShapeDtypeStruct((fronts, panel + EXTRA, width), bf16),
+        out_shape=jax.ShapeDtypeStruct((fronts, panel, width + 128), bf16),
         scratch_shapes=[pltpu.VMEM((rows, width), bf16)],
         compiler_params=params(),
     )(pairs_here, exchange(sent), after, *picked, env)
     home = lax.all_to_all(homeward, ("parity", "half"), 0, 0, tiled=True)
-    values = jnp.sum(home[:, panel:, :128].astype(f32), axis=(1, 2))
-    return home[None, :, :panel], values[:, None]
+    out, values = pl.pallas_call(
+        out_kernel,
+        in_specs=[VMEM],
+        out_specs=[VMEM] * 2,
+        out_shape=[
+            jax.ShapeDtypeStruct((1, fronts, panel, width), bf16),
+            jax.ShapeDtypeStruct((1, fronts), f32),
+        ],
+        compiler_params=params(),
+    )(home)
+    return out, values.reshape(fronts, 1)
 
 
 def solution(mesh):

time: 265 us -> 264 us (level)
  no operation moved by 1% of the time
where the time goes in v4:
time: 264 us; the launch traced here: 263 us
  blocking collectives  112 us (42%)
  waiting for transfers between devices  57.6 us (22%)
  Pallas kernels  46 us (17%)
  starting transfers between devices  26.3 us (10%)
  between operations  14.3 us (5%)
  local copies, waits for them, and re-layouts  5.71 us (2%)
    all_to_all x7, blocking collectives, exchange(): return lax.all_to_all(sent, 'member', 0, 0, tiled=True)  98.2 us
    ppermute x3, waiting for transfers between devices, second_ring(): lax.ppermute(row, bond, shifts(side, m, False))  18.3 us
    all_to_all x1, blocking collectives, on_device(): home = lax.all_to_all(homeward, ('parity', 'half'), 0, 0, tiled=True)  14.1 us
    all_to_all x1, waiting for transfers between devices, exchange(): return lax.all_to_all(sent, 'member', 0, 0, tiled=True)  14 us
    ppermute x3, waiting for transfers between devices, on_device(): env = lax.ppermute(env, 'pair', [(now, now + 1)])  13.5 us
    ppermute x3, waiting for transfers between devices, first_ring(): lax.ppermute(chip, bond, shifts(side, k, True))  10.4 us
    ppermute x4, starting transfers between devices, swap_cores(): return [lax.ppermute(p, ('half', 'member'), twins(side)) for p in pieces]  8.65 us
    pallas_call x2, Pallas kernels, on_device(): pl.pallas_call(functools.partial(middle_kernel, now), in_specs=[VMEM] * 7...  6.99 us
  transfers between devices with their start and end apart: 19, of which 8 were waited for; matrix products, arithmetic and copies ran while one was open for 1% of the time, Pallas kernels for 7%

profile of v4, /device:TPU:192, one launch (start us, length us, event | category | flops | bytes accessed | tf_op | source)
XLA Modules:
  0.0 263.2 jit_solution(18145071616860883344)
XLA Ops:
  7.2 0.0 all-gather.3.cloned.1.call-start
  7.2 1.0 copy.13
  8.2 1.1 collective-permute-start.1
  9.3 0.8 dynamic-slice_bitcast_fusion
  10.2 3.2 %collective-permute-start = (bf16[32,1024]{1,0:T(8,128)(2,1)S(1)}, bf16[32,1024]{1,0:T(8,128)(2,1)S(1)}, u32[]{:S(2)}, u32[]{:S(2)}) collective-permute-start(bf16[32,1024]{1,0:T(8,128)(2,1)S(1)} %dynamic-slice_bitcast_fusion), channel_id=1, source_target_pairs={{0,16},{16,0},{1,17},{17,1},{2,18},{18,2},{3,19},{19,3},{4,20},{20... | collective-permute-start | bytes 196616 | tf_op jit(solution)/shard_map/ppermute | solution.py:448
  13.4 0.8 copy.11.operators_ref
  14.2 0.1 stack.70.where_ref
  14.3 0.7 copy-done.2
  15.0 0.7 copy-done.3
  15.6 0.7 copy-done.4
  16.3 1.5 shard_map.77
  17.8 0.7 broadcast_select_fusion
  18.6 0.0 all-gather.3.cloned.1.call-update
  18.6 0.0 copy-start.1
  18.6 0.9 copy-done.1
  19.6 0.7 shard_map.78
  20.2 0.1 collective-permute-start.2
  20.3 1.3 collective-permute-done.2
  21.7 2.8 %collective-permute-start.5 = (bf16[2,4,32,512]{3,2,1,0:T(8,128)(2,1)S(1)}, bf16[2,4,32,512]{3,2,1,0:T(8,128)(2,1)S(1)}, u32[]{:S(2)}, u32[]{:S(2)}) collective-permute-start(bf16[2,4,32,512]{3,2,1,0:T(8,128)(2,1)S(1)} %maximum_select_fusion.1), channel_id=1, source_target_pairs={{0,6},{1,25},{2,0},{3,27},{4,2},{5,29},{6,4},{7,31},{8,14},{9,1},{... | collective-permute-start | bytes 786440 | tf_op jit(solution)/shard_map/ppermute | solution.py:409
  24.5 0.8 collective-permute-start.4
  25.3 0.9 collective-permute-start.3
  26.3 5.0 %collective-permute-done.5 = bf16[2,4,32,512]{3,2,1,0:T(8,128)(2,1)S(1)} collective-permute-done((bf16[2,4,32,512]{3,2,1,0:T(8,128)(2,1)S(1)}, bf16[2,4,32,512]{3,2,1,0:T(8,128)(2,1)S(1)}, u32[]{:S(2)}, u32[]{:S(2)}) %collective-permute-start.5) | collective-permute-done | bytes 262176 | tf_op jit(solution)/shard_map/ppermute | solution.py:409
  31.3 1.2 collective-permute-done.4
  32.5 4.1 %collective-permute-done.3 = bf16[2,4,32,512]{3,2,1,0:T(8,128)(2,1)S(1)} collective-permute-done((bf16[2,4,32,512]{3,2,1,0:T(8,128)(2,1)S(1)}, bf16[2,4,32,512]{3,2,1,0:T(8,128)(2,1)S(1)}, u32[]{:S(2)}, u32[]{:S(2)}) %collective-permute-start.3) | collective-permute-done | bytes 262176 | tf_op jit(solution)/shard_map/ppermute | solution.py:409
  36.6 0.1 pad_maximum_fusion.refs_0_
  36.8 0.2 collective-permute-start.9
  37.0 1.2 collective-permute-start.8
  38.2 0.7 collective-permute-start.7
  38.9 14.0 %collective-permute-done.9.refs_3_ = bf16[4,2,4,32,512]{4,3,2,1,0:T(8,128)(2,1)S(1)} collective-permute-done((bf16[4,2,4,32,512]{4,3,2,1,0:T(8,128)(2,1)S(1)}, bf16[4,2,4,32,512]{4,3,2,1,0:T(8,128)(2,1)S(1)}, u32[]{:S(2)}, u32[]{:S(2)}) %collective-permute-start.9) | collective-permute-done | bytes 1048608 | tf_op jit(solution)/shard_map/ppermute | solution.py:414
  52.9 8.6 %collective-permute-start.13 = (bf16[4,2,4,32,512]{4,3,2,1,0:T(8,128)(2,1)S(1)}, bf16[4,2,4,32,512]{4,3,2,1,0:T(8,128)(2,1)}, u32[]{:S(2)}, u32[]{:S(2)}) collective-permute-start(bf16[4,2,4,32,512]{4,3,2,1,0:T(8,128)(2,1)S(1)} %collective-permute-done.9.refs_3_), channel_id=1, source_target_pairs={{0,1},{1,0},{2,3},{3,2},{4,5},{5,4},{6,7},{7,6},{8,9},{9,8},{10,11... | collective-permute-start | bytes 3145736 | tf_op jit(solution)/shard_map/ppermute | solution.py:418
  61.5 0.1 collective-permute-start.12
  61.5 4.3 %collective-permute-done.7.refs_1_ = bf16[4,2,4,32,512]{4,3,2,1,0:T(8,128)(2,1)} collective-permute-done((bf16[4,2,4,32,512]{4,3,2,1,0:T(8,128)(2,1)S(1)}, bf16[4,2,4,32,512]{4,3,2,1,0:T(8,128)(2,1)}, u32[]{:S(2)}, u32[]{:S(2)}) %collective-permute-start.7) | collective-permute-done | bytes 1048608 | tf_op jit(solution)/shard_map/ppermute | solution.py:414
  65.9 4.8 %shard_map.79 = (bf16[16,32,512]{2,1,0:T(8,128)(2,1)}, f32[2,8,128]{2,1,0:T(8,128)S(1)}) custom-call(s32[8]{0:T(128)S(1)} %stack.70.where_ref, f32[2,4,4]{2,1,0:T(4,128)S(1)} %get-tuple-element.70.mix_ref, f32[2,4,4]{2,1,0:T(4,128)S(1)} %get-tuple-element.69.look_ref, bf16[64,1024]{1,0:T(8,128)(2,1)S(1)} %get-tuple-element.74.env_ref, ...), custom_call_target="tpu_custom_call" | custom-call | tf_op jit(solution)/shard_map/pallas_call | solution.py:492
  70.7 3.8 %all-to-all-start = ((bf16[16,32,512]{2,1,0:T(8,128)(2,1)}), bf16[16,32,512]{2,1,0:T(8,128)(2,1)S(1)}, u32[]{:S(2)}, u32[]{:S(2)}) async-start(bf16[16,32,512]{2,1,0:T(8,128)(2,1)} %get-tuple-element.79), calls=%async_computation | async-start | bytes 1048576 | tf_op jit(solution)/shard_map/all_to_all | solution.py:490
  74.4 14.0 %all-to-all-done.moved_ref = bf16[16,32,512]{2,1,0:T(8,128)(2,1)S(1)} async-done(((bf16[16,32,512]{2,1,0:T(8,128)(2,1)}), bf16[16,32,512]{2,1,0:T(8,128)(2,1)S(1)}, u32[]{:S(2)}, u32[]{:S(2)}) %all-to-all-start) | async-done | bytes 524320 | tf_op jit(solution)/shard_map/all_to_all | solution.py:490
  88.4 5.2 %shard_map.80.env_ref.refs_0_ = bf16[64,1024]{1,0:T(8,128)(2,1)S(1)} custom-call(s32[8]{0:T(128)S(1)} %stack.70.where_ref, bf16[16,32,512]{2,1,0:T(8,128)(2,1)S(1)} %all-to-all-done.moved_ref, bf16[4,2,4,32,512]{4,3,2,1,0:T(8,128)(2,1)} %copy-done.5, bf16[4,2,4,32,512]{4,3,2,1,0:T(8,128)(2,1)} %collective-permute-done.7.refs_1_, ...), custom_call_target="tpu_custom_call" | custom-call | tf_op jit(solution)/shard_map/pallas_call | solution.py:507
  93.7 0.0 all-gather.3.cloned.1.call-done
  93.7 5.3 %shard_map.81 = (bf16[16,64,256]{2,1,0:T(8,128)(2,1)S(1)}, f32[2,8,128]{2,1,0:T(8,128)S(1)}) custom-call(s32[8]{0:T(128)S(1)} %stack.70.where_ref, f32[2,4,4]{2,1,0:T(4,128)S(1)} %get-tuple-element.70.mix_ref, f32[2,4,4]{2,1,0:T(4,128)S(1)} %get-tuple-element.69.look_ref, bf16[64,1024]{1,0:T(8,128)(2,1)S(1)} %shard_map.80.env_ref.refs_0_, ...), custom_call_target="tpu_custom_call" | custom-call | tf_op jit(solution)/shard_map/pallas_call | solution.py:517
  99.0 15.8 %all_to_all.45.moved_ref = bf16[16,64,256]{2,1,0:T(8,128)(2,1)S(1)} all-to-all(bf16[16,64,256]{2,1,0:T(8,128)(2,1)S(1)} %get-tuple-element.83), channel_id=1, replica_groups=mesh['pair'=4,'parity'=2,'half'=2,'member'=16] {'member'}, dimensions={0} | all-to-all | bytes 1048576 | tf_op jit(solution)/shard_map/all_to_all | solution.py:490
  114.8 1.6 shard_map.82.refs_3_
  116.4 0.7 collective-permute-start.14
  117.1 4.2 %shard_map.83.refs_0_.tensor_ref.old_ref = bf16[16,2,2,4,32,512]{5,4,3,2,1,0:T(8,128)(2,1)S(1)} custom-call(s32[8]{0:T(128)S(1)} %stack.70.where_ref, bf16[4,2,4,32,512]{4,3,2,1,0:T(8,128)(2,1)} %copy-done.5, bf16[4,2,4,32,512]{4,3,2,1,0:T(8,128)(2,1)} %collective-permute-done.7.refs_1_, bf16[4,2,4,32,512]{4,3,2,1,0:T(8,128)(2,1)} %collective-permute-done.8.refs_2_, ...), custom_call_target="tpu_custom_call" | custom-call | tf_op jit(solution)/shard_map/pallas_call | solution.py:550
  121.4 1.2 shard_map.84.bank_ref
  122.6 1.8 shard_map.85
  124.4 13.5 %all_to_all.46.moved_ref = bf16[16,64,256]{2,1,0:T(8,128)(2,1)S(1)} all-to-all(bf16[16,64,256]{2,1,0:T(8,128)(2,1)S(1)} %get-tuple-element.94), channel_id=1, replica_groups=mesh['pair'=4,'parity'=2,'half'=2,'member'=16] {'member'}, dimensions={0} | all-to-all | bytes 1048576 | tf_op jit(solution)/shard_map/all_to_all | solution.py:490
  137.9 3.5 %shard_map.86 = (bf16[16,64,256]{2,1,0:T(8,128)(2,1)S(1)}, f32[2,8,128]{2,1,0:T(8,128)S(1)}, bf16[64,1024]{1,0:T(8,128)(2,1)S(1)}) custom-call(s32[8,128]{1,0:T(8,128)S(1)} %get-tuple-element.66.pair_ref, f32[32,256]{1,0:T(8,128)S(1)} %get-tuple-element.67.mix_ref, f32[2,4,64,1024]{3,2,1,0:T(8,128)S(1)} %shard_map.84.bank_ref, ...), custom_call_target="tpu_custom_call" | custom-call | tf_op jit(solution)/shard_map/pallas_call | solution.py:532
  141.4 13.5 %all_to_all.47.moved_ref = bf16[16,64,256]{2,1,0:T(8,128)(2,1)S(1)} all-to-all(bf16[16,64,256]{2,1,0:T(8,128)(2,1)S(1)} %get-tuple-element.96), channel_id=1, replica_groups=mesh['pair'=4,'parity'=2,'half'=2,'member'=16] {'member'}, dimensions={0} | all-to-all | bytes 1048576 | tf_op jit(solution)/shard_map/all_to_all | solution.py:490
  154.8 1.6 shard_map.87.refs_4_
  156.4 0.9 collective-permute-start.15
  157.3 1.8 shard_map.88
  159.1 13.5 %all_to_all.48.moved_ref = bf16[16,64,256]{2,1,0:T(8,128)(2,1)S(1)} all-to-all(bf16[16,64,256]{2,1,0:T(8,128)(2,1)S(1)} %get-tuple-element.98), channel_id=1, replica_groups=mesh['pair'=4,'parity'=2,'half'=2,'member'=16] {'member'}, dimensions={0} | all-to-all | bytes 1048576 | tf_op jit(solution)/shard_map/all_to_all | solution.py:490
  172.6 3.5 %shard_map.89 = (bf16[16,64,256]{2,1,0:T(8,128)(2,1)S(1)}, f32[2,8,128]{2,1,0:T(8,128)S(1)}, bf16[64,1024]{1,0:T(8,128)(2,1)S(1)}) custom-call(s32[8,128]{1,0:T(8,128)S(1)} %get-tuple-element.66.pair_ref, f32[32,256]{1,0:T(8,128)S(1)} %get-tuple-element.67.mix_ref, f32[2,4,64,1024]{3,2,1,0:T(8,128)S(1)} %shard_map.84.bank_ref, ...), custom_call_target="tpu_custom_call" | custom-call | tf_op jit(solution)/shard_map/pallas_call | solution.py:532
  176.1 13.5 %all_to_all.49.moved_ref = bf16[16,64,256]{2,1,0:T(8,128)(2,1)S(1)} all-to-all(bf16[16,64,256]{2,1,0:T(8,128)(2,1)S(1)} %get-tuple-element.100), channel_id=1, replica_groups=mesh['pair'=4,'parity'=2,'half'=2,'member'=16] {'member'}, dimensions={0} | all-to-all | bytes 1048576 | tf_op jit(solution)/shard_map/all_to_all | solution.py:490
  189.6 1.6 shard_map.90.refs_5_
  191.2 1.3 collective-permute-start.16
  192.5 0.1 shard_map.91
  192.6 13.5 %collective-permute-done.16.env_ref = bf16[64,1024]{1,0:T(8,128)(2,1)S(1)} collective-permute-done((bf16[64,1024]{1,0:T(8,128)(2,1)S(1)}, bf16[64,1024]{1,0:T(8,128)(2,1)S(1)}, u32[]{:S(2)}, u32[]{:S(2)}) %collective-permute-start.16) | collective-permute-done | bytes 131104 | tf_op jit(solution)/shard_map/ppermute | solution.py:576
  206.1 1.8 shard_map.92
  207.9 13.9 %all_to_all.50.moved_ref = bf16[16,64,256]{2,1,0:T(8,128)(2,1)S(1)} all-to-all(bf16[16,64,256]{2,1,0:T(8,128)(2,1)S(1)} %get-tuple-element.114), channel_id=1, replica_groups=mesh['pair'=4,'parity'=2,'half'=2,'member'=16] {'member'}, dimensions={0} | all-to-all | bytes 1048576 | tf_op jit(solution)/shard_map/all_to_all | solution.py:490
  221.8 3.5 %shard_map.93 = (bf16[16,80,256]{2,1,0:T(8,128)(2,1)S(1)}, bf16[64,1024]{1,0:T(8,128)(2,1)S(1)}) custom-call(s32[8,128]{1,0:T(8,128)S(1)} %get-tuple-element.66.pair_ref, f32[32,256]{1,0:T(8,128)S(1)} %get-tuple-element.67.mix_ref, f32[2,4,64,1024]{3,2,1,0:T(8,128)S(1)} %shard_map.84.bank_ref, bf16[16,64,256]{2,1,0:T(8,128)(2,1)S(1)} %all_to_all.50.moved_ref, ...), custom_call_target="tpu_custom_call" | custom-call | tf_op jit(solution)/shard_map/pallas_call | solution.py:587
  225.3 14.6 %all_to_all.51.moved_ref = bf16[16,80,256]{2,1,0:T(8,128)(2,1)S(1)} all-to-all(bf16[16,80,256]{2,1,0:T(8,128)(2,1)S(1)} %get-tuple-element.116), channel_id=1, replica_groups=mesh['pair'=4,'parity'=2,'half'=2,'member'=16] {'member'}, dimensions={0} | all-to-all | bytes 1310720 | tf_op jit(solution)/shard_map/all_to_all | solution.py:490
  239.9 1.6 shard_map.94
  241.5 14.1 %all_to_all.52.home_ref = bf16[4,32,1152]{2,1,0:T(8,128)(2,1)S(1)} all-to-all(bf16[4,32,1152]{2,1,0:T(8,128)(2,1)S(1)} %shard_map.94), channel_id=1, replica_groups=mesh['pair'=4,'parity'=2,'half'=2,'member'=16] {'parity','half'}, dimensions={0} | all-to-all | bytes 589824 | tf_op jit(solution)/shard_map/all_to_all | solution.py:602
  255.6 0.7 shard_map.95
  (24 shorter events, 0.1 us)
Async XLA Ops:
  7.2 86.6 %all-gather.3.cloned.1.call-start = ((), (), s32[]{:S(2)}) async-start(), calls=%async_computation.9 | async-start | bytes 8650752 | tf_op jit(solution)/shard_map/all_gather | solution.py:469
  8.2 9.6 %collective-permute-start.1 = (bf16[4,32,1024]{2,1,0:T(8,128)(2,1)S(1)}, bf16[4,32,1024]{2,1,0:T(8,128)(2,1)S(1)}, u32[]{:S(2)}, u32[]{:S(2)}) collective-permute-start(bf16[4,32,1024]{2,1,0:T(8,128)(2,1)S(1)} %bitcast.33), channel_id=1, source_target_pairs={{0,32},{32,0},{1,33},{33,1},{2,34},{34,2},{3,35},{35,3},{4,36},{36... | collective-permute-start | bytes 786440 | tf_op jit(solution)/shard_map/ppermute | solution.py:446
  10.2 7.6 %collective-permute-start = (bf16[32,1024]{1,0:T(8,128)(2,1)S(1)}, bf16[32,1024]{1,0:T(8,128)(2,1)S(1)}, u32[]{:S(2)}, u32[]{:S(2)}) collective-permute-start(bf16[32,1024]{1,0:T(8,128)(2,1)S(1)} %dynamic-slice_bitcast_fusion), channel_id=1, source_target_pairs={{0,16},{16,0},{1,17},{17,1},{2,18},{18,2},{3,19},{19,3},{4,20},{20... | collective-permute-start | bytes 196616 | tf_op jit(solution)/shard_map/ppermute | solution.py:448
  14.3 0.7 copy-start.2
  15.0 0.7 copy-start.3
  15.6 0.7 copy-start.4
  18.6 1.0 copy-start.1
  20.2 1.4 collective-permute-start.2
  21.7 9.6 %collective-permute-start.5 = (bf16[2,4,32,512]{3,2,1,0:T(8,128)(2,1)S(1)}, bf16[2,4,32,512]{3,2,1,0:T(8,128)(2,1)S(1)}, u32[]{:S(2)}, u32[]{:S(2)}) collective-permute-start(bf16[2,4,32,512]{3,2,1,0:T(8,128)(2,1)S(1)} %maximum_select_fusion.1), channel_id=1, source_target_pairs={{0,6},{1,25},{2,0},{3,27},{4,2},{5,29},{6,4},{7,31},{8,14},{9,1},{... | collective-permute-start | bytes 786440 | tf_op jit(solution)/shard_map/ppermute | solution.py:409
  24.5 8.0 %collective-permute-start.4 = (bf16[2,4,32,512]{3,2,1,0:T(8,128)(2,1)S(1)}, bf16[2,4,32,512]{3,2,1,0:T(8,128)(2,1)S(1)}, u32[]{:S(2)}, u32[]{:S(2)}) collective-permute-start(bf16[2,4,32,512]{3,2,1,0:T(8,128)(2,1)S(1)} %maximum_select_fusion.1), channel_id=1, source_target_pairs={{0,4},{1,17},{2,6},{3,19},{4,0},{5,21},{6,2},{7,23},{8,12},{9,25},... | collective-permute-start | bytes 786440 | tf_op jit(solution)/shard_map/ppermute | solution.py:409
  25.3 11.3 %collective-permute-start.3 = (bf16[2,4,32,512]{3,2,1,0:T(8,128)(2,1)S(1)}, bf16[2,4,32,512]{3,2,1,0:T(8,128)(2,1)S(1)}, u32[]{:S(2)}, u32[]{:S(2)}) collective-permute-start(bf16[2,4,32,512]{3,2,1,0:T(8,128)(2,1)S(1)} %maximum_select_fusion.1), channel_id=1, source_target_pairs={{0,2},{1,9},{2,4},{3,11},{4,6},{5,13},{6,0},{7,15},{8,10},{9,17},{... | collective-permute-start | bytes 786440 | tf_op jit(solution)/shard_map/ppermute | solution.py:409
  26.2 10.6 %collective-permute-start.6 = (bf16[64,1024]{1,0:T(8,128)(2,1)S(1)}, bf16[64,1024]{1,0:T(8,128)(2,1)S(1)}, u32[]{:S(2)}, u32[]{:S(2)}) collective-permute-start(bf16[64,1024]{1,0:T(8,128)(2,1)S(1)} %get-tuple-element.74.env_ref), channel_id=1, source_target_pairs={{0,1},{1,0},{2,3},{3,2},{4,5},{5,4},{6,7},{7,6},{8,9},{9,8},{10,11... | collective-permute-start | bytes 393224 | tf_op jit(solution)/shard_map/ppermute | solution.py:478
  36.8 29.1 %copy-start.5 = (bf16[4,2,4,32,512]{4,3,2,1,0:T(8,128)(2,1)}, bf16[4,2,4,32,512]{4,3,2,1,0:T(8,128)(2,1)S(1)}, u32[]{:S(2)}) copy-start(bf16[4,2,4,32,512]{4,3,2,1,0:T(8,128)(2,1)S(1)} %pad_maximum_fusion.refs_0_) | copy-start | bytes 3145732
  36.8 16.1 %collective-permute-start.9 = (bf16[4,2,4,32,512]{4,3,2,1,0:T(8,128)(2,1)S(1)}, bf16[4,2,4,32,512]{4,3,2,1,0:T(8,128)(2,1)S(1)}, u32[]{:S(2)}, u32[]{:S(2)}) collective-permute-start(bf16[4,2,4,32,512]{4,3,2,1,0:T(8,128)(2,1)S(1)} %pad_maximum_fusion.refs_0_), channel_id=1, source_target_pairs={{0,24},{1,7},{2,26},{3,1},{4,28},{5,3},{6,30},{7,5},{8,0},{9,15},{... | collective-permute-start | bytes 3145736 | tf_op jit(solution)/shard_map/ppermute | solution.py:414
  37.0 24.5 %collective-permute-start.8 = (bf16[4,2,4,32,512]{4,3,2,1,0:T(8,128)(2,1)S(1)}, bf16[4,2,4,32,512]{4,3,2,1,0:T(8,128)(2,1)}, u32[]{:S(2)}, u32[]{:S(2)}) collective-permute-start(bf16[4,2,4,32,512]{4,3,2,1,0:T(8,128)(2,1)S(1)} %pad_maximum_fusion.refs_0_), channel_id=1, source_target_pairs={{0,16},{1,5},{2,18},{3,7},{4,20},{5,1},{6,22},{7,3},{8,24},{9,13},... | collective-permute-start | bytes 3145736 | tf_op jit(solution)/shard_map/ppermute | solution.py:414
  38.2 27.7 %collective-permute-start.7 = (bf16[4,2,4,32,512]{4,3,2,1,0:T(8,128)(2,1)S(1)}, bf16[4,2,4,32,512]{4,3,2,1,0:T(8,128)(2,1)}, u32[]{:S(2)}, u32[]{:S(2)}) collective-permute-start(bf16[4,2,4,32,512]{4,3,2,1,0:T(8,128)(2,1)S(1)} %pad_maximum_fusion.refs_0_), channel_id=1, source_target_pairs={{0,8},{1,3},{2,10},{3,5},{4,12},{5,7},{6,14},{7,1},{8,16},{9,11},{... | collective-permute-start | bytes 3145736 | tf_op jit(solution)/shard_map/ppermute | solution.py:414
  38.9 35.5 %collective-permute-start.10 = (bf16[4,2,4,32,512]{4,3,2,1,0:T(8,128)(2,1)S(1)}, bf16[4,2,4,32,512]{4,3,2,1,0:T(8,128)(2,1)}, u32[]{:S(2)}, u32[]{:S(2)}) collective-permute-start(bf16[4,2,4,32,512]{4,3,2,1,0:T(8,128)(2,1)S(1)} %pad_maximum_fusion.refs_0_), channel_id=1, source_target_pairs={{0,1},{1,0},{2,3},{3,2},{4,5},{5,4},{6,7},{7,6},{8,9},{9,8},{10,11... | collective-permute-start | bytes 3145736 | tf_op jit(solution)/shard_map/ppermute | solution.py:418
  52.9 13.0 %copy-start.6 = (bf16[4,2,4,32,512]{4,3,2,1,0:T(8,128)(2,1)}, bf16[4,2,4,32,512]{4,3,2,1,0:T(8,128)(2,1)S(1)}, u32[]{:S(2)}) copy-start(bf16[4,2,4,32,512]{4,3,2,1,0:T(8,128)(2,1)S(1)} %collective-permute-done.9.refs_3_) | copy-start | bytes 3145732
  52.9 35.5 %collective-permute-start.13 = (bf16[4,2,4,32,512]{4,3,2,1,0:T(8,128)(2,1)S(1)}, bf16[4,2,4,32,512]{4,3,2,1,0:T(8,128)(2,1)}, u32[]{:S(2)}, u32[]{:S(2)}) collective-permute-start(bf16[4,2,4,32,512]{4,3,2,1,0:T(8,128)(2,1)S(1)} %collective-permute-done.9.refs_3_), channel_id=1, source_target_pairs={{0,1},{1,0},{2,3},{3,2},{4,5},{5,4},{6,7},{7,6},{8,9},{9,8},{10,11... | collective-permute-start | bytes 3145736 | tf_op jit(solution)/shard_map/ppermute | solution.py:418
  61.5 27.0 %collective-permute-start.12 = (bf16[4,2,4,32,512]{4,3,2,1,0:T(8,128)(2,1)}, bf16[4,2,4,32,512]{4,3,2,1,0:T(8,128)(2,1)}, u32[]{:S(2)}, u32[]{:S(2)}) collective-permute-start(bf16[4,2,4,32,512]{4,3,2,1,0:T(8,128)(2,1)} %collective-permute-done.8.refs_2_), channel_id=1, source_target_pairs={{0,1},{1,0},{2,3},{3,2},{4,5},{5,4},{6,7},{7,6},{8,9},{9,8},{10,11... | collective-permute-start | bytes 3145736 | tf_op jit(solution)/shard_map/ppermute | solution.py:418
  65.9 22.6 %collective-permute-start.11 = (bf16[4,2,4,32,512]{4,3,2,1,0:T(8,128)(2,1)}, bf16[4,2,4,32,512]{4,3,2,1,0:T(8,128)(2,1)}, u32[]{:S(2)}, u32[]{:S(2)}) collective-permute-start(bf16[4,2,4,32,512]{4,3,2,1,0:T(8,128)(2,1)} %collective-permute-done.7.refs_1_), channel_id=1, source_target_pairs={{0,1},{1,0},{2,3},{3,2},{4,5},{5,4},{6,7},{7,6},{8,9},{9,8},{10,11... | collective-permute-start | bytes 3145736 | tf_op jit(solution)/shard_map/ppermute | solution.py:418
  70.7 17.8 %all-to-all-start = ((bf16[16,32,512]{2,1,0:T(8,128)(2,1)}), bf16[16,32,512]{2,1,0:T(8,128)(2,1)S(1)}, u32[]{:S(2)}, u32[]{:S(2)}) async-start(bf16[16,32,512]{2,1,0:T(8,128)(2,1)} %get-tuple-element.79), calls=%async_computation | async-start | bytes 1048576 | tf_op jit(solution)/shard_map/all_to_all | solution.py:490
  93.7 21.1 %copy-start = (bf16[128,32,1024]{2,1,0:T(8,128)(2,1)S(1)}, bf16[128,32,1024]{2,1,0:T(8,128)(2,1)}, u32[]{:S(2)}) copy-start(bf16[128,32,1024]{2,1,0:T(8,128)(2,1)} %all-gather.3.cloned.1.call-done) | copy-start | bytes 25165828
  116.4 6.1 %collective-permute-start.14 = (bf16[64,1024]{1,0:T(8,128)(2,1)S(1)}, bf16[64,1024]{1,0:T(8,128)(2,1)S(1)}, u32[]{:S(2)}, u32[]{:S(2)}) collective-permute-start(bf16[64,1024]{1,0:T(8,128)(2,1)S(1)} %shard_map.82.refs_3_), channel_id=1, source_target_pairs={{0,64},{1,65},{2,66},{3,67},{4,68},{5,69},{6,70},{7,71},{8,72},{9,... | collective-permute-start | bytes 393224 | tf_op jit(solution)/shard_map/ppermute | solution.py:576
  156.4 0.9 collective-permute-start.15
  191.2 14.9 %collective-permute-start.16 = (bf16[64,1024]{1,0:T(8,128)(2,1)S(1)}, bf16[64,1024]{1,0:T(8,128)(2,1)S(1)}, u32[]{:S(2)}, u32[]{:S(2)}) collective-permute-start(bf16[64,1024]{1,0:T(8,128)(2,1)S(1)} %shard_map.90.refs_5_), channel_id=1, source_target_pairs={{128,192},{129,193},{130,194},{131,195},{132,196},{133,197},{134,1... | collective-permute-start | bytes 393224 | tf_op jit(solution)/shard_map/ppermute | solution.py:576
Sparse Core Ops, SparseCore 0:
  18.7 74.9 all-gather.2

commit v5 on v4

--- a/solution.py
+++ b/solution.py
@@ -146,22 +146,45 @@
 
 
 def stream_kernel(
-    now, where_ref, mix_ref, look_ref, env_ref, tensor_ref, seen_ref, out_ref, new_ref, held, sems
+    now, where_ref, mix_ref, look_ref, env_ref, twin_ref, tensor_ref, seen_ref, out_ref, new_ref, held, sems
 ):
+    core = where_ref[4]
+    peers, phys, panel, wide = held.shape
     copies = []
-    for c in range(held.shape[3] // COLS):
-        cols = pl.ds(c * COLS, COLS)
+    for c in range(wide // COLS):
+        place = pl.ds(pl.multiple_of(core * wide + c * COLS, COLS), COLS)
         copies.append(
             pltpu.make_async_copy(
-                tensor_ref.at[:, :, :, cols], held.at[:, :, :, cols], sems.at[c]
+                tensor_ref.at[:, :, :, place], held.at[:, :, :, pl.ds(c * COLS, COLS)], sems.at[c]
             )
         )
         copies[-1].start()
-    arrived = [copy.wait for copy in copies]
-    total = spread(1, where_ref, mix_ref, look_ref, env_ref[...], held, out_ref, arrived)
+    own, twin = env_ref[...], twin_ref[...]
+    env = jnp.concatenate(
+        [jnp.where(core == 0, own, twin), jnp.where(core == 0, twin, own)], axis=0
+    )
+    even = where_ref[0] - core
+    total = jnp.zeros(new_ref.shape[1:], jnp.float32)
+    for c, copy in enumerate(copies):
+        copy.wait()
+        cols = slice(c * COLS, (c + 1) * COLS)
+        prods = [
+            jnp.dot(env, held[:, t, :, cols].reshape(-1, COLS), preferred_element_type=jnp.float32)
+            for t in range(phys)
+        ]
+        for s in range(phys):
+            rows = [held[h * (peers // 2) + even + o, s, :, cols] for o in range(2) for h in range(2)]
+            seen = jnp.concatenate(rows, axis=0).astype(jnp.float32)
+            seen = seen * sum(look_ref[1, s, t] * prods[t] for t in range(phys))
+            seen = jnp.sum(seen.reshape(-1, 8, COLS), axis=0)
+            total += sum(seen[:, b : b + 128] for b in range(0, COLS, 128))
+        mixed = [sum(mix_ref[1, s, t] * prods[t] for t in range(phys)) for s in range(phys)]
+        tall = [mixed[s][q * panel : (q + 1) * panel] for q in range(4) for s in range(phys)]
+        turned = jnp.concatenate(tall, axis=0).astype(jnp.bfloat16).T
+        per = COLS // panel
+        out_ref[c * per : (c + 1) * per] = turned.reshape(per, panel, 4 * phys * panel)
     new_ref[0] = seen_ref[0]
-    first_row = lax.broadcasted_iota(jnp.int32, new_ref.shape[1:], 0) == 0
-    new_ref[1] = jnp.where(first_row, jnp.broadcast_to(total, new_ref.shape[1:]), 0.0)
+    new_ref[1] = total
 
 
 def load(side, where_ref, pieces, tensor_ref, sems):
@@ -513,18 +536,19 @@
         compiler_params=params(),
     )(where, moved, *in_hbm(everything))
     evens, odds = [env], []
-    env, after = lax.optimization_barrier((env, after))
+    twin = lax.ppermute(env, bond, twins(side))
+    env, twin, after = lax.optimization_barrier((env, twin, after))
     sent, seen = pl.pallas_call(
         functools.partial(stream_kernel, 0),
-        in_specs=[SMEM] * 3 + [VMEM, HBM, VMEM],
+        in_specs=[SMEM] * 3 + [VMEM] * 2 + [HBM, VMEM],
         out_specs=[VMEM] * 2,
-        out_shape=[sent_shape(0), seen_shape],
+        out_shape=[jax.ShapeDtypeStruct((members, panel, 2 * lanes), bf16), seen_shape],
         scratch_shapes=[
-            pltpu.VMEM(after.shape, bf16),
-            pltpu.SemaphoreType.DMA((width // COLS,)),
+            pltpu.VMEM(after.shape[:3] + (width // 2,), bf16),
+            pltpu.SemaphoreType.DMA((width // 2 // COLS,)),
         ],
         compiler_params=params(),
-    )(*small, env, *in_hbm([after]), seen)
+    )(*small, env, twin, *in_hbm([after]), seen)
     after = pltpu.with_memory_space_constraint(after, pltpu.VMEM)
     before = None
     for now in range(pairs - 1):

time: 264 us -> 264 us (level)
  transfers between devices with their start and end apart: 19 -> 20, of which waited for: 8 -> 9; matrix products, arithmetic and copies ran while one was open for 1% -> 1% of each run, Pallas kernels for 7% -> 7%
where the time goes in v5:
time: 264 us; the launch traced here: 263 us
  blocking collectives  112 us (42%)
  waiting for transfers between devices  58.7 us (22%)
  Pallas kernels  44.7 us (17%)
  starting transfers between devices  26.6 us (10%)
  between operations  14.3 us (5%)
  local copies, waits for them, and re-layouts  5.71 us (2%)
    all_to_all x7, blocking collectives, exchange(): return lax.all_to_all(sent, 'member', 0, 0, tiled=True)  98.3 us
    ppermute x3, waiting for transfers between devices, second_ring(): lax.ppermute(row, bond, shifts(side, m, False))  18.3 us
    all_to_all x1, waiting for transfers between devices, exchange(): return lax.all_to_all(sent, 'member', 0, 0, tiled=True)  14 us
    all_to_all x1, blocking collectives, on_device(): home = lax.all_to_all(homeward, ('parity', 'half'), 0, 0, tiled=True)  13.7 us
    ppermute x3, waiting for transfers between devices, on_device(): env = lax.ppermute(env, 'pair', [(now, now + 1)])  13.5 us
    ppermute x3, waiting for transfers between devices, first_ring(): lax.ppermute(chip, bond, shifts(side, k, True))  10.4 us
    ppermute x4, starting transfers between devices, swap_cores(): return [lax.ppermute(p, ('half', 'member'), twins(side)) for p in pieces]  8.65 us
    pallas_call x2, Pallas kernels, on_device(): pl.pallas_call(functools.partial(middle_kernel, now), in_specs=[VMEM] * 7...  6.99 us
  transfers between devices with their start and end apart: 20, of which 9 were waited for; matrix products, arithmetic and copies ran while one was open for 1% of the time, Pallas kernels for 7%

profile of v5, /device:TPU:192, one launch (start us, length us, event | category | flops | bytes accessed | tf_op | source)
XLA Modules:
  0.0 262.9 jit_solution(12449913910397626897)
XLA Ops:
  7.2 0.0 all-gather.3.cloned.1.call-start
  7.2 1.0 copy.13
  8.2 1.1 collective-permute-start.1
  9.3 0.8 dynamic-slice_bitcast_fusion
  10.2 3.2 %collective-permute-start = (bf16[32,1024]{1,0:T(8,128)(2,1)S(1)}, bf16[32,1024]{1,0:T(8,128)(2,1)S(1)}, u32[]{:S(2)}, u32[]{:S(2)}) collective-permute-start(bf16[32,1024]{1,0:T(8,128)(2,1)S(1)} %dynamic-slice_bitcast_fusion), channel_id=1, source_target_pairs={{0,16},{16,0},{1,17},{17,1},{2,18},{18,2},{3,19},{19,3},{4,20},{20... | collective-permute-start | bytes 196616 | tf_op jit(solution)/shard_map/ppermute | solution.py:471
  13.4 0.8 copy.11.operators_ref
  14.2 0.1 stack.70.where_ref
  14.3 0.7 copy-done.2
  15.0 0.7 copy-done.3
  15.6 0.7 copy-done.4
  16.3 1.5 shard_map.77
  17.8 0.7 broadcast_select_fusion
  18.6 0.0 all-gather.3.cloned.1.call-update
  18.6 0.9 copy-done.1
  19.6 0.7 shard_map.78
  20.2 0.1 collective-permute-start.2
  20.3 1.3 collective-permute-done.2
  21.7 2.8 %collective-permute-start.5 = (bf16[2,4,32,512]{3,2,1,0:T(8,128)(2,1)S(1)}, bf16[2,4,32,512]{3,2,1,0:T(8,128)(2,1)S(1)}, u32[]{:S(2)}, u32[]{:S(2)}) collective-permute-start(bf16[2,4,32,512]{3,2,1,0:T(8,128)(2,1)S(1)} %maximum_select_fusion.1), channel_id=1, source_target_pairs={{0,6},{1,25},{2,0},{3,27},{4,2},{5,29},{6,4},{7,31},{8,14},{9,1},{... | collective-permute-start | bytes 786440 | tf_op jit(solution)/shard_map/ppermute | solution.py:432
  24.5 0.8 collective-permute-start.4
  25.3 0.9 collective-permute-start.3
  26.3 5.0 %collective-permute-done.5 = bf16[2,4,32,512]{3,2,1,0:T(8,128)(2,1)S(1)} collective-permute-done((bf16[2,4,32,512]{3,2,1,0:T(8,128)(2,1)S(1)}, bf16[2,4,32,512]{3,2,1,0:T(8,128)(2,1)S(1)}, u32[]{:S(2)}, u32[]{:S(2)}) %collective-permute-start.5) | collective-permute-done | bytes 262176 | tf_op jit(solution)/shard_map/ppermute | solution.py:432
  31.3 1.2 collective-permute-done.4
  32.5 4.1 %collective-permute-done.3 = bf16[2,4,32,512]{3,2,1,0:T(8,128)(2,1)S(1)} collective-permute-done((bf16[2,4,32,512]{3,2,1,0:T(8,128)(2,1)S(1)}, bf16[2,4,32,512]{3,2,1,0:T(8,128)(2,1)S(1)}, u32[]{:S(2)}, u32[]{:S(2)}) %collective-permute-start.3) | collective-permute-done | bytes 262176 | tf_op jit(solution)/shard_map/ppermute | solution.py:432
  36.6 0.1 pad_maximum_fusion.refs_0_
  36.8 0.2 collective-permute-start.9
  37.0 1.2 collective-permute-start.8
  38.2 0.7 collective-permute-start.7
  38.9 14.0 %collective-permute-done.9.refs_3_ = bf16[4,2,4,32,512]{4,3,2,1,0:T(8,128)(2,1)S(1)} collective-permute-done((bf16[4,2,4,32,512]{4,3,2,1,0:T(8,128)(2,1)S(1)}, bf16[4,2,4,32,512]{4,3,2,1,0:T(8,128)(2,1)S(1)}, u32[]{:S(2)}, u32[]{:S(2)}) %collective-permute-start.9) | collective-permute-done | bytes 1048608 | tf_op jit(solution)/shard_map/ppermute | solution.py:437
  52.9 8.6 %collective-permute-start.13 = (bf16[4,2,4,32,512]{4,3,2,1,0:T(8,128)(2,1)S(1)}, bf16[4,2,4,32,512]{4,3,2,1,0:T(8,128)(2,1)}, u32[]{:S(2)}, u32[]{:S(2)}) collective-permute-start(bf16[4,2,4,32,512]{4,3,2,1,0:T(8,128)(2,1)S(1)} %collective-permute-done.9.refs_3_), channel_id=1, source_target_pairs={{0,1},{1,0},{2,3},{3,2},{4,5},{5,4},{6,7},{7,6},{8,9},{9,8},{10,11... | collective-permute-start | bytes 3145736 | tf_op jit(solution)/shard_map/ppermute | solution.py:441
  61.5 0.1 collective-permute-start.12
  61.5 4.3 %collective-permute-done.7.refs_1_ = bf16[4,2,4,32,512]{4,3,2,1,0:T(8,128)(2,1)} collective-permute-done((bf16[4,2,4,32,512]{4,3,2,1,0:T(8,128)(2,1)S(1)}, bf16[4,2,4,32,512]{4,3,2,1,0:T(8,128)(2,1)}, u32[]{:S(2)}, u32[]{:S(2)}) %collective-permute-start.7) | collective-permute-done | bytes 1048608 | tf_op jit(solution)/shard_map/ppermute | solution.py:437
  65.9 4.8 %shard_map.79 = (bf16[16,32,512]{2,1,0:T(8,128)(2,1)}, f32[2,8,128]{2,1,0:T(8,128)S(1)}) custom-call(s32[8]{0:T(128)S(1)} %stack.70.where_ref, f32[2,4,4]{2,1,0:T(4,128)S(1)} %get-tuple-element.71.mix_ref, f32[2,4,4]{2,1,0:T(4,128)S(1)} %get-tuple-element.70.look_ref, bf16[64,1024]{1,0:T(8,128)(2,1)S(1)} %get-tuple-element.75.env_ref, ...), custom_call_target="tpu_custom_call" | custom-call | tf_op jit(solution)/shard_map/pallas_call | solution.py:515
  70.6 3.8 %all-to-all-start = ((bf16[16,32,512]{2,1,0:T(8,128)(2,1)}), bf16[16,32,512]{2,1,0:T(8,128)(2,1)S(1)}, u32[]{:S(2)}, u32[]{:S(2)}) async-start(bf16[16,32,512]{2,1,0:T(8,128)(2,1)} %get-tuple-element.80), calls=%async_computation | async-start | bytes 1048576 | tf_op jit(solution)/shard_map/all_to_all | solution.py:513
  74.4 14.0 %all-to-all-done.moved_ref = bf16[16,32,512]{2,1,0:T(8,128)(2,1)S(1)} async-done(((bf16[16,32,512]{2,1,0:T(8,128)(2,1)}), bf16[16,32,512]{2,1,0:T(8,128)(2,1)S(1)}, u32[]{:S(2)}, u32[]{:S(2)}) %all-to-all-start) | async-done | bytes 524320 | tf_op jit(solution)/shard_map/all_to_all | solution.py:513
  88.4 5.3 %shard_map.80.env_ref.refs_0_ = bf16[64,1024]{1,0:T(8,128)(2,1)S(1)} custom-call(s32[8]{0:T(128)S(1)} %stack.70.where_ref, bf16[16,32,512]{2,1,0:T(8,128)(2,1)S(1)} %all-to-all-done.moved_ref, bf16[4,2,4,32,512]{4,3,2,1,0:T(8,128)(2,1)} %copy-done.5, bf16[4,2,4,32,512]{4,3,2,1,0:T(8,128)(2,1)} %collective-permute-done.7.refs_1_, ...), custom_call_target="tpu_custom_call" | custom-call | tf_op jit(solution)/shard_map/pallas_call | solution.py:530
  93.7 0.3 collective-permute-start.14
  94.0 1.1 collective-permute-done.14.twin_ref
  95.1 3.9 %shard_map.81 = (bf16[16,32,512]{2,1,0:T(8,128)(2,1)S(1)}, f32[2,8,128]{2,1,0:T(8,128)S(1)}) custom-call(s32[8]{0:T(128)S(1)} %stack.70.where_ref, f32[2,4,4]{2,1,0:T(4,128)S(1)} %get-tuple-element.71.mix_ref, f32[2,4,4]{2,1,0:T(4,128)S(1)} %get-tuple-element.70.look_ref, bf16[64,1024]{1,0:T(8,128)(2,1)S(1)} %shard_map.80.env_ref.refs_0_, ...), custom_call_target="tpu_custom_call" | custom-call | tf_op jit(solution)/shard_map/pallas_call | solution.py:541
  99.1 15.9 %all_to_all.45.moved_ref = bf16[16,32,512]{2,1,0:T(8,128)(2,1)S(1)} all-to-all(bf16[16,32,512]{2,1,0:T(8,128)(2,1)S(1)} %get-tuple-element.85), channel_id=1, replica_groups=mesh['pair'=4,'parity'=2,'half'=2,'member'=16] {'member'}, dimensions={0} | all-to-all | bytes 1048576 | tf_op jit(solution)/shard_map/all_to_all | solution.py:513
  114.9 1.6 shard_map.82.refs_3_
  116.5 0.7 collective-permute-start.15
  117.2 4.2 %shard_map.83.refs_0_.tensor_ref.old_ref = bf16[16,2,2,4,32,512]{5,4,3,2,1,0:T(8,128)(2,1)S(1)} custom-call(s32[8]{0:T(128)S(1)} %stack.70.where_ref, bf16[4,2,4,32,512]{4,3,2,1,0:T(8,128)(2,1)} %copy-done.5, bf16[4,2,4,32,512]{4,3,2,1,0:T(8,128)(2,1)} %collective-permute-done.7.refs_1_, bf16[4,2,4,32,512]{4,3,2,1,0:T(8,128)(2,1)} %collective-permute-done.8.refs_2_, ...), custom_call_target="tpu_custom_call" | custom-call | tf_op jit(solution)/shard_map/pallas_call | solution.py:574
  121.5 1.2 shard_map.84.bank_ref
  122.7 1.8 shard_map.85
  124.5 13.5 %all_to_all.46.moved_ref = bf16[16,64,256]{2,1,0:T(8,128)(2,1)S(1)} all-to-all(bf16[16,64,256]{2,1,0:T(8,128)(2,1)S(1)} %get-tuple-element.96), channel_id=1, replica_groups=mesh['pair'=4,'parity'=2,'half'=2,'member'=16] {'member'}, dimensions={0} | all-to-all | bytes 1048576 | tf_op jit(solution)/shard_map/all_to_all | solution.py:513
  138.0 3.5 %shard_map.86 = (bf16[16,64,256]{2,1,0:T(8,128)(2,1)S(1)}, f32[2,8,128]{2,1,0:T(8,128)S(1)}, bf16[64,1024]{1,0:T(8,128)(2,1)S(1)}) custom-call(s32[8,128]{1,0:T(8,128)S(1)} %get-tuple-element.67.pair_ref, f32[32,256]{1,0:T(8,128)S(1)} %get-tuple-element.68.mix_ref, f32[2,4,64,1024]{3,2,1,0:T(8,128)S(1)} %shard_map.84.bank_ref, ...), custom_call_target="tpu_custom_call" | custom-call | tf_op jit(solution)/shard_map/pallas_call | solution.py:556
  141.5 13.5 %all_to_all.47.moved_ref = bf16[16,64,256]{2,1,0:T(8,128)(2,1)S(1)} all-to-all(bf16[16,64,256]{2,1,0:T(8,128)(2,1)S(1)} %get-tuple-element.98), channel_id=1, replica_groups=mesh['pair'=4,'parity'=2,'half'=2,'member'=16] {'member'}, dimensions={0} | all-to-all | bytes 1048576 | tf_op jit(solution)/shard_map/all_to_all | solution.py:513
  155.0 1.6 shard_map.87.refs_4_
  156.5 0.9 collective-permute-start.16
  157.4 1.8 shard_map.88
  159.3 13.5 %all_to_all.48.moved_ref = bf16[16,64,256]{2,1,0:T(8,128)(2,1)S(1)} all-to-all(bf16[16,64,256]{2,1,0:T(8,128)(2,1)S(1)} %get-tuple-element.100), channel_id=1, replica_groups=mesh['pair'=4,'parity'=2,'half'=2,'member'=16] {'member'}, dimensions={0} | all-to-all | bytes 1048576 | tf_op jit(solution)/shard_map/all_to_all | solution.py:513
  172.7 3.5 %shard_map.89 = (bf16[16,64,256]{2,1,0:T(8,128)(2,1)S(1)}, f32[2,8,128]{2,1,0:T(8,128)S(1)}, bf16[64,1024]{1,0:T(8,128)(2,1)S(1)}) custom-call(s32[8,128]{1,0:T(8,128)S(1)} %get-tuple-element.67.pair_ref, f32[32,256]{1,0:T(8,128)S(1)} %get-tuple-element.68.mix_ref, f32[2,4,64,1024]{3,2,1,0:T(8,128)S(1)} %shard_map.84.bank_ref, ...), custom_call_target="tpu_custom_call" | custom-call | tf_op jit(solution)/shard_map/pallas_call | solution.py:556
  176.2 13.5 %all_to_all.49.moved_ref = bf16[16,64,256]{2,1,0:T(8,128)(2,1)S(1)} all-to-all(bf16[16,64,256]{2,1,0:T(8,128)(2,1)S(1)} %get-tuple-element.102), channel_id=1, replica_groups=mesh['pair'=4,'parity'=2,'half'=2,'member'=16] {'member'}, dimensions={0} | all-to-all | bytes 1048576 | tf_op jit(solution)/shard_map/all_to_all | solution.py:513
  189.7 1.6 shard_map.90.refs_5_
  191.3 1.3 collective-permute-start.17
  192.6 0.1 shard_map.91
  192.7 13.5 %collective-permute-done.17.env_ref = bf16[64,1024]{1,0:T(8,128)(2,1)S(1)} collective-permute-done((bf16[64,1024]{1,0:T(8,128)(2,1)S(1)}, bf16[64,1024]{1,0:T(8,128)(2,1)S(1)}, u32[]{:S(2)}, u32[]{:S(2)}) %collective-permute-start.17) | collective-permute-done | bytes 131104 | tf_op jit(solution)/shard_map/ppermute | solution.py:600
  206.2 1.8 shard_map.92
  208.0 13.9 %all_to_all.50.moved_ref = bf16[16,64,256]{2,1,0:T(8,128)(2,1)S(1)} all-to-all(bf16[16,64,256]{2,1,0:T(8,128)(2,1)S(1)} %get-tuple-element.116), channel_id=1, replica_groups=mesh['pair'=4,'parity'=2,'half'=2,'member'=16] {'member'}, dimensions={0} | all-to-all | bytes 1048576 | tf_op jit(solution)/shard_map/all_to_all | solution.py:513
  221.9 3.5 %shard_map.93 = (bf16[16,80,256]{2,1,0:T(8,128)(2,1)S(1)}, bf16[64,1024]{1,0:T(8,128)(2,1)S(1)}) custom-call(s32[8,128]{1,0:T(8,128)S(1)} %get-tuple-element.67.pair_ref, f32[32,256]{1,0:T(8,128)S(1)} %get-tuple-element.68.mix_ref, f32[2,4,64,1024]{3,2,1,0:T(8,128)S(1)} %shard_map.84.bank_ref, bf16[16,64,256]{2,1,0:T(8,128)(2,1)S(1)} %all_to_all.50.moved_ref, ...), custom_call_target="tpu_custom_call" | custom-call | tf_op jit(solution)/shard_map/pallas_call | solution.py:611
  225.4 14.6 %all_to_all.51.moved_ref = bf16[16,80,256]{2,1,0:T(8,128)(2,1)S(1)} all-to-all(bf16[16,80,256]{2,1,0:T(8,128)(2,1)S(1)} %get-tuple-element.118), channel_id=1, replica_groups=mesh['pair'=4,'parity'=2,'half'=2,'member'=16] {'member'}, dimensions={0} | all-to-all | bytes 1310720 | tf_op jit(solution)/shard_map/all_to_all | solution.py:513
  240.0 1.6 shard_map.94
  241.7 13.7 %all_to_all.52.home_ref = bf16[4,32,1152]{2,1,0:T(8,128)(2,1)S(1)} all-to-all(bf16[4,32,1152]{2,1,0:T(8,128)(2,1)S(1)} %shard_map.94), channel_id=1, replica_groups=mesh['pair'=4,'parity'=2,'half'=2,'member'=16] {'parity','half'}, dimensions={0} | all-to-all | bytes 589824 | tf_op jit(solution)/shard_map/all_to_all | solution.py:626
  255.3 0.7 shard_map.95
  (26 shorter events, 0.1 us)
Async XLA Ops:
  7.2 88.0 %all-gather.3.cloned.1.call-start = ((), (), s32[]{:S(2)}) async-start(), calls=%async_computation.9 | async-start | bytes 8650752 | tf_op jit(solution)/shard_map/all_gather | solution.py:492
  8.2 9.6 %collective-permute-start.1 = (bf16[4,32,1024]{2,1,0:T(8,128)(2,1)S(1)}, bf16[4,32,1024]{2,1,0:T(8,128)(2,1)S(1)}, u32[]{:S(2)}, u32[]{:S(2)}) collective-permute-start(bf16[4,32,1024]{2,1,0:T(8,128)(2,1)S(1)} %bitcast.33), channel_id=1, source_target_pairs={{0,32},{32,0},{1,33},{33,1},{2,34},{34,2},{3,35},{35,3},{4,36},{36... | collective-permute-start | bytes 786440 | tf_op jit(solution)/shard_map/ppermute | solution.py:469
  10.2 7.6 %collective-permute-start = (bf16[32,1024]{1,0:T(8,128)(2,1)S(1)}, bf16[32,1024]{1,0:T(8,128)(2,1)S(1)}, u32[]{:S(2)}, u32[]{:S(2)}) collective-permute-start(bf16[32,1024]{1,0:T(8,128)(2,1)S(1)} %dynamic-slice_bitcast_fusion), channel_id=1, source_target_pairs={{0,16},{16,0},{1,17},{17,1},{2,18},{18,2},{3,19},{19,3},{4,20},{20... | collective-permute-start | bytes 196616 | tf_op jit(solution)/shard_map/ppermute | solution.py:471
  14.3 0.7 copy-start.2
  15.0 0.7 copy-start.3
  15.6 0.7 copy-start.4
  18.6 1.0 copy-start.1
  20.2 1.4 collective-permute-start.2
  21.7 9.6 %collective-permute-start.5 = (bf16[2,4,32,512]{3,2,1,0:T(8,128)(2,1)S(1)}, bf16[2,4,32,512]{3,2,1,0:T(8,128)(2,1)S(1)}, u32[]{:S(2)}, u32[]{:S(2)}) collective-permute-start(bf16[2,4,32,512]{3,2,1,0:T(8,128)(2,1)S(1)} %maximum_select_fusion.1), channel_id=1, source_target_pairs={{0,6},{1,25},{2,0},{3,27},{4,2},{5,29},{6,4},{7,31},{8,14},{9,1},{... | collective-permute-start | bytes 786440 | tf_op jit(solution)/shard_map/ppermute | solution.py:432
  24.5 8.0 %collective-permute-start.4 = (bf16[2,4,32,512]{3,2,1,0:T(8,128)(2,1)S(1)}, bf16[2,4,32,512]{3,2,1,0:T(8,128)(2,1)S(1)}, u32[]{:S(2)}, u32[]{:S(2)}) collective-permute-start(bf16[2,4,32,512]{3,2,1,0:T(8,128)(2,1)S(1)} %maximum_select_fusion.1), channel_id=1, source_target_pairs={{0,4},{1,17},{2,6},{3,19},{4,0},{5,21},{6,2},{7,23},{8,12},{9,25},... | collective-permute-start | bytes 786440 | tf_op jit(solution)/shard_map/ppermute | solution.py:432
  25.3 11.3 %collective-permute-start.3 = (bf16[2,4,32,512]{3,2,1,0:T(8,128)(2,1)S(1)}, bf16[2,4,32,512]{3,2,1,0:T(8,128)(2,1)S(1)}, u32[]{:S(2)}, u32[]{:S(2)}) collective-permute-start(bf16[2,4,32,512]{3,2,1,0:T(8,128)(2,1)S(1)} %maximum_select_fusion.1), channel_id=1, source_target_pairs={{0,2},{1,9},{2,4},{3,11},{4,6},{5,13},{6,0},{7,15},{8,10},{9,17},{... | collective-permute-start | bytes 786440 | tf_op jit(solution)/shard_map/ppermute | solution.py:432
  26.2 10.6 %collective-permute-start.6 = (bf16[64,1024]{1,0:T(8,128)(2,1)S(1)}, bf16[64,1024]{1,0:T(8,128)(2,1)S(1)}, u32[]{:S(2)}, u32[]{:S(2)}) collective-permute-start(bf16[64,1024]{1,0:T(8,128)(2,1)S(1)} %get-tuple-element.75.env_ref), channel_id=1, source_target_pairs={{0,1},{1,0},{2,3},{3,2},{4,5},{5,4},{6,7},{7,6},{8,9},{9,8},{10,11... | collective-permute-start | bytes 393224 | tf_op jit(solution)/shard_map/ppermute | solution.py:501
  36.8 29.1 %copy-start.5 = (bf16[4,2,4,32,512]{4,3,2,1,0:T(8,128)(2,1)}, bf16[4,2,4,32,512]{4,3,2,1,0:T(8,128)(2,1)S(1)}, u32[]{:S(2)}) copy-start(bf16[4,2,4,32,512]{4,3,2,1,0:T(8,128)(2,1)S(1)} %pad_maximum_fusion.refs_0_) | copy-start | bytes 3145732
  36.8 16.1 %collective-permute-start.9 = (bf16[4,2,4,32,512]{4,3,2,1,0:T(8,128)(2,1)S(1)}, bf16[4,2,4,32,512]{4,3,2,1,0:T(8,128)(2,1)S(1)}, u32[]{:S(2)}, u32[]{:S(2)}) collective-permute-start(bf16[4,2,4,32,512]{4,3,2,1,0:T(8,128)(2,1)S(1)} %pad_maximum_fusion.refs_0_), channel_id=1, source_target_pairs={{0,24},{1,7},{2,26},{3,1},{4,28},{5,3},{6,30},{7,5},{8,0},{9,15},{... | collective-permute-start | bytes 3145736 | tf_op jit(solution)/shard_map/ppermute | solution.py:437
  37.0 24.5 %collective-permute-start.8 = (bf16[4,2,4,32,512]{4,3,2,1,0:T(8,128)(2,1)S(1)}, bf16[4,2,4,32,512]{4,3,2,1,0:T(8,128)(2,1)}, u32[]{:S(2)}, u32[]{:S(2)}) collective-permute-start(bf16[4,2,4,32,512]{4,3,2,1,0:T(8,128)(2,1)S(1)} %pad_maximum_fusion.refs_0_), channel_id=1, source_target_pairs={{0,16},{1,5},{2,18},{3,7},{4,20},{5,1},{6,22},{7,3},{8,24},{9,13},... | collective-permute-start | bytes 3145736 | tf_op jit(solution)/shard_map/ppermute | solution.py:437
  38.2 27.7 %collective-permute-start.7 = (bf16[4,2,4,32,512]{4,3,2,1,0:T(8,128)(2,1)S(1)}, bf16[4,2,4,32,512]{4,3,2,1,0:T(8,128)(2,1)}, u32[]{:S(2)}, u32[]{:S(2)}) collective-permute-start(bf16[4,2,4,32,512]{4,3,2,1,0:T(8,128)(2,1)S(1)} %pad_maximum_fusion.refs_0_), channel_id=1, source_target_pairs={{0,8},{1,3},{2,10},{3,5},{4,12},{5,7},{6,14},{7,1},{8,16},{9,11},{... | collective-permute-start | bytes 3145736 | tf_op jit(solution)/shard_map/ppermute | solution.py:437
  38.9 35.5 %collective-permute-start.10 = (bf16[4,2,4,32,512]{4,3,2,1,0:T(8,128)(2,1)S(1)}, bf16[4,2,4,32,512]{4,3,2,1,0:T(8,128)(2,1)}, u32[]{:S(2)}, u32[]{:S(2)}) collective-permute-start(bf16[4,2,4,32,512]{4,3,2,1,0:T(8,128)(2,1)S(1)} %pad_maximum_fusion.refs_0_), channel_id=1, source_target_pairs={{0,1},{1,0},{2,3},{3,2},{4,5},{5,4},{6,7},{7,6},{8,9},{9,8},{10,11... | collective-permute-start | bytes 3145736 | tf_op jit(solution)/shard_map/ppermute | solution.py:441
  52.9 13.0 %copy-start.6 = (bf16[4,2,4,32,512]{4,3,2,1,0:T(8,128)(2,1)}, bf16[4,2,4,32,512]{4,3,2,1,0:T(8,128)(2,1)S(1)}, u32[]{:S(2)}) copy-start(bf16[4,2,4,32,512]{4,3,2,1,0:T(8,128)(2,1)S(1)} %collective-permute-done.9.refs_3_) | copy-start | bytes 3145732
  52.9 35.5 %collective-permute-start.13 = (bf16[4,2,4,32,512]{4,3,2,1,0:T(8,128)(2,1)S(1)}, bf16[4,2,4,32,512]{4,3,2,1,0:T(8,128)(2,1)}, u32[]{:S(2)}, u32[]{:S(2)}) collective-permute-start(bf16[4,2,4,32,512]{4,3,2,1,0:T(8,128)(2,1)S(1)} %collective-permute-done.9.refs_3_), channel_id=1, source_target_pairs={{0,1},{1,0},{2,3},{3,2},{4,5},{5,4},{6,7},{7,6},{8,9},{9,8},{10,11... | collective-permute-start | bytes 3145736 | tf_op jit(solution)/shard_map/ppermute | solution.py:441
  61.5 27.0 %collective-permute-start.12 = (bf16[4,2,4,32,512]{4,3,2,1,0:T(8,128)(2,1)}, bf16[4,2,4,32,512]{4,3,2,1,0:T(8,128)(2,1)}, u32[]{:S(2)}, u32[]{:S(2)}) collective-permute-start(bf16[4,2,4,32,512]{4,3,2,1,0:T(8,128)(2,1)} %collective-permute-done.8.refs_2_), channel_id=1, source_target_pairs={{0,1},{1,0},{2,3},{3,2},{4,5},{5,4},{6,7},{7,6},{8,9},{9,8},{10,11... | collective-permute-start | bytes 3145736 | tf_op jit(solution)/shard_map/ppermute | solution.py:441
  65.9 22.6 %collective-permute-start.11 = (bf16[4,2,4,32,512]{4,3,2,1,0:T(8,128)(2,1)}, bf16[4,2,4,32,512]{4,3,2,1,0:T(8,128)(2,1)}, u32[]{:S(2)}, u32[]{:S(2)}) collective-permute-start(bf16[4,2,4,32,512]{4,3,2,1,0:T(8,128)(2,1)} %collective-permute-done.7.refs_1_), channel_id=1, source_target_pairs={{0,1},{1,0},{2,3},{3,2},{4,5},{5,4},{6,7},{7,6},{8,9},{9,8},{10,11... | collective-permute-start | bytes 3145736 | tf_op jit(solution)/shard_map/ppermute | solution.py:441
  70.6 17.8 %all-to-all-start = ((bf16[16,32,512]{2,1,0:T(8,128)(2,1)}), bf16[16,32,512]{2,1,0:T(8,128)(2,1)S(1)}, u32[]{:S(2)}, u32[]{:S(2)}) async-start(bf16[16,32,512]{2,1,0:T(8,128)(2,1)} %get-tuple-element.80), calls=%async_computation | async-start | bytes 1048576 | tf_op jit(solution)/shard_map/all_to_all | solution.py:513
  93.7 1.4 collective-permute-start.14
  95.1 19.8 %copy-start = (bf16[128,32,1024]{2,1,0:T(8,128)(2,1)S(1)}, bf16[128,32,1024]{2,1,0:T(8,128)(2,1)}, u32[]{:S(2)}) copy-start(bf16[128,32,1024]{2,1,0:T(8,128)(2,1)} %all-gather.3.cloned.1.call-done) | copy-start | bytes 25165828
  116.5 6.1 %collective-permute-start.15 = (bf16[64,1024]{1,0:T(8,128)(2,1)S(1)}, bf16[64,1024]{1,0:T(8,128)(2,1)S(1)}, u32[]{:S(2)}, u32[]{:S(2)}) collective-permute-start(bf16[64,1024]{1,0:T(8,128)(2,1)S(1)} %shard_map.82.refs_3_), channel_id=1, source_target_pairs={{0,64},{1,65},{2,66},{3,67},{4,68},{5,69},{6,70},{7,71},{8,72},{9,... | collective-permute-start | bytes 393224 | tf_op jit(solution)/shard_map/ppermute | solution.py:600
  156.5 0.9 collective-permute-start.16
  191.3 14.9 %collective-permute-start.17 = (bf16[64,1024]{1,0:T(8,128)(2,1)S(1)}, bf16[64,1024]{1,0:T(8,128)(2,1)S(1)}, u32[]{:S(2)}, u32[]{:S(2)}) collective-permute-start(bf16[64,1024]{1,0:T(8,128)(2,1)S(1)} %shard_map.90.refs_5_), channel_id=1, source_target_pairs={{128,192},{129,193},{130,194},{131,195},{132,196},{133,197},{134,1... | collective-permute-start | bytes 393224 | tf_op jit(solution)/shard_map/ppermute | solution.py:600
Sparse Core Ops, SparseCore 0:
  18.7 74.9 all-gather.2

commit v6 on v5

--- a/solution.py
+++ b/solution.py
@@ -17,6 +17,13 @@
 def two_parts(value):
     high = value.astype(jnp.bfloat16).astype(jnp.float32)
     return jnp.concatenate([high, value - high], axis=0).astype(jnp.bfloat16)
+
+
+def for_first_pair(kernel):
+    def guarded(static, where_ref, *refs):
+        pl.when(where_ref[1] == 0)(functools.partial(kernel, static, where_ref, *refs))
+
+    return guarded
 
 
 def columns(tensor_ref, t, c):
@@ -115,6 +122,7 @@
         copy.wait()
 
 
+@for_first_pair
 def pieces_kernel(side, where_ref, moved_ref, *refs):
     pieces, (env_ref, tensor, sems) = refs[:-3], refs[-3:]
     copies = lay(side, where_ref, pieces, tensor, sems)
@@ -145,6 +153,7 @@
             ).astype(jnp.bfloat16)
 
 
+@for_first_pair
 def stream_kernel(
     now, where_ref, mix_ref, look_ref, env_ref, twin_ref, tensor_ref, seen_ref, out_ref, new_ref, held, sems
 ):
@@ -206,6 +215,7 @@
     return blocks
 
 
+@for_first_pair
 def start_kernel(side, where_ref, mix_ref, look_ref, env_ref, twin_ref, *refs):
     pieces, (out_ref, new_ref, tensor, sems) = refs[:-4], refs[-4:]
     core = where_ref[4]

time: 264 us -> 260 us (0.985)
  Pallas kernels: 44.7 us -> 34.2 us
  waiting for transfers between devices: 58.7 us -> 65.5 us
    all_gather x1, waiting for transfers between devices: 0.01 us -> 5.74 us  [on_device(): after = lax.all_gather(jnp.where(parity == 0, near, mine), bond, axis=0)]
    pallas_call x1, Pallas kernels: 5.25 us -> 1.02 us  [on_device(): pl.pallas_call(functools.partial(pieces_kernel, side), in_specs=[SMEM, VM...]
    pallas_call x1, Pallas kernels: 3.91 us -> 0.69 us  [on_device(): pl.pallas_call(functools.partial(stream_kernel, 0), in_specs=[SMEM] * 3 +...]
    pallas_call x1, Pallas kernels: 4.77 us -> 1.75 us  [on_device(): pl.pallas_call(functools.partial(start_kernel, side), in_specs=[SMEM] * 3...]
  transfers between devices with their start and end apart: 20 -> 20, of which waited for: 9 -> 10; matrix products, arithmetic and copies ran while one was open for 1% -> 1% of each run, Pallas kernels for 7% -> 4%
where the time goes in v6:
time: 260 us; the launch traced here: 259 us
  blocking collectives  112 us (43%)
  waiting for transfers between devices  65.5 us (25%)
  Pallas kernels  34.2 us (13%)
  starting transfers between devices  26.5 us (10%)
  between operations  14.3 us (6%)
  local copies, waits for them, and re-layouts  5.71 us (2%)
    all_to_all x7, blocking collectives, exchange(): return lax.all_to_all(sent, 'member', 0, 0, tiled=True)  97.2 us
    ppermute x3, waiting for transfers between devices, second_ring(): lax.ppermute(row, bond, shifts(side, m, False))  18.3 us
    all_to_all x1, blocking collectives, on_device(): home = lax.all_to_all(homeward, ('parity', 'half'), 0, 0, tiled=True)  14.8 us
    ppermute x3, waiting for transfers between devices, on_device(): env = lax.ppermute(env, 'pair', [(now, now + 1)])  14.6 us
    all_to_all x1, waiting for transfers between devices, exchange(): return lax.all_to_all(sent, 'member', 0, 0, tiled=True)  14.1 us
    ppermute x3, waiting for transfers between devices, first_ring(): lax.ppermute(chip, bond, shifts(side, k, True))  10.4 us
    ppermute x4, starting transfers between devices, swap_cores(): return [lax.ppermute(p, ('half', 'member'), twins(side)) for p in pieces]  8.65 us
    pallas_call x2, Pallas kernels, on_device(): pl.pallas_call(functools.partial(middle_kernel, now), in_specs=[VMEM] * 7...  6.98 us
  transfers between devices with their start and end apart: 20, of which 10 were waited for; matrix products, arithmetic and copies ran while one was open for 1% of the time, Pallas kernels for 4%

profile of v6, /device:TPU:192, one launch (start us, length us, event | category | flops | bytes accessed | tf_op | source)
XLA Modules:
  0.0 259.1 jit_solution(7911875466526561160)
XLA Ops:
  7.2 0.0 all-gather.3.cloned.1.call-start
  7.2 1.0 copy.13
  8.2 1.1 collective-permute-start.1
  9.3 0.8 dynamic-slice_bitcast_fusion
  10.2 3.2 %collective-permute-start = (bf16[32,1024]{1,0:T(8,128)(2,1)S(1)}, bf16[32,1024]{1,0:T(8,128)(2,1)S(1)}, u32[]{:S(2)}, u32[]{:S(2)}) collective-permute-start(bf16[32,1024]{1,0:T(8,128)(2,1)S(1)} %dynamic-slice_bitcast_fusion), channel_id=1, source_target_pairs={{0,16},{16,0},{1,17},{17,1},{2,18},{18,2},{3,19},{19,3},{4,20},{20... | collective-permute-start | bytes 196616 | tf_op jit(solution)/shard_map/ppermute | solution.py:481
  13.4 0.8 copy.11.operators_ref
  14.2 0.1 stack.70.where_ref
  14.3 0.7 copy-done.2
  15.0 0.7 copy-done.3
  15.6 0.7 copy-done.4
  16.3 1.5 shard_map.77
  17.8 0.7 broadcast_select_fusion
  18.6 0.9 copy-done.1
  19.6 0.7 shard_map.78
  20.2 0.1 collective-permute-start.2
  20.3 1.3 collective-permute-done.2
  21.7 2.8 %collective-permute-start.5 = (bf16[2,4,32,512]{3,2,1,0:T(8,128)(2,1)S(1)}, bf16[2,4,32,512]{3,2,1,0:T(8,128)(2,1)S(1)}, u32[]{:S(2)}, u32[]{:S(2)}) collective-permute-start(bf16[2,4,32,512]{3,2,1,0:T(8,128)(2,1)S(1)} %maximum_select_fusion.1), channel_id=1, source_target_pairs={{0,6},{1,25},{2,0},{3,27},{4,2},{5,29},{6,4},{7,31},{8,14},{9,1},{... | collective-permute-start | bytes 786440 | tf_op jit(solution)/shard_map/ppermute | solution.py:442
  24.5 0.8 collective-permute-start.4
  25.3 0.9 collective-permute-start.3
  26.3 5.0 %collective-permute-done.5 = bf16[2,4,32,512]{3,2,1,0:T(8,128)(2,1)S(1)} collective-permute-done((bf16[2,4,32,512]{3,2,1,0:T(8,128)(2,1)S(1)}, bf16[2,4,32,512]{3,2,1,0:T(8,128)(2,1)S(1)}, u32[]{:S(2)}, u32[]{:S(2)}) %collective-permute-start.5) | collective-permute-done | bytes 262176 | tf_op jit(solution)/shard_map/ppermute | solution.py:442
  31.3 1.2 collective-permute-done.4
  32.5 4.1 %collective-permute-done.3 = bf16[2,4,32,512]{3,2,1,0:T(8,128)(2,1)S(1)} collective-permute-done((bf16[2,4,32,512]{3,2,1,0:T(8,128)(2,1)S(1)}, bf16[2,4,32,512]{3,2,1,0:T(8,128)(2,1)S(1)}, u32[]{:S(2)}, u32[]{:S(2)}) %collective-permute-start.3) | collective-permute-done | bytes 262176 | tf_op jit(solution)/shard_map/ppermute | solution.py:442
  36.6 0.1 pad_maximum_fusion.refs_4_.refs_1_.refs_0_
  36.8 0.2 collective-permute-start.9
  37.0 1.2 collective-permute-start.8
  38.2 0.7 collective-permute-start.7
  38.9 14.0 %collective-permute-done.9.refs_7_.refs_4_.refs_3_ = bf16[4,2,4,32,512]{4,3,2,1,0:T(8,128)(2,1)S(1)} collective-permute-done((bf16[4,2,4,32,512]{4,3,2,1,0:T(8,128)(2,1)S(1)}, bf16[4,2,4,32,512]{4,3,2,1,0:T(8,128)(2,1)S(1)}, u32[]{:S(2)}, u32[]{:S(2)}) %collective-permute-start.9) | collective-permute-done | bytes 1048608 | tf_op jit(solution)/shard_map/ppermute | solution.py:447
  52.9 8.6 %collective-permute-start.13 = (bf16[4,2,4,32,512]{4,3,2,1,0:T(8,128)(2,1)S(1)}, bf16[4,2,4,32,512]{4,3,2,1,0:T(8,128)(2,1)}, u32[]{:S(2)}, u32[]{:S(2)}) collective-permute-start(bf16[4,2,4,32,512]{4,3,2,1,0:T(8,128)(2,1)S(1)} %collective-permute-done.9.refs_7_.refs_4_.refs_3_), channel_id=1, source_target_pairs={{0,1},{1,0},{2,3},{3,2},{4,5},{5,4},{6,7},{7,6},{8,9},{9,8},{10,11... | collective-permute-start | bytes 3145736 | tf_op jit(solution)/shard_map/ppermute | solution.py:451
  61.5 0.1 collective-permute-start.12
  61.5 4.3 %collective-permute-done.7.refs_5_.refs_2_.refs_1_ = bf16[4,2,4,32,512]{4,3,2,1,0:T(8,128)(2,1)} collective-permute-done((bf16[4,2,4,32,512]{4,3,2,1,0:T(8,128)(2,1)S(1)}, bf16[4,2,4,32,512]{4,3,2,1,0:T(8,128)(2,1)}, u32[]{:S(2)}, u32[]{:S(2)}) %collective-permute-start.7) | collective-permute-done | bytes 1048608 | tf_op jit(solution)/shard_map/ppermute | solution.py:447
  65.9 1.8 shard_map.79
  67.6 3.6 %all-to-all-start = ((bf16[16,32,512]{2,1,0:T(8,128)(2,1)}), bf16[16,32,512]{2,1,0:T(8,128)(2,1)S(1)}, u32[]{:S(2)}, u32[]{:S(2)}) async-start(bf16[16,32,512]{2,1,0:T(8,128)(2,1)} %get-tuple-element.80), calls=%async_computation | async-start | bytes 1048576 | tf_op jit(solution)/shard_map/all_to_all | solution.py:523
  71.2 14.1 %all-to-all-done.refs_0_ = bf16[16,32,512]{2,1,0:T(8,128)(2,1)S(1)} async-done(((bf16[16,32,512]{2,1,0:T(8,128)(2,1)}), bf16[16,32,512]{2,1,0:T(8,128)(2,1)S(1)}, u32[]{:S(2)}, u32[]{:S(2)}) %all-to-all-start) | async-done | bytes 524320 | tf_op jit(solution)/shard_map/all_to_all | solution.py:523
  85.3 1.0 shard_map.80.refs_2_.refs_0_
  86.4 0.6 collective-permute-start.14
  87.0 1.0 collective-permute-done.14.refs_3_
  87.9 5.7 %all-gather.3.cloned.1.call-done = bf16[128,32,1024]{2,1,0:T(8,128)(2,1)} async-done(((bf16[4,32,1024]{2,1,0:T(8,128)(2,1)}), bf16[128,32,1024]{2,1,0:T(8,128)(2,1)}) %all-gather.3.cloned.1.call-update) | async-done | bytes 8388624 | tf_op jit(solution)/shard_map/all_gather | solution.py:502
  93.7 0.7 shard_map.81
  94.4 14.6 %all_to_all.45.moved_ref = bf16[16,32,512]{2,1,0:T(8,128)(2,1)S(1)} all-to-all(bf16[16,32,512]{2,1,0:T(8,128)(2,1)S(1)} %get-tuple-element.85), channel_id=1, replica_groups=mesh['pair'=4,'parity'=2,'half'=2,'member'=16] {'member'}, dimensions={0} | all-to-all | bytes 1048576 | tf_op jit(solution)/shard_map/all_to_all | solution.py:523
  109.0 1.6 shard_map.82.refs_3_
  110.6 0.7 collective-permute-start.15
  111.3 4.2 %shard_map.83.refs_0_.tensor_ref.old_ref = bf16[16,2,2,4,32,512]{5,4,3,2,1,0:T(8,128)(2,1)S(1)} custom-call(s32[8]{0:T(128)S(1)} %stack.70.where_ref, bf16[4,2,4,32,512]{4,3,2,1,0:T(8,128)(2,1)} %copy-done.5, bf16[4,2,4,32,512]{4,3,2,1,0:T(8,128)(2,1)} %collective-permute-done.7.refs_5_.refs_2_.refs_1_, ...), custom_call_target="tpu_custom_call" | custom-call | tf_op jit(solution)/shard_map/pallas_call | solution.py:584
  115.5 1.2 shard_map.84.bank_ref
  116.7 1.8 shard_map.85
  118.5 13.5 %all_to_all.46.moved_ref = bf16[16,64,256]{2,1,0:T(8,128)(2,1)S(1)} all-to-all(bf16[16,64,256]{2,1,0:T(8,128)(2,1)S(1)} %get-tuple-element.96), channel_id=1, replica_groups=mesh['pair'=4,'parity'=2,'half'=2,'member'=16] {'member'}, dimensions={0} | all-to-all | bytes 1048576 | tf_op jit(solution)/shard_map/all_to_all | solution.py:523
  132.0 3.5 %shard_map.86 = (bf16[16,64,256]{2,1,0:T(8,128)(2,1)S(1)}, f32[2,8,128]{2,1,0:T(8,128)S(1)}, bf16[64,1024]{1,0:T(8,128)(2,1)S(1)}) custom-call(s32[8,128]{1,0:T(8,128)S(1)} %get-tuple-element.67.pair_ref, f32[32,256]{1,0:T(8,128)S(1)} %get-tuple-element.68.mix_ref, f32[2,4,64,1024]{3,2,1,0:T(8,128)S(1)} %shard_map.84.bank_ref, ...), custom_call_target="tpu_custom_call" | custom-call | tf_op jit(solution)/shard_map/pallas_call | solution.py:566
  135.5 13.5 %all_to_all.47.moved_ref = bf16[16,64,256]{2,1,0:T(8,128)(2,1)S(1)} all-to-all(bf16[16,64,256]{2,1,0:T(8,128)(2,1)S(1)} %get-tuple-element.98), channel_id=1, replica_groups=mesh['pair'=4,'parity'=2,'half'=2,'member'=16] {'member'}, dimensions={0} | all-to-all | bytes 1048576 | tf_op jit(solution)/shard_map/all_to_all | solution.py:523
  149.0 1.6 shard_map.87.refs_4_
  150.6 0.7 collective-permute-start.16
  151.3 1.8 shard_map.88
  153.1 13.7 %all_to_all.48.moved_ref = bf16[16,64,256]{2,1,0:T(8,128)(2,1)S(1)} all-to-all(bf16[16,64,256]{2,1,0:T(8,128)(2,1)S(1)} %get-tuple-element.100), channel_id=1, replica_groups=mesh['pair'=4,'parity'=2,'half'=2,'member'=16] {'member'}, dimensions={0} | all-to-all | bytes 1048576 | tf_op jit(solution)/shard_map/all_to_all | solution.py:523
  166.8 3.5 %shard_map.89 = (bf16[16,64,256]{2,1,0:T(8,128)(2,1)S(1)}, f32[2,8,128]{2,1,0:T(8,128)S(1)}, bf16[64,1024]{1,0:T(8,128)(2,1)S(1)}) custom-call(s32[8,128]{1,0:T(8,128)S(1)} %get-tuple-element.67.pair_ref, f32[32,256]{1,0:T(8,128)S(1)} %get-tuple-element.68.mix_ref, f32[2,4,64,1024]{3,2,1,0:T(8,128)S(1)} %shard_map.84.bank_ref, ...), custom_call_target="tpu_custom_call" | custom-call | tf_op jit(solution)/shard_map/pallas_call | solution.py:566
  170.3 13.5 %all_to_all.49.moved_ref = bf16[16,64,256]{2,1,0:T(8,128)(2,1)S(1)} all-to-all(bf16[16,64,256]{2,1,0:T(8,128)(2,1)S(1)} %get-tuple-element.102), channel_id=1, replica_groups=mesh['pair'=4,'parity'=2,'half'=2,'member'=16] {'member'}, dimensions={0} | all-to-all | bytes 1048576 | tf_op jit(solution)/shard_map/all_to_all | solution.py:523
  183.8 1.6 shard_map.90.refs_5_
  185.4 1.3 collective-permute-start.17
  186.7 0.1 shard_map.91
  186.7 14.6 %collective-permute-done.17.env_ref = bf16[64,1024]{1,0:T(8,128)(2,1)S(1)} collective-permute-done((bf16[64,1024]{1,0:T(8,128)(2,1)S(1)}, bf16[64,1024]{1,0:T(8,128)(2,1)S(1)}, u32[]{:S(2)}, u32[]{:S(2)}) %collective-permute-start.17) | collective-permute-done | bytes 131104 | tf_op jit(solution)/shard_map/ppermute | solution.py:610
  201.4 1.8 shard_map.92
  203.2 13.9 %all_to_all.50.moved_ref = bf16[16,64,256]{2,1,0:T(8,128)(2,1)S(1)} all-to-all(bf16[16,64,256]{2,1,0:T(8,128)(2,1)S(1)} %get-tuple-element.116), channel_id=1, replica_groups=mesh['pair'=4,'parity'=2,'half'=2,'member'=16] {'member'}, dimensions={0} | all-to-all | bytes 1048576 | tf_op jit(solution)/shard_map/all_to_all | solution.py:523
  217.0 3.5 %shard_map.93 = (bf16[16,80,256]{2,1,0:T(8,128)(2,1)S(1)}, bf16[64,1024]{1,0:T(8,128)(2,1)S(1)}) custom-call(s32[8,128]{1,0:T(8,128)S(1)} %get-tuple-element.67.pair_ref, f32[32,256]{1,0:T(8,128)S(1)} %get-tuple-element.68.mix_ref, f32[2,4,64,1024]{3,2,1,0:T(8,128)S(1)} %shard_map.84.bank_ref, bf16[16,64,256]{2,1,0:T(8,128)(2,1)S(1)} %all_to_all.50.moved_ref, ...), custom_call_target="tpu_custom_call" | custom-call | tf_op jit(solution)/shard_map/pallas_call | solution.py:621
  220.5 14.6 %all_to_all.51.moved_ref = bf16[16,80,256]{2,1,0:T(8,128)(2,1)S(1)} all-to-all(bf16[16,80,256]{2,1,0:T(8,128)(2,1)S(1)} %get-tuple-element.118), channel_id=1, replica_groups=mesh['pair'=4,'parity'=2,'half'=2,'member'=16] {'member'}, dimensions={0} | all-to-all | bytes 1310720 | tf_op jit(solution)/shard_map/all_to_all | solution.py:523
  235.2 1.6 shard_map.94
  236.8 14.8 %all_to_all.52.home_ref = bf16[4,32,1152]{2,1,0:T(8,128)(2,1)S(1)} all-to-all(bf16[4,32,1152]{2,1,0:T(8,128)(2,1)S(1)} %shard_map.94), channel_id=1, replica_groups=mesh['pair'=4,'parity'=2,'half'=2,'member'=16] {'parity','half'}, dimensions={0} | all-to-all | bytes 589824 | tf_op jit(solution)/shard_map/all_to_all | solution.py:636
  251.6 0.7 shard_map.95
  (26 shorter events, 0.1 us)
Async XLA Ops:
  7.2 86.5 %all-gather.3.cloned.1.call-start = ((), (), s32[]{:S(2)}) async-start(), calls=%async_computation.9 | async-start | bytes 8650752 | tf_op jit(solution)/shard_map/all_gather | solution.py:502
  8.2 9.6 %collective-permute-start.1 = (bf16[4,32,1024]{2,1,0:T(8,128)(2,1)S(1)}, bf16[4,32,1024]{2,1,0:T(8,128)(2,1)S(1)}, u32[]{:S(2)}, u32[]{:S(2)}) collective-permute-start(bf16[4,32,1024]{2,1,0:T(8,128)(2,1)S(1)} %bitcast.33), channel_id=1, source_target_pairs={{0,32},{32,0},{1,33},{33,1},{2,34},{34,2},{3,35},{35,3},{4,36},{36... | collective-permute-start | bytes 786440 | tf_op jit(solution)/shard_map/ppermute | solution.py:479
  10.2 7.6 %collective-permute-start = (bf16[32,1024]{1,0:T(8,128)(2,1)S(1)}, bf16[32,1024]{1,0:T(8,128)(2,1)S(1)}, u32[]{:S(2)}, u32[]{:S(2)}) collective-permute-start(bf16[32,1024]{1,0:T(8,128)(2,1)S(1)} %dynamic-slice_bitcast_fusion), channel_id=1, source_target_pairs={{0,16},{16,0},{1,17},{17,1},{2,18},{18,2},{3,19},{19,3},{4,20},{20... | collective-permute-start | bytes 196616 | tf_op jit(solution)/shard_map/ppermute | solution.py:481
  14.3 0.7 copy-start.2
  15.0 0.7 copy-start.3
  15.6 0.7 copy-start.4
  18.6 1.0 copy-start.1
  20.2 1.4 collective-permute-start.2
  21.7 9.6 %collective-permute-start.5 = (bf16[2,4,32,512]{3,2,1,0:T(8,128)(2,1)S(1)}, bf16[2,4,32,512]{3,2,1,0:T(8,128)(2,1)S(1)}, u32[]{:S(2)}, u32[]{:S(2)}) collective-permute-start(bf16[2,4,32,512]{3,2,1,0:T(8,128)(2,1)S(1)} %maximum_select_fusion.1), channel_id=1, source_target_pairs={{0,6},{1,25},{2,0},{3,27},{4,2},{5,29},{6,4},{7,31},{8,14},{9,1},{... | collective-permute-start | bytes 786440 | tf_op jit(solution)/shard_map/ppermute | solution.py:442
  24.5 8.0 %collective-permute-start.4 = (bf16[2,4,32,512]{3,2,1,0:T(8,128)(2,1)S(1)}, bf16[2,4,32,512]{3,2,1,0:T(8,128)(2,1)S(1)}, u32[]{:S(2)}, u32[]{:S(2)}) collective-permute-start(bf16[2,4,32,512]{3,2,1,0:T(8,128)(2,1)S(1)} %maximum_select_fusion.1), channel_id=1, source_target_pairs={{0,4},{1,17},{2,6},{3,19},{4,0},{5,21},{6,2},{7,23},{8,12},{9,25},... | collective-permute-start | bytes 786440 | tf_op jit(solution)/shard_map/ppermute | solution.py:442
  25.3 11.3 %collective-permute-start.3 = (bf16[2,4,32,512]{3,2,1,0:T(8,128)(2,1)S(1)}, bf16[2,4,32,512]{3,2,1,0:T(8,128)(2,1)S(1)}, u32[]{:S(2)}, u32[]{:S(2)}) collective-permute-start(bf16[2,4,32,512]{3,2,1,0:T(8,128)(2,1)S(1)} %maximum_select_fusion.1), channel_id=1, source_target_pairs={{0,2},{1,9},{2,4},{3,11},{4,6},{5,13},{6,0},{7,15},{8,10},{9,17},{... | collective-permute-start | bytes 786440 | tf_op jit(solution)/shard_map/ppermute | solution.py:442
  26.2 10.6 %collective-permute-start.6 = (bf16[64,1024]{1,0:T(8,128)(2,1)S(1)}, bf16[64,1024]{1,0:T(8,128)(2,1)S(1)}, u32[]{:S(2)}, u32[]{:S(2)}) collective-permute-start(bf16[64,1024]{1,0:T(8,128)(2,1)S(1)} %get-tuple-element.75.refs_2_), channel_id=1, source_target_pairs={{0,1},{1,0},{2,3},{3,2},{4,5},{5,4},{6,7},{7,6},{8,9},{9,8},{10,11... | collective-permute-start | bytes 393224 | tf_op jit(solution)/shard_map/ppermute | solution.py:511
  36.8 29.1 %copy-start.5 = (bf16[4,2,4,32,512]{4,3,2,1,0:T(8,128)(2,1)}, bf16[4,2,4,32,512]{4,3,2,1,0:T(8,128)(2,1)S(1)}, u32[]{:S(2)}) copy-start(bf16[4,2,4,32,512]{4,3,2,1,0:T(8,128)(2,1)S(1)} %pad_maximum_fusion.refs_4_.refs_1_.refs_0_) | copy-start | bytes 3145732
  36.8 16.1 %collective-permute-start.9 = (bf16[4,2,4,32,512]{4,3,2,1,0:T(8,128)(2,1)S(1)}, bf16[4,2,4,32,512]{4,3,2,1,0:T(8,128)(2,1)S(1)}, u32[]{:S(2)}, u32[]{:S(2)}) collective-permute-start(bf16[4,2,4,32,512]{4,3,2,1,0:T(8,128)(2,1)S(1)} %pad_maximum_fusion.refs_4_.refs_1_.refs_0_), channel_id=1, source_target_pairs={{0,24},{1,7},{2,26},{3,1},{4,28},{5,3},{6,30},{7,5},{8,0},{9,15},{... | collective-permute-start | bytes 3145736 | tf_op jit(solution)/shard_map/ppermute | solution.py:447
  37.0 24.5 %collective-permute-start.8 = (bf16[4,2,4,32,512]{4,3,2,1,0:T(8,128)(2,1)S(1)}, bf16[4,2,4,32,512]{4,3,2,1,0:T(8,128)(2,1)}, u32[]{:S(2)}, u32[]{:S(2)}) collective-permute-start(bf16[4,2,4,32,512]{4,3,2,1,0:T(8,128)(2,1)S(1)} %pad_maximum_fusion.refs_4_.refs_1_.refs_0_), channel_id=1, source_target_pairs={{0,16},{1,5},{2,18},{3,7},{4,20},{5,1},{6,22},{7,3},{8,24},{9,13},... | collective-permute-start | bytes 3145736 | tf_op jit(solution)/shard_map/ppermute | solution.py:447
  38.2 27.7 %collective-permute-start.7 = (bf16[4,2,4,32,512]{4,3,2,1,0:T(8,128)(2,1)S(1)}, bf16[4,2,4,32,512]{4,3,2,1,0:T(8,128)(2,1)}, u32[]{:S(2)}, u32[]{:S(2)}) collective-permute-start(bf16[4,2,4,32,512]{4,3,2,1,0:T(8,128)(2,1)S(1)} %pad_maximum_fusion.refs_4_.refs_1_.refs_0_), channel_id=1, source_target_pairs={{0,8},{1,3},{2,10},{3,5},{4,12},{5,7},{6,14},{7,1},{8,16},{9,11},{... | collective-permute-start | bytes 3145736 | tf_op jit(solution)/shard_map/ppermute | solution.py:447
  38.9 32.3 %collective-permute-start.10 = (bf16[4,2,4,32,512]{4,3,2,1,0:T(8,128)(2,1)S(1)}, bf16[4,2,4,32,512]{4,3,2,1,0:T(8,128)(2,1)}, u32[]{:S(2)}, u32[]{:S(2)}) collective-permute-start(bf16[4,2,4,32,512]{4,3,2,1,0:T(8,128)(2,1)S(1)} %pad_maximum_fusion.refs_4_.refs_1_.refs_0_), channel_id=1, source_target_pairs={{0,1},{1,0},{2,3},{3,2},{4,5},{5,4},{6,7},{7,6},{8,9},{9,8},{10,11... | collective-permute-start | bytes 3145736 | tf_op jit(solution)/shard_map/ppermute | solution.py:451
  52.9 13.0 %copy-start.6 = (bf16[4,2,4,32,512]{4,3,2,1,0:T(8,128)(2,1)}, bf16[4,2,4,32,512]{4,3,2,1,0:T(8,128)(2,1)S(1)}, u32[]{:S(2)}) copy-start(bf16[4,2,4,32,512]{4,3,2,1,0:T(8,128)(2,1)S(1)} %collective-permute-done.9.refs_7_.refs_4_.refs_3_) | copy-start | bytes 3145732
  52.9 32.4 %collective-permute-start.13 = (bf16[4,2,4,32,512]{4,3,2,1,0:T(8,128)(2,1)S(1)}, bf16[4,2,4,32,512]{4,3,2,1,0:T(8,128)(2,1)}, u32[]{:S(2)}, u32[]{:S(2)}) collective-permute-start(bf16[4,2,4,32,512]{4,3,2,1,0:T(8,128)(2,1)S(1)} %collective-permute-done.9.refs_7_.refs_4_.refs_3_), channel_id=1, source_target_pairs={{0,1},{1,0},{2,3},{3,2},{4,5},{5,4},{6,7},{7,6},{8,9},{9,8},{10,11... | collective-permute-start | bytes 3145736 | tf_op jit(solution)/shard_map/ppermute | solution.py:451
  61.5 23.9 %collective-permute-start.12 = (bf16[4,2,4,32,512]{4,3,2,1,0:T(8,128)(2,1)}, bf16[4,2,4,32,512]{4,3,2,1,0:T(8,128)(2,1)}, u32[]{:S(2)}, u32[]{:S(2)}) collective-permute-start(bf16[4,2,4,32,512]{4,3,2,1,0:T(8,128)(2,1)} %collective-permute-done.8.refs_6_.refs_3_.refs_2_), channel_id=1, source_target_pairs={{0,1},{1,0},{2,3},{3,2},{4,5},{5,4},{6,7},{7,6},{8,9},{9,8},{10,11... | collective-permute-start | bytes 3145736 | tf_op jit(solution)/shard_map/ppermute | solution.py:451
  65.9 19.5 %collective-permute-start.11 = (bf16[4,2,4,32,512]{4,3,2,1,0:T(8,128)(2,1)}, bf16[4,2,4,32,512]{4,3,2,1,0:T(8,128)(2,1)}, u32[]{:S(2)}, u32[]{:S(2)}) collective-permute-start(bf16[4,2,4,32,512]{4,3,2,1,0:T(8,128)(2,1)} %collective-permute-done.7.refs_5_.refs_2_.refs_1_), channel_id=1, source_target_pairs={{0,1},{1,0},{2,3},{3,2},{4,5},{5,4},{6,7},{7,6},{8,9},{9,8},{10,11... | collective-permute-start | bytes 3145736 | tf_op jit(solution)/shard_map/ppermute | solution.py:451
  67.6 17.7 %all-to-all-start = ((bf16[16,32,512]{2,1,0:T(8,128)(2,1)}), bf16[16,32,512]{2,1,0:T(8,128)(2,1)S(1)}, u32[]{:S(2)}, u32[]{:S(2)}) async-start(bf16[16,32,512]{2,1,0:T(8,128)(2,1)} %get-tuple-element.80), calls=%async_computation | async-start | bytes 1048576 | tf_op jit(solution)/shard_map/all_to_all | solution.py:523
  86.4 1.6 collective-permute-start.14
  93.7 15.3 %copy-start = (bf16[128,32,1024]{2,1,0:T(8,128)(2,1)S(1)}, bf16[128,32,1024]{2,1,0:T(8,128)(2,1)}, u32[]{:S(2)}) copy-start(bf16[128,32,1024]{2,1,0:T(8,128)(2,1)} %all-gather.3.cloned.1.call-done) | copy-start | bytes 25165828
  110.6 6.1 %collective-permute-start.15 = (bf16[64,1024]{1,0:T(8,128)(2,1)S(1)}, bf16[64,1024]{1,0:T(8,128)(2,1)S(1)}, u32[]{:S(2)}, u32[]{:S(2)}) collective-permute-start(bf16[64,1024]{1,0:T(8,128)(2,1)S(1)} %shard_map.82.refs_3_), channel_id=1, source_target_pairs={{0,64},{1,65},{2,66},{3,67},{4,68},{5,69},{6,70},{7,71},{8,72},{9,... | collective-permute-start | bytes 393224 | tf_op jit(solution)/shard_map/ppermute | solution.py:610
  150.6 0.7 collective-permute-start.16
  185.4 16.0 %collective-permute-start.17 = (bf16[64,1024]{1,0:T(8,128)(2,1)S(1)}, bf16[64,1024]{1,0:T(8,128)(2,1)S(1)}, u32[]{:S(2)}, u32[]{:S(2)}) collective-permute-start(bf16[64,1024]{1,0:T(8,128)(2,1)S(1)} %shard_map.90.refs_5_), channel_id=1, source_target_pairs={{128,192},{129,193},{130,194},{131,195},{132,196},{133,197},{134,1... | collective-permute-start | bytes 393224 | tf_op jit(solution)/shard_map/ppermute | solution.py:610
Sparse Core Ops, SparseCore 0:
  18.7 74.9 all-gather.2

commit v7 on v6

--- a/solution.py
+++ b/solution.py
@@ -77,7 +77,12 @@
 def gather(moved_ref, tensor_ref, env_ref):
     rows, width = env_ref.shape
     half = moved_ref.shape[0]
-    if moved_ref.shape[1] < rows:
+    if moved_ref.shape[2] < COLS:
+        left = [
+            jnp.concatenate([moved_ref[g, :rows], moved_ref[g, rows : 2 * rows]], axis=1)
+            for g in range(half)
+        ]
+    elif moved_ref.shape[1] < rows:
         left = [
             jnp.concatenate([moved_ref[g], moved_ref[g + 1]], axis=0) for g in range(0, half, 2)
         ]
@@ -279,7 +284,12 @@
         turned = tall.astype(jnp.bfloat16).T.reshape(COLS // panel, panel, 2 * phys * panel)
         first = c * (COLS // panel)
         h, first = first // half, first % half
-        out_ref[first : first + COLS // panel, h * panel : (h + 1) * panel, :] = turned
+        lanes = out_ref.shape[2]
+        for part in range(turned.shape[2] // lanes):
+            top = part * 2 * panel + h * panel
+            out_ref[first : first + COLS // panel, top : top + panel, :] = turned[
+                :, :, part * lanes : (part + 1) * lanes
+            ]
     return total
 
 
@@ -303,9 +313,10 @@
 ):
     gather(moved_ref, old_ref, env_ref)
     total = spread_plain(1, mix_ref, bank_ref, env_ref[...], tensor_ref, out_ref)
-    rows, lanes = env_ref.shape[0], out_ref.shape[2]
+    rows, lanes = 2 * env_ref.shape[0], out_ref.shape[2]
     odd = jnp.where(pair_ref[...] == now, total, seen_ref[1])
-    extra = jnp.concatenate([two_parts(v) for v in (seen_ref[0], odd)], axis=1)
+    extra = [two_parts(v[:4] + v[4:]).astype(jnp.float32) for v in (seen_ref[0], odd)]
+    extra = jnp.concatenate(extra, axis=0).astype(jnp.bfloat16)
     out_ref[:, rows:, :] = jnp.broadcast_to(extra[None], (out_ref.shape[0], EXTRA, lanes))
 
 
@@ -347,11 +358,11 @@
     rows = env.shape[0]
     panel = rows // 2
     here = pair_ref[:1, :1] == now
-    values = jnp.sum(moved_ref[:, rows:].astype(jnp.float32), axis=0)
+    values = jnp.sum(moved_ref[:, 2 * rows :].astype(jnp.float32), axis=0)
     for q, (kept, last) in enumerate(((even_ref, six_ref), (odd_ref, env))):
         result = jnp.where(here, last[...], kept[...])
-        value = values[:, q * 128 : (q + 1) * 128]
-        extra = two_parts(value[:8] + value[8:])
+        value = values[q * 8 : q * 8 + 4] + values[q * 8 + 4 : q * 8 + 8]
+        extra = two_parts(jnp.concatenate([value, jnp.zeros_like(value)], axis=0))
         extra = jnp.concatenate([extra, jnp.zeros_like(extra)], axis=0)
         width = result.shape[1]
         for h in range(2):
@@ -622,7 +633,7 @@
         functools.partial(end_kernel, pairs - 1),
         in_specs=[VMEM] * 7,
         out_specs=[VMEM] * 2,
-        out_shape=[sent_shape(EXTRA), env_shape],
+        out_shape=[jax.ShapeDtypeStruct((members, 2 * rows + EXTRA, lanes // 2), bf16), env_shape],
         compiler_params=params(),
     )(*vectors, moved, before, after, seen)
     homeward = pl.pallas_call(

time: 260 us -> 259 us (level)
  no operation moved by 1% of the time
where the time goes in v7:
time: 259 us
  blocking collectives  112 us (43%)
  waiting for transfers between devices  65.5 us (25%)
  Pallas kernels  34.2 us (13%)
  starting transfers between devices  26.5 us (10%)
  between operations  14.3 us (6%)
  local copies, waits for them, and re-layouts  5.71 us (2%)
    all_to_all x7, blocking collectives, exchange(): return lax.all_to_all(sent, 'member', 0, 0, tiled=True)  96.7 us
    ppermute x3, waiting for transfers between devices, second_ring(): lax.ppermute(row, bond, shifts(side, m, False))  18.3 us
    all_to_all x1, blocking collectives, on_device(): home = lax.all_to_all(homeward, ('parity', 'half'), 0, 0, tiled=True)  14.8 us
    ppermute x3, waiting for transfers between devices, on_device(): env = lax.ppermute(env, 'pair', [(now, now + 1)])  14.6 us
    all_to_all x1, waiting for transfers between devices, exchange(): return lax.all_to_all(sent, 'member', 0, 0, tiled=True)  14.1 us
    ppermute x3, waiting for transfers between devices, first_ring(): lax.ppermute(chip, bond, shifts(side, k, True))  10.4 us
    ppermute x4, starting transfers between devices, swap_cores(): return [lax.ppermute(p, ('half', 'member'), twins(side)) for p in pieces]  8.65 us
    pallas_call x2, Pallas kernels, on_device(): pl.pallas_call(functools.partial(middle_kernel, now), in_specs=[VMEM] * 7...  6.98 us
  transfers between devices with their start and end apart: 20, of which 10 were waited for; matrix products, arithmetic and copies ran while one was open for 1% of the time, Pallas kernels for 4%

profile of v7, /device:TPU:192, one launch (start us, length us, event | category | flops | bytes accessed | tf_op | source)
XLA Modules:
  0.0 258.7 jit_solution(991444345832023249)
XLA Ops:
  7.2 0.0 all-gather.3.cloned.1.call-start
  7.2 1.0 copy.13
  8.2 1.1 collective-permute-start.1
  9.3 0.8 dynamic-slice_bitcast_fusion
  10.2 3.2 %collective-permute-start = (bf16[32,1024]{1,0:T(8,128)(2,1)S(1)}, bf16[32,1024]{1,0:T(8,128)(2,1)S(1)}, u32[]{:S(2)}, u32[]{:S(2)}) collective-permute-start(bf16[32,1024]{1,0:T(8,128)(2,1)S(1)} %dynamic-slice_bitcast_fusion), channel_id=1, source_target_pairs={{0,16},{16,0},{1,17},{17,1},{2,18},{18,2},{3,19},{19,3},{4,20},{20... | collective-permute-start | bytes 196616 | tf_op jit(solution)/shard_map/ppermute | solution.py:492
  13.4 0.8 copy.11.operators_ref
  14.2 0.1 stack.70.where_ref
  14.3 0.7 copy-done.2
  15.0 0.7 copy-done.3
  15.6 0.7 copy-done.4
  16.3 1.5 shard_map.77
  17.8 0.7 broadcast_select_fusion
  18.6 0.9 copy-done.1
  19.6 0.7 shard_map.78
  20.2 0.1 collective-permute-start.2
  20.3 1.3 collective-permute-done.2
  21.7 2.8 %collective-permute-start.5 = (bf16[2,4,32,512]{3,2,1,0:T(8,128)(2,1)S(1)}, bf16[2,4,32,512]{3,2,1,0:T(8,128)(2,1)S(1)}, u32[]{:S(2)}, u32[]{:S(2)}) collective-permute-start(bf16[2,4,32,512]{3,2,1,0:T(8,128)(2,1)S(1)} %maximum_select_fusion.1), channel_id=1, source_target_pairs={{0,6},{1,25},{2,0},{3,27},{4,2},{5,29},{6,4},{7,31},{8,14},{9,1},{... | collective-permute-start | bytes 786440 | tf_op jit(solution)/shard_map/ppermute | solution.py:453
  24.5 0.8 collective-permute-start.4
  25.3 0.9 collective-permute-start.3
  26.3 5.0 %collective-permute-done.5 = bf16[2,4,32,512]{3,2,1,0:T(8,128)(2,1)S(1)} collective-permute-done((bf16[2,4,32,512]{3,2,1,0:T(8,128)(2,1)S(1)}, bf16[2,4,32,512]{3,2,1,0:T(8,128)(2,1)S(1)}, u32[]{:S(2)}, u32[]{:S(2)}) %collective-permute-start.5) | collective-permute-done | bytes 262176 | tf_op jit(solution)/shard_map/ppermute | solution.py:453
  31.3 1.2 collective-permute-done.4
  32.5 4.1 %collective-permute-done.3 = bf16[2,4,32,512]{3,2,1,0:T(8,128)(2,1)S(1)} collective-permute-done((bf16[2,4,32,512]{3,2,1,0:T(8,128)(2,1)S(1)}, bf16[2,4,32,512]{3,2,1,0:T(8,128)(2,1)S(1)}, u32[]{:S(2)}, u32[]{:S(2)}) %collective-permute-start.3) | collective-permute-done | bytes 262176 | tf_op jit(solution)/shard_map/ppermute | solution.py:453
  36.6 0.1 pad_maximum_fusion.refs_4_.refs_1_.refs_0_
  36.8 0.2 collective-permute-start.9
  37.0 1.2 collective-permute-start.8
  38.2 0.7 collective-permute-start.7
  38.9 14.0 %collective-permute-done.9.refs_7_.refs_4_.refs_3_ = bf16[4,2,4,32,512]{4,3,2,1,0:T(8,128)(2,1)S(1)} collective-permute-done((bf16[4,2,4,32,512]{4,3,2,1,0:T(8,128)(2,1)S(1)}, bf16[4,2,4,32,512]{4,3,2,1,0:T(8,128)(2,1)S(1)}, u32[]{:S(2)}, u32[]{:S(2)}) %collective-permute-start.9) | collective-permute-done | bytes 1048608 | tf_op jit(solution)/shard_map/ppermute | solution.py:458
  52.9 8.6 %collective-permute-start.13 = (bf16[4,2,4,32,512]{4,3,2,1,0:T(8,128)(2,1)S(1)}, bf16[4,2,4,32,512]{4,3,2,1,0:T(8,128)(2,1)}, u32[]{:S(2)}, u32[]{:S(2)}) collective-permute-start(bf16[4,2,4,32,512]{4,3,2,1,0:T(8,128)(2,1)S(1)} %collective-permute-done.9.refs_7_.refs_4_.refs_3_), channel_id=1, source_target_pairs={{0,1},{1,0},{2,3},{3,2},{4,5},{5,4},{6,7},{7,6},{8,9},{9,8},{10,11... | collective-permute-start | bytes 3145736 | tf_op jit(solution)/shard_map/ppermute | solution.py:462
  61.5 0.1 collective-permute-start.12
  61.5 4.3 %collective-permute-done.7.refs_5_.refs_2_.refs_1_ = bf16[4,2,4,32,512]{4,3,2,1,0:T(8,128)(2,1)} collective-permute-done((bf16[4,2,4,32,512]{4,3,2,1,0:T(8,128)(2,1)S(1)}, bf16[4,2,4,32,512]{4,3,2,1,0:T(8,128)(2,1)}, u32[]{:S(2)}, u32[]{:S(2)}) %collective-permute-start.7) | collective-permute-done | bytes 1048608 | tf_op jit(solution)/shard_map/ppermute | solution.py:458
  65.9 1.8 shard_map.79
  67.6 3.6 %all-to-all-start = ((bf16[16,32,512]{2,1,0:T(8,128)(2,1)}), bf16[16,32,512]{2,1,0:T(8,128)(2,1)S(1)}, u32[]{:S(2)}, u32[]{:S(2)}) async-start(bf16[16,32,512]{2,1,0:T(8,128)(2,1)} %get-tuple-element.80), calls=%async_computation | async-start | bytes 1048576 | tf_op jit(solution)/shard_map/all_to_all | solution.py:534
  71.2 14.1 %all-to-all-done.refs_0_ = bf16[16,32,512]{2,1,0:T(8,128)(2,1)S(1)} async-done(((bf16[16,32,512]{2,1,0:T(8,128)(2,1)}), bf16[16,32,512]{2,1,0:T(8,128)(2,1)S(1)}, u32[]{:S(2)}, u32[]{:S(2)}) %all-to-all-start) | async-done | bytes 524320 | tf_op jit(solution)/shard_map/all_to_all | solution.py:534
  85.3 1.0 shard_map.80.refs_2_.refs_0_
  86.4 0.6 collective-permute-start.14
  87.0 1.0 collective-permute-done.14.refs_3_
  87.9 5.7 %all-gather.3.cloned.1.call-done = bf16[128,32,1024]{2,1,0:T(8,128)(2,1)} async-done(((bf16[4,32,1024]{2,1,0:T(8,128)(2,1)}), bf16[128,32,1024]{2,1,0:T(8,128)(2,1)}) %all-gather.3.cloned.1.call-update) | async-done | bytes 8388624 | tf_op jit(solution)/shard_map/all_gather | solution.py:513
  93.7 0.7 shard_map.81
  94.4 14.6 %all_to_all.45.moved_ref = bf16[16,32,512]{2,1,0:T(8,128)(2,1)S(1)} all-to-all(bf16[16,32,512]{2,1,0:T(8,128)(2,1)S(1)} %get-tuple-element.85), channel_id=1, replica_groups=mesh['pair'=4,'parity'=2,'half'=2,'member'=16] {'member'}, dimensions={0} | all-to-all | bytes 1048576 | tf_op jit(solution)/shard_map/all_to_all | solution.py:534
  109.0 1.6 shard_map.82.refs_3_
  110.6 0.7 collective-permute-start.15
  111.3 4.2 %shard_map.83.refs_0_.tensor_ref.old_ref = bf16[16,2,2,4,32,512]{5,4,3,2,1,0:T(8,128)(2,1)S(1)} custom-call(s32[8]{0:T(128)S(1)} %stack.70.where_ref, bf16[4,2,4,32,512]{4,3,2,1,0:T(8,128)(2,1)} %copy-done.5, bf16[4,2,4,32,512]{4,3,2,1,0:T(8,128)(2,1)} %collective-permute-done.7.refs_5_.refs_2_.refs_1_, ...), custom_call_target="tpu_custom_call" | custom-call | tf_op jit(solution)/shard_map/pallas_call | solution.py:595
  115.5 1.2 shard_map.84.bank_ref
  116.7 1.8 shard_map.85
  118.5 13.5 %all_to_all.46.moved_ref = bf16[16,64,256]{2,1,0:T(8,128)(2,1)S(1)} all-to-all(bf16[16,64,256]{2,1,0:T(8,128)(2,1)S(1)} %get-tuple-element.96), channel_id=1, replica_groups=mesh['pair'=4,'parity'=2,'half'=2,'member'=16] {'member'}, dimensions={0} | all-to-all | bytes 1048576 | tf_op jit(solution)/shard_map/all_to_all | solution.py:534
  132.0 3.5 %shard_map.86 = (bf16[16,64,256]{2,1,0:T(8,128)(2,1)S(1)}, f32[2,8,128]{2,1,0:T(8,128)S(1)}, bf16[64,1024]{1,0:T(8,128)(2,1)S(1)}) custom-call(s32[8,128]{1,0:T(8,128)S(1)} %get-tuple-element.67.pair_ref, f32[32,256]{1,0:T(8,128)S(1)} %get-tuple-element.68.mix_ref, f32[2,4,64,1024]{3,2,1,0:T(8,128)S(1)} %shard_map.84.bank_ref, ...), custom_call_target="tpu_custom_call" | custom-call | tf_op jit(solution)/shard_map/pallas_call | solution.py:577
  135.5 13.5 %all_to_all.47.moved_ref = bf16[16,64,256]{2,1,0:T(8,128)(2,1)S(1)} all-to-all(bf16[16,64,256]{2,1,0:T(8,128)(2,1)S(1)} %get-tuple-element.98), channel_id=1, replica_groups=mesh['pair'=4,'parity'=2,'half'=2,'member'=16] {'member'}, dimensions={0} | all-to-all | bytes 1048576 | tf_op jit(solution)/shard_map/all_to_all | solution.py:534
  149.0 1.6 shard_map.87.refs_4_
  150.6 0.7 collective-permute-start.16
  151.3 1.8 shard_map.88
  153.1 13.7 %all_to_all.48.moved_ref = bf16[16,64,256]{2,1,0:T(8,128)(2,1)S(1)} all-to-all(bf16[16,64,256]{2,1,0:T(8,128)(2,1)S(1)} %get-tuple-element.100), channel_id=1, replica_groups=mesh['pair'=4,'parity'=2,'half'=2,'member'=16] {'member'}, dimensions={0} | all-to-all | bytes 1048576 | tf_op jit(solution)/shard_map/all_to_all | solution.py:534
  166.8 3.5 %shard_map.89 = (bf16[16,64,256]{2,1,0:T(8,128)(2,1)S(1)}, f32[2,8,128]{2,1,0:T(8,128)S(1)}, bf16[64,1024]{1,0:T(8,128)(2,1)S(1)}) custom-call(s32[8,128]{1,0:T(8,128)S(1)} %get-tuple-element.67.pair_ref, f32[32,256]{1,0:T(8,128)S(1)} %get-tuple-element.68.mix_ref, f32[2,4,64,1024]{3,2,1,0:T(8,128)S(1)} %shard_map.84.bank_ref, ...), custom_call_target="tpu_custom_call" | custom-call | tf_op jit(solution)/shard_map/pallas_call | solution.py:577
  170.3 13.5 %all_to_all.49.moved_ref = bf16[16,64,256]{2,1,0:T(8,128)(2,1)S(1)} all-to-all(bf16[16,64,256]{2,1,0:T(8,128)(2,1)S(1)} %get-tuple-element.102), channel_id=1, replica_groups=mesh['pair'=4,'parity'=2,'half'=2,'member'=16] {'member'}, dimensions={0} | all-to-all | bytes 1048576 | tf_op jit(solution)/shard_map/all_to_all | solution.py:534
  183.8 1.6 shard_map.90.refs_5_
  185.4 1.3 collective-permute-start.17
  186.7 0.1 shard_map.91
  186.7 14.6 %collective-permute-done.17.env_ref = bf16[64,1024]{1,0:T(8,128)(2,1)S(1)} collective-permute-done((bf16[64,1024]{1,0:T(8,128)(2,1)S(1)}, bf16[64,1024]{1,0:T(8,128)(2,1)S(1)}, u32[]{:S(2)}, u32[]{:S(2)}) %collective-permute-start.17) | collective-permute-done | bytes 131104 | tf_op jit(solution)/shard_map/ppermute | solution.py:621
  201.4 1.8 shard_map.92
  203.2 13.9 %all_to_all.50.moved_ref = bf16[16,64,256]{2,1,0:T(8,128)(2,1)S(1)} all-to-all(bf16[16,64,256]{2,1,0:T(8,128)(2,1)S(1)} %get-tuple-element.116), channel_id=1, replica_groups=mesh['pair'=4,'parity'=2,'half'=2,'member'=16] {'member'}, dimensions={0} | all-to-all | bytes 1048576 | tf_op jit(solution)/shard_map/all_to_all | solution.py:534
  217.0 3.5 %shard_map.93 = (bf16[16,144,128]{2,1,0:T(8,128)(2,1)S(1)}, bf16[64,1024]{1,0:T(8,128)(2,1)S(1)}) custom-call(s32[8,128]{1,0:T(8,128)S(1)} %get-tuple-element.67.pair_ref, f32[32,256]{1,0:T(8,128)S(1)} %get-tuple-element.68.mix_ref, f32[2,4,64,1024]{3,2,1,0:T(8,128)S(1)} %shard_map.84.bank_ref, bf16[16,64,256]{2,1,0:T(8,128)(2,1)S(1)} %all_to_all.50.moved_ref, ...), custom_call_target="tpu_custom_call" | custom-call | tf_op jit(solution)/shard_map/pallas_call | solution.py:632
  220.6 14.1 %all_to_all.51.moved_ref = bf16[16,144,128]{2,1,0:T(8,128)(2,1)S(1)} all-to-all(bf16[16,144,128]{2,1,0:T(8,128)(2,1)S(1)} %get-tuple-element.118), channel_id=1, replica_groups=mesh['pair'=4,'parity'=2,'half'=2,'member'=16] {'member'}, dimensions={0} | all-to-all | bytes 1179648 | tf_op jit(solution)/shard_map/all_to_all | solution.py:534
  234.7 1.6 shard_map.94
  236.3 14.8 %all_to_all.52.home_ref = bf16[4,32,1152]{2,1,0:T(8,128)(2,1)S(1)} all-to-all(bf16[4,32,1152]{2,1,0:T(8,128)(2,1)S(1)} %shard_map.94), channel_id=1, replica_groups=mesh['pair'=4,'parity'=2,'half'=2,'member'=16] {'parity','half'}, dimensions={0} | all-to-all | bytes 589824 | tf_op jit(solution)/shard_map/all_to_all | solution.py:647
  251.1 0.7 shard_map.95
  (26 shorter events, 0.1 us)
Async XLA Ops:
  7.2 86.5 %all-gather.3.cloned.1.call-start = ((), (), s32[]{:S(2)}) async-start(), calls=%async_computation.9 | async-start | bytes 8650752 | tf_op jit(solution)/shard_map/all_gather | solution.py:513
  8.2 9.6 %collective-permute-start.1 = (bf16[4,32,1024]{2,1,0:T(8,128)(2,1)S(1)}, bf16[4,32,1024]{2,1,0:T(8,128)(2,1)S(1)}, u32[]{:S(2)}, u32[]{:S(2)}) collective-permute-start(bf16[4,32,1024]{2,1,0:T(8,128)(2,1)S(1)} %bitcast.33), channel_id=1, source_target_pairs={{0,32},{32,0},{1,33},{33,1},{2,34},{34,2},{3,35},{35,3},{4,36},{36... | collective-permute-start | bytes 786440 | tf_op jit(solution)/shard_map/ppermute | solution.py:490
  10.2 7.6 %collective-permute-start = (bf16[32,1024]{1,0:T(8,128)(2,1)S(1)}, bf16[32,1024]{1,0:T(8,128)(2,1)S(1)}, u32[]{:S(2)}, u32[]{:S(2)}) collective-permute-start(bf16[32,1024]{1,0:T(8,128)(2,1)S(1)} %dynamic-slice_bitcast_fusion), channel_id=1, source_target_pairs={{0,16},{16,0},{1,17},{17,1},{2,18},{18,2},{3,19},{19,3},{4,20},{20... | collective-permute-start | bytes 196616 | tf_op jit(solution)/shard_map/ppermute | solution.py:492
  14.3 0.7 copy-start.2
  15.0 0.7 copy-start.3
  15.6 0.7 copy-start.4
  18.6 1.0 copy-start.1
  20.2 1.4 collective-permute-start.2
  21.7 9.6 %collective-permute-start.5 = (bf16[2,4,32,512]{3,2,1,0:T(8,128)(2,1)S(1)}, bf16[2,4,32,512]{3,2,1,0:T(8,128)(2,1)S(1)}, u32[]{:S(2)}, u32[]{:S(2)}) collective-permute-start(bf16[2,4,32,512]{3,2,1,0:T(8,128)(2,1)S(1)} %maximum_select_fusion.1), channel_id=1, source_target_pairs={{0,6},{1,25},{2,0},{3,27},{4,2},{5,29},{6,4},{7,31},{8,14},{9,1},{... | collective-permute-start | bytes 786440 | tf_op jit(solution)/shard_map/ppermute | solution.py:453
  24.5 8.0 %collective-permute-start.4 = (bf16[2,4,32,512]{3,2,1,0:T(8,128)(2,1)S(1)}, bf16[2,4,32,512]{3,2,1,0:T(8,128)(2,1)S(1)}, u32[]{:S(2)}, u32[]{:S(2)}) collective-permute-start(bf16[2,4,32,512]{3,2,1,0:T(8,128)(2,1)S(1)} %maximum_select_fusion.1), channel_id=1, source_target_pairs={{0,4},{1,17},{2,6},{3,19},{4,0},{5,21},{6,2},{7,23},{8,12},{9,25},... | collective-permute-start | bytes 786440 | tf_op jit(solution)/shard_map/ppermute | solution.py:453
  25.3 11.3 %collective-permute-start.3 = (bf16[2,4,32,512]{3,2,1,0:T(8,128)(2,1)S(1)}, bf16[2,4,32,512]{3,2,1,0:T(8,128)(2,1)S(1)}, u32[]{:S(2)}, u32[]{:S(2)}) collective-permute-start(bf16[2,4,32,512]{3,2,1,0:T(8,128)(2,1)S(1)} %maximum_select_fusion.1), channel_id=1, source_target_pairs={{0,2},{1,9},{2,4},{3,11},{4,6},{5,13},{6,0},{7,15},{8,10},{9,17},{... | collective-permute-start | bytes 786440 | tf_op jit(solution)/shard_map/ppermute | solution.py:453
  26.2 10.6 %collective-permute-start.6 = (bf16[64,1024]{1,0:T(8,128)(2,1)S(1)}, bf16[64,1024]{1,0:T(8,128)(2,1)S(1)}, u32[]{:S(2)}, u32[]{:S(2)}) collective-permute-start(bf16[64,1024]{1,0:T(8,128)(2,1)S(1)} %get-tuple-element.75.refs_2_), channel_id=1, source_target_pairs={{0,1},{1,0},{2,3},{3,2},{4,5},{5,4},{6,7},{7,6},{8,9},{9,8},{10,11... | collective-permute-start | bytes 393224 | tf_op jit(solution)/shard_map/ppermute | solution.py:522
  36.8 29.1 %copy-start.5 = (bf16[4,2,4,32,512]{4,3,2,1,0:T(8,128)(2,1)}, bf16[4,2,4,32,512]{4,3,2,1,0:T(8,128)(2,1)S(1)}, u32[]{:S(2)}) copy-start(bf16[4,2,4,32,512]{4,3,2,1,0:T(8,128)(2,1)S(1)} %pad_maximum_fusion.refs_4_.refs_1_.refs_0_) | copy-start | bytes 3145732
  36.8 16.1 %collective-permute-start.9 = (bf16[4,2,4,32,512]{4,3,2,1,0:T(8,128)(2,1)S(1)}, bf16[4,2,4,32,512]{4,3,2,1,0:T(8,128)(2,1)S(1)}, u32[]{:S(2)}, u32[]{:S(2)}) collective-permute-start(bf16[4,2,4,32,512]{4,3,2,1,0:T(8,128)(2,1)S(1)} %pad_maximum_fusion.refs_4_.refs_1_.refs_0_), channel_id=1, source_target_pairs={{0,24},{1,7},{2,26},{3,1},{4,28},{5,3},{6,30},{7,5},{8,0},{9,15},{... | collective-permute-start | bytes 3145736 | tf_op jit(solution)/shard_map/ppermute | solution.py:458
  37.0 24.5 %collective-permute-start.8 = (bf16[4,2,4,32,512]{4,3,2,1,0:T(8,128)(2,1)S(1)}, bf16[4,2,4,32,512]{4,3,2,1,0:T(8,128)(2,1)}, u32[]{:S(2)}, u32[]{:S(2)}) collective-permute-start(bf16[4,2,4,32,512]{4,3,2,1,0:T(8,128)(2,1)S(1)} %pad_maximum_fusion.refs_4_.refs_1_.refs_0_), channel_id=1, source_target_pairs={{0,16},{1,5},{2,18},{3,7},{4,20},{5,1},{6,22},{7,3},{8,24},{9,13},... | collective-permute-start | bytes 3145736 | tf_op jit(solution)/shard_map/ppermute | solution.py:458
  38.2 27.7 %collective-permute-start.7 = (bf16[4,2,4,32,512]{4,3,2,1,0:T(8,128)(2,1)S(1)}, bf16[4,2,4,32,512]{4,3,2,1,0:T(8,128)(2,1)}, u32[]{:S(2)}, u32[]{:S(2)}) collective-permute-start(bf16[4,2,4,32,512]{4,3,2,1,0:T(8,128)(2,1)S(1)} %pad_maximum_fusion.refs_4_.refs_1_.refs_0_), channel_id=1, source_target_pairs={{0,8},{1,3},{2,10},{3,5},{4,12},{5,7},{6,14},{7,1},{8,16},{9,11},{... | collective-permute-start | bytes 3145736 | tf_op jit(solution)/shard_map/ppermute | solution.py:458
  38.9 32.3 %collective-permute-start.10 = (bf16[4,2,4,32,512]{4,3,2,1,0:T(8,128)(2,1)S(1)}, bf16[4,2,4,32,512]{4,3,2,1,0:T(8,128)(2,1)}, u32[]{:S(2)}, u32[]{:S(2)}) collective-permute-start(bf16[4,2,4,32,512]{4,3,2,1,0:T(8,128)(2,1)S(1)} %pad_maximum_fusion.refs_4_.refs_1_.refs_0_), channel_id=1, source_target_pairs={{0,1},{1,0},{2,3},{3,2},{4,5},{5,4},{6,7},{7,6},{8,9},{9,8},{10,11... | collective-permute-start | bytes 3145736 | tf_op jit(solution)/shard_map/ppermute | solution.py:462
  52.9 13.0 %copy-start.6 = (bf16[4,2,4,32,512]{4,3,2,1,0:T(8,128)(2,1)}, bf16[4,2,4,32,512]{4,3,2,1,0:T(8,128)(2,1)S(1)}, u32[]{:S(2)}) copy-start(bf16[4,2,4,32,512]{4,3,2,1,0:T(8,128)(2,1)S(1)} %collective-permute-done.9.refs_7_.refs_4_.refs_3_) | copy-start | bytes 3145732
  52.9 32.4 %collective-permute-start.13 = (bf16[4,2,4,32,512]{4,3,2,1,0:T(8,128)(2,1)S(1)}, bf16[4,2,4,32,512]{4,3,2,1,0:T(8,128)(2,1)}, u32[]{:S(2)}, u32[]{:S(2)}) collective-permute-start(bf16[4,2,4,32,512]{4,3,2,1,0:T(8,128)(2,1)S(1)} %collective-permute-done.9.refs_7_.refs_4_.refs_3_), channel_id=1, source_target_pairs={{0,1},{1,0},{2,3},{3,2},{4,5},{5,4},{6,7},{7,6},{8,9},{9,8},{10,11... | collective-permute-start | bytes 3145736 | tf_op jit(solution)/shard_map/ppermute | solution.py:462
  61.5 23.9 %collective-permute-start.12 = (bf16[4,2,4,32,512]{4,3,2,1,0:T(8,128)(2,1)}, bf16[4,2,4,32,512]{4,3,2,1,0:T(8,128)(2,1)}, u32[]{:S(2)}, u32[]{:S(2)}) collective-permute-start(bf16[4,2,4,32,512]{4,3,2,1,0:T(8,128)(2,1)} %collective-permute-done.8.refs_6_.refs_3_.refs_2_), channel_id=1, source_target_pairs={{0,1},{1,0},{2,3},{3,2},{4,5},{5,4},{6,7},{7,6},{8,9},{9,8},{10,11... | collective-permute-start | bytes 3145736 | tf_op jit(solution)/shard_map/ppermute | solution.py:462
  65.9 19.5 %collective-permute-start.11 = (bf16[4,2,4,32,512]{4,3,2,1,0:T(8,128)(2,1)}, bf16[4,2,4,32,512]{4,3,2,1,0:T(8,128)(2,1)}, u32[]{:S(2)}, u32[]{:S(2)}) collective-permute-start(bf16[4,2,4,32,512]{4,3,2,1,0:T(8,128)(2,1)} %collective-permute-done.7.refs_5_.refs_2_.refs_1_), channel_id=1, source_target_pairs={{0,1},{1,0},{2,3},{3,2},{4,5},{5,4},{6,7},{7,6},{8,9},{9,8},{10,11... | collective-permute-start | bytes 3145736 | tf_op jit(solution)/shard_map/ppermute | solution.py:462
  67.6 17.7 %all-to-all-start = ((bf16[16,32,512]{2,1,0:T(8,128)(2,1)}), bf16[16,32,512]{2,1,0:T(8,128)(2,1)S(1)}, u32[]{:S(2)}, u32[]{:S(2)}) async-start(bf16[16,32,512]{2,1,0:T(8,128)(2,1)} %get-tuple-element.80), calls=%async_computation | async-start | bytes 1048576 | tf_op jit(solution)/shard_map/all_to_all | solution.py:534
  86.4 1.6 collective-permute-start.14
  93.7 15.3 %copy-start = (bf16[128,32,1024]{2,1,0:T(8,128)(2,1)S(1)}, bf16[128,32,1024]{2,1,0:T(8,128)(2,1)}, u32[]{:S(2)}) copy-start(bf16[128,32,1024]{2,1,0:T(8,128)(2,1)} %all-gather.3.cloned.1.call-done) | copy-start | bytes 25165828
  110.6 6.1 %collective-permute-start.15 = (bf16[64,1024]{1,0:T(8,128)(2,1)S(1)}, bf16[64,1024]{1,0:T(8,128)(2,1)S(1)}, u32[]{:S(2)}, u32[]{:S(2)}) collective-permute-start(bf16[64,1024]{1,0:T(8,128)(2,1)S(1)} %shard_map.82.refs_3_), channel_id=1, source_target_pairs={{0,64},{1,65},{2,66},{3,67},{4,68},{5,69},{6,70},{7,71},{8,72},{9,... | collective-permute-start | bytes 393224 | tf_op jit(solution)/shard_map/ppermute | solution.py:621
  150.6 0.7 collective-permute-start.16
  185.4 16.0 %collective-permute-start.17 = (bf16[64,1024]{1,0:T(8,128)(2,1)S(1)}, bf16[64,1024]{1,0:T(8,128)(2,1)S(1)}, u32[]{:S(2)}, u32[]{:S(2)}) collective-permute-start(bf16[64,1024]{1,0:T(8,128)(2,1)S(1)} %shard_map.90.refs_5_), channel_id=1, source_target_pairs={{128,192},{129,193},{130,194},{131,195},{132,196},{133,197},{134,1... | collective-permute-start | bytes 393224 | tf_op jit(solution)/shard_map/ppermute | solution.py:621
Sparse Core Ops, SparseCore 0:
  18.7 74.9 all-gather.2
